TPU v7x, 32 devices: a whole 2x2x4 slice. The times are simulated.
32 devices in a mesh: grp: 4 (over y, x), shard: 8 (over z, core).
Axes of the slice: x: 2, y: 2, z: 4, core: 2. Of those that a mesh axis runs over, the one named last changes fastest.
Arguments:
- token_table: bfloat16 [30720, 768], P('shard'), may hold values from -6 to 6
- enc_weight: bfloat16 [768, 768], replicated, may hold values from -0.21875 to 0.21875
- enc_gain: float32 [768], replicated, may hold values from 0.1 to 1.9
- label_tokens: int32 [4096, 8], P(('grp', 'shard')), may hold values from 0 to 30719, as said below
- ref_owner: int32 [4096, 1], P(('grp', 'shard')), may hold values from 0 to 7; in each aligned block of 128 rows (0 to 127, 128 to 255, ...) at most 32 rows name the same one
- ref_row: int32 [4096], P(('grp', 'shard')), may hold values from 0 to 1279
- free_rows: bfloat16 [40960, 768], P(('grp', 'shard')), may hold values from -0.21875 to 0.21875
- docs: bfloat16 [64, 768], P(('grp', 'shard')), may hold values from -6 to 6
- positives: int32 [64, 5], P(('grp', 'shard')), may hold values from 0 to 40959
Outputs:
- free_grad: bfloat16 [40960, 768], P(('grp', 'shard'))
- doc_grad: float32 [64, 768], P(('grp', 'shard'))
- ref_grad: bfloat16 [4096, 768], P(('grp', 'shard'))
Inputs may be any that keep to these rules, and one draw needn't show every extreme that they name: `label_tokens`: among the 1024 tokens of one device's labels, at most 160 lie in any one block of 3840 consecutive ids, and some block holds exactly 160 of them. `ref_owner`: among one device's 128 refreshed labels at most 32 name one owner.
All inputs are finite; a program needn't handle non-finite values.
Results may differ from a plain program's by a relative error of at most 0.0055.
Values may be sent and summed in bfloat16 or wider, within the bound.
No kernel may reach another device: no remote copies, remote signals or barrier semaphores. Data moves between devices by JAX's collectives and lax.ppermute only.
A program may use at most 64 MiB of HBM per device.

v0:
```python
import jax
import jax.numpy as jnp
from jax import lax
from jax.sharding import PartitionSpec as P


def slot_within(owner, count):
    marks = (owner[:, None] == jnp.arange(count, dtype=jnp.int32)[None, :]).astype(jnp.int32)
    return jnp.sum(jnp.cumsum(marks, axis=0) * marks, axis=1) - 1


def label_terms(doc_block, pos_block, head, label_columns):
    logits = lax.dot_general(
        doc_block, head, (((1,), (1,)), ((), ())), preferred_element_type=jnp.float32
    )
    hits = jnp.zeros(logits.shape, jnp.bool_)
    for column in range(pos_block.shape[1]):
        hits = hits | (pos_block[:, column : column + 1] == label_columns[None, :])
    errors = (jax.nn.sigmoid(logits) - hits.astype(jnp.float32)).astype(jnp.bfloat16)
    head_part = lax.dot_general(
        errors, doc_block, (((0,), (0,)), ((), ())), preferred_element_type=jnp.float32
    )
    rows_grad = jnp.dot(errors, head, preferred_element_type=jnp.float32)
    return (head_part, rows_grad)


def on_device(
    token_table, enc_weight, enc_gain, label_tokens, ref_owner, ref_row, free_rows, docs, positives
):
    shards = lax.axis_size("shard")
    vocab_rows = token_table.shape[0]
    width = token_table.shape[1]
    label_count, text_length = label_tokens.shape
    token_count = label_count * text_length
    token_cap = 5 * token_count // (4 * shards)
    token_ids = label_tokens.reshape(token_count)
    token_owner = token_ids // vocab_rows
    token_dest = token_owner * token_cap + slot_within(token_owner, shards)
    send_ids = (
        jnp.full((shards * token_cap,), -1, jnp.int32)
        .at[token_dest]
        .set(token_ids - token_owner * vocab_rows)
    )
    send_ids = send_ids.reshape(shards, token_cap)
    asked = lax.all_to_all(send_ids, "shard", split_axis=0, concat_axis=0, tiled=True)
    valid = (asked >= 0)[..., None]
    found = jnp.where(valid, token_table[jnp.maximum(asked, 0)], jnp.zeros((), jnp.bfloat16))
    token_found = lax.all_to_all(found, "shard", split_axis=0, concat_axis=0, tiled=True)
    token_embed = token_found.reshape(shards * token_cap, width)[token_dest]
    pooled = jnp.mean(
        token_embed.reshape(label_count, text_length, width).astype(jnp.float32), axis=1
    ).astype(jnp.bfloat16)
    projected = jnp.dot(pooled, enc_weight, preferred_element_type=jnp.float32)
    norm_scale = lax.rsqrt(jnp.mean(projected * projected, axis=1, keepdims=True) + 1e-06)
    encoded = (projected * norm_scale * enc_gain * width ** (-0.5)).astype(jnp.bfloat16)
    label_cap = 2 * label_count // shards
    label_owner = ref_owner[:, 0]
    label_dest = label_owner * label_cap + slot_within(label_owner, shards)
    send_vectors = jnp.zeros((shards * label_cap, width), jnp.bfloat16).at[label_dest].set(encoded)
    send_rows = jnp.full((shards * label_cap,), -1, jnp.int32).at[label_dest].set(ref_row)
    got_vectors, got_rows = (
        lax.all_to_all(send_vectors, "shard", split_axis=0, concat_axis=0, tiled=True),
        lax.all_to_all(send_rows, "shard", split_axis=0, concat_axis=0, tiled=True),
    )
    slab_rows = free_rows.shape[0]
    target = jnp.where(got_rows >= 0, got_rows, slab_rows)
    delta = (
        jnp.zeros((slab_rows, width), jnp.float32)
        .at[target]
        .add(got_vectors.astype(jnp.float32), mode="drop")
    )
    head = (free_rows.astype(jnp.float32) + delta).astype(jnp.bfloat16)
    label_columns = lax.axis_index(("grp", "shard")) * slab_rows + jnp.arange(
        slab_rows, dtype=jnp.int32
    )
    all_docs, all_positives = (
        lax.all_gather(docs, ("grp", "shard"), axis=0, tiled=True),
        lax.all_gather(positives, ("grp", "shard"), axis=0, tiled=True),
    )
    head_grad, doc_terms = label_terms(all_docs, all_positives, head, label_columns)
    free_grad = head_grad.astype(jnp.bfloat16)
    doc_grad = lax.psum_scatter(doc_terms, ("grp", "shard"), scatter_dimension=0, tiled=True)
    picked = jnp.where(
        (got_rows >= 0)[:, None], free_grad[jnp.maximum(got_rows, 0)], jnp.zeros((), jnp.bfloat16)
    )
    returned = lax.all_to_all(picked, "shard", split_axis=0, concat_axis=0, tiled=True)
    ref_grad = returned[label_dest]
    return (free_grad, doc_grad, ref_grad)


def solution(mesh):
    in_specs = (
        P("shard", None),
        P(),
        P(),
        P(("grp", "shard"), None),
        P(("grp", "shard"), None),
        P(("grp", "shard")),
        P(("grp", "shard"), None),
        P(("grp", "shard"), None),
        P(("grp", "shard"), None),
    )
    out_specs = (P(("grp", "shard"), None), P(("grp", "shard"), None), P(("grp", "shard"), None))
    return jax.shard_map(
        on_device, mesh=mesh, in_specs=in_specs, out_specs=out_specs, check_vma=False
    )
```

profile of v0, /device:TPU:1, one launch (start us, length us, event | category | flops | bytes accessed | tf_op | source)
XLA Modules:
  0.0 346.5 jit_solution(10584223842846736815)
XLA Ops:
  7.2 0.9 copy.38
  8.1 0.1 reshape.230
  8.2 0.1 div.46
  8.3 0.1 div.44
  8.4 0.1 and.28
  8.5 0.1 and.26
  8.7 2.3 reduce-window.6
  10.9 0.3 slice_reduce_fusion
  11.2 0.2 reduce-window.9
  11.5 4.3 %scatter_custom_fusion.1 = s32[1280]{0:T(1024)S(1)} fusion(s32[1024]{0:T(1024)S(1)} %bitcast.72, s32[1024]{0:T(1024)S(1)} %get-tuple-element.8, s32[]{:T(128)} %constant.20.clone.1), kind=kCustom, calls=%fused_computation.66 | custom fusion | bytes 5124 | tf_op jit(solution)/shard_map/scatter | solution.py:42
  15.9 11.1 %all_to_all.44 = s32[8,1,160]{2,1,0:T(1,128)S(1)} all-to-all(s32[8,1,160]{2,1,0:T(1,128)S(1)} %all_to_all.32), channel_id=1, replica_groups=mesh['grp'=4,'shard'=8] {'shard'}, dimensions={0} | all-to-all | bytes 10240 | tf_op jit(solution)/shard_map/all_to_all | solution.py:45
  27.1 8.6 %gather_fusion = bf16[1280,768]{1,0:T(8,128)(2,1)S(1)} fusion(bf16[3840,768]{1,0:T(8,128)(2,1)} %param.9, s32[2048]{0:T(1024)S(1)} %pad_clamp_fusion), kind=kCustom, calls=%fused_computation | custom fusion | bytes 3937280 | tf_op jit(solution)/shard_map/gather | solution.py:47
  35.7 1.5 broadcast_select_fusion
  37.2 4.3 %all-to-all-start.2 = ((bf16[8,160,768]{2,1,0:T(8,128)(2,1)}), bf16[8,160,768]{2,1,0:T(8,128)(2,1)S(1)}, u32[]{:S(2)}, u32[]{:S(2)}) async-start(bf16[8,160,768]{2,1,0:T(8,128)(2,1)} %broadcast_select_fusion), calls=%async_computation.2 | async-start | bytes 3932160 | tf_op jit(solution)/shard_map/all_to_all | solution.py:48
  41.7 0.2 reduce_window_sum.26
  41.9 0.2 select_reduce_fusion
  42.0 1.1 scatter_custom_fusion
  43.2 0.7 all_to_all.29
  43.8 73.0 %all-gather.1 = s32[32,2,5]{2,1,0:T(2,128)S(1)} all-gather(s32[1,2,5]{2,1,0:T(2,128)S(1)} %bitcast.84), channel_id=1, replica_groups=mesh['grp'=4,'shard'=8] {'grp','shard'}, dimensions={0}, use_global_device_ids=true | all-gather | bytes 1320 | tf_op jit(solution)/shard_map/all_gather | solution.py:78
  116.9 0.7 fusion.32
  117.6 3.4 all-to-all-start
  121.0 5.2 %gather_fusion.1 = bf16[1024,768]{1,0:T(8,128)(2,1)} fusion(bf16[1280,768]{1,0:T(8,128)(2,1)S(1)} %bitcast.63, s32[1024]{0:T(1024)S(1)} %broadcast_clamp_fusion), kind=kCustom, calls=%fused_computation.1 | custom fusion | bytes 3149824 | tf_op jit(solution)/shard_map/gather | solution.py:49
  126.2 2.5 convert_reduce_fusion
  128.7 0.4 multiply_reduce_fusion
  129.1 0.6 add_rsqrt_fusion
  129.7 2.1 scatter_custom_fusion.2
  131.8 5.1 %all-to-all-start.3 = ((bf16[8,32,768]{2,1,0:T(8,128)(2,1)}), bf16[8,32,768]{2,1,0:T(8,128)(2,1)S(1)}, u32[]{:S(2)}, u32[]{:S(2)}) async-start(bf16[8,32,768]{2,1,0:T(8,128)(2,1)} %bitcast.67), calls=%async_computation.3 | async-start | bytes 786432 | tf_op jit(solution)/shard_map/all_to_all | solution.py:62
  137.0 44.9 %all-gather = bf16[32,2,768]{2,1,0:T(2,128)(2,1)} all-gather(bf16[1,2,768]{2,1,0:T(2,128)(2,1)S(1)} %bitcast.76), channel_id=1, replica_groups=mesh['grp'=4,'shard'=8] {'grp','shard'}, dimensions={0}, use_global_device_ids=true | all-gather | bytes 101376 | tf_op jit(solution)/shard_map/all_gather | solution.py:77
  181.9 2.2 convert_element_type.41
  184.1 0.8 copy.50
  184.9 0.8 copy.51
  185.7 0.8 copy.52
  186.6 0.8 copy.53
  187.4 0.8 copy.54
  188.2 0.9 reshape.302
  189.2 0.5 broadcast.296
  189.7 0.7 reduce.5
  190.5 6.2 %scatter_custom_fusion.3 = f32[1280,768]{1,0:T(8,128)} fusion(f32[1280,768]{1,0:T(8,128)} %convert_element_type.41, s32[256]{0:T(256)S(1)} %bitcast.85, bf16[256,768]{1,0:T(8,128)(2,1)S(1)} %bitcast.66), kind=kCustom, calls=%fused_computation.21 | custom fusion | flops 393216 | bytes 4325376 | tf_op jit(solution)/shard_map/scatter-add | solution.py:70
  196.7 2.9 fusion.5
  199.6 0.6 copy-done.3
  200.3 1.6 convolution_convert_fusion
  201.9 1.2 gather_fusion.2
  203.1 0.8 broadcast_select_fusion.1
  203.9 3.5 %all-to-all-start.4 = ((bf16[8,32,768]{2,1,0:T(8,128)(2,1)}), bf16[8,32,768]{2,1,0:T(8,128)(2,1)S(1)}, u32[]{:S(2)}, u32[]{:S(2)}) async-start(bf16[8,32,768]{2,1,0:T(8,128)(2,1)} %broadcast_select_fusion.1), calls=%async_computation.4 | async-start | bytes 786432 | tf_op jit(solution)/shard_map/all_to_all | solution.py:86
  207.5 3.4 fusion.6
  210.9 125.9 %all-reduce.3.cloned.1.call-done = f32[64,768]{1,0:T(8,128)} async-done(((f32[64,768]{1,0:T(8,128)}), f32[64,768]{1,0:T(8,128)}) %all-reduce.3.cloned.1.call-update) | async-done | bytes 196624
  336.7 1.3 constant_dynamic-slice_fusion
  338.1 1.5 gather_fusion.3
  (46 shorter events, 0.7 us)
Async XLA Ops:
  7.2 121.5 %copy-start = (bf16[768,768]{1,0:T(8,128)(2,1)S(1)}, bf16[768,768]{1,0:T(8,128)(2,1)}, u32[]{:S(2)}) copy-start(bf16[768,768]{1,0:T(8,128)(2,1)} %param.10) | copy-start | bytes 3538948
  37.2 4.4 %copy-start.7 = (s32[128,1]{0,1:T(1,128)S(1)}, s32[128,1]{0,1:T(1,128)}, u32[]{:S(2)}) copy-start(s32[128,1]{0,1:T(1,128)} %param.13) | copy-start | bytes 1540
  37.2 6.6 %copy-start.8 = (s32[2,5]{1,0:T(2,128)S(1)}, s32[2,5]{1,0:T(2,128)}, u32[]{:S(2)}) copy-start(s32[2,5]{1,0:T(2,128)} %param.17) | copy-start | bytes 124
  37.2 80.3 %all-to-all-start.2 = ((bf16[8,160,768]{2,1,0:T(8,128)(2,1)}), bf16[8,160,768]{2,1,0:T(8,128)(2,1)S(1)}, u32[]{:S(2)}, u32[]{:S(2)}) async-start(bf16[8,160,768]{2,1,0:T(8,128)(2,1)} %broadcast_select_fusion), calls=%async_computation.2 | async-start | bytes 3932160 | tf_op jit(solution)/shard_map/all_to_all | solution.py:48
  117.6 14.2 %all-to-all-start = ((s32[8,32,1]{1,2,0:T(1,128)}), s32[8,32,1]{1,2,0:T(1,128)S(1)}, u32[]{:S(2)}, u32[]{:S(2)}) async-start(s32[8,32,1]{1,2,0:T(1,128)} %all_to_all.29), calls=%async_computation | async-start | bytes 8192 | tf_op jit(solution)/shard_map/all_to_all | solution.py:63
  126.2 3.5 %copy-start.5 = (f32[768]{0:T(1024)S(1)}, f32[768]{0:T(1024)}, u32[]{:S(2)}) copy-start(f32[768]{0:T(1024)} %param.11) | copy-start | bytes 9220
  128.7 8.3 %copy-start.6 = (bf16[2,768]{1,0:T(2,128)(2,1)S(1)}, bf16[2,768]{1,0:T(2,128)(2,1)}, u32[]{:S(2)}) copy-start(bf16[2,768]{1,0:T(2,128)(2,1)} %param.16) | copy-start | bytes 9220
  128.7 53.2 %copy-start.2 = (bf16[1280,768]{1,0:T(8,128)(2,1)S(1)}, bf16[1280,768]{1,0:T(8,128)(2,1)}, u32[]{:S(2)}) copy-start(bf16[1280,768]{1,0:T(8,128)(2,1)} %param.15) | copy-start | bytes 5898244
  131.8 58.7 %all-to-all-start.3 = ((bf16[8,32,768]{2,1,0:T(8,128)(2,1)}), bf16[8,32,768]{2,1,0:T(8,128)(2,1)S(1)}, u32[]{:S(2)}, u32[]{:S(2)}) async-start(bf16[8,32,768]{2,1,0:T(8,128)(2,1)} %bitcast.67), calls=%async_computation.3 | async-start | bytes 786432 | tf_op jit(solution)/shard_map/all_to_all | solution.py:62
  189.2 7.6 %copy-start.4 = (bf16[64,768]{1,0:T(8,128)(2,1)}, bf16[64,768]{1,0:T(8,128)(2,1)S(1)}, u32[]{:S(2)}) copy-start(bf16[64,768]{1,0:T(8,128)(2,1)S(1)} %reshape.302) | copy-start | bytes 294916
  199.6 0.7 copy-start.3
  201.9 2.0 copy-start.1
  203.9 134.1 %all-to-all-start.4 = ((bf16[8,32,768]{2,1,0:T(8,128)(2,1)}), bf16[8,32,768]{2,1,0:T(8,128)(2,1)S(1)}, u32[]{:S(2)}, u32[]{:S(2)}) async-start(bf16[8,32,768]{2,1,0:T(8,128)(2,1)} %broadcast_select_fusion.1), calls=%async_computation.4 | async-start | bytes 786432 | tf_op jit(solution)/shard_map/all_to_all | solution.py:86
  207.5 129.3 %all-reduce.3.cloned.1.call-start = ((), (), s32[]{:S(2)}) async-start(), calls=%async_computation.5 | async-start | bytes 393216
Sparse Core Ops, SparseCore 0:
  214.4 122.2 all-reduce.2
where the time goes:
time: 349 us; the launch traced here: 346 us
  blocking collectives  129 us (37%)
  waiting for transfers between devices  126 us (36%)
  local copies, waits for them, and re-layouts  32.9 us (9%)
  other arithmetic  19.7 us (6%)
  starting transfers between devices  16.4 us (5%)
  between operations  14.3 us (4%)
  matrix products  8.25 us (2%)
    unnamed x2, waiting for transfers between devices  126 us
    all_gather x1, blocking collectives, on_device(): lax.all_gather(positives, ('grp', 'shard'), axis=0, tiled=True)  73 us
    all_gather x1, blocking collectives, on_device(): lax.all_gather(docs, ('grp', 'shard'), axis=0, tiled=True)  44.9 us
    all_to_all x1, blocking collectives, on_device(): lax.all_to_all(send_ids, 'shard', split_axis=0, concat_axis=0, tiled=True)  11.1 us
    gather x1, local copies, waits for them, and re-layouts, on_device(): token_table[jnp.maximum(asked, 0)]  8.6 us
    unnamed x26, local copies, waits for them, and re-layouts  8.03 us
  transfers between devices with their start and end apart: 5, of which 1 were waited for; matrix products, arithmetic and copies ran while one was open for 8% of the time, Pallas kernels for 0%

commit v1 on v0

v1 whole, which is shorter than its diff:
```python
import jax
import jax.numpy as jnp
from jax import lax
from jax.sharding import PartitionSpec as P

BF16 = jnp.bfloat16
F32 = jnp.float32
I32 = jnp.int32
ALL = ("grp", "shard")


def exchange(blocks, axes):
    return lax.all_to_all(blocks, axes, split_axis=0, concat_axis=0, tiled=True)


def inclusive_counts(marks):
    count = marks.shape[0]
    rows = lax.broadcasted_iota(I32, (count, count), 0)
    cols = lax.broadcasted_iota(I32, (count, count), 1)
    return jnp.dot((cols <= rows).astype(BF16), marks.astype(BF16), preferred_element_type=F32).astype(I32)


def token_places(owner, shards, cap):
    labels, length = owner.shape
    marks = (owner[:, :, None] == jnp.arange(shards, dtype=I32)).astype(I32)
    within = inclusive_counts(marks.reshape(labels, length * shards)).reshape(labels, length, shards)
    totals = within[-1]
    before = jnp.cumsum(totals, axis=0) - totals
    slot = jnp.sum((within + before[None] - 1) * marks, axis=2)
    return owner * cap + slot


def label_places(owner, shards, cap):
    marks = (owner[:, None] == jnp.arange(shards, dtype=I32)).astype(I32)
    slot = jnp.sum((inclusive_counts(marks) - 1) * marks, axis=1)
    return owner * cap + slot


def placed(values, places, size):
    hit = places[:, None] == jnp.arange(size, dtype=I32)[None, :]
    return jnp.sum(jnp.where(hit, values[:, None] + 1, 0), axis=0) - 1


def on_device(
    token_table, enc_weight, enc_gain, label_tokens, ref_owner, ref_row, free_rows, docs, positives
):
    shards = lax.axis_size("shard")
    devices = shards * lax.axis_size("grp")
    vocab_rows, width = token_table.shape
    labels, length = label_tokens.shape
    own_docs = docs.shape[0]
    pos_count = positives.shape[1]
    slab_rows = free_rows.shape[0]
    tokens = labels * length
    token_cap = 5 * tokens // (4 * shards)
    label_cap = 2 * labels // shards

    token_owner = label_tokens // vocab_rows
    token_dest = token_places(token_owner, shards, token_cap)
    send_ids = placed(
        (label_tokens - token_owner * vocab_rows).reshape(tokens),
        token_dest.reshape(tokens),
        shards * token_cap,
    )
    label_dest = label_places(ref_owner[:, 0], shards, label_cap)
    send_rows = placed(ref_row, label_dest, shards * label_cap)
    asked = exchange(
        jnp.concatenate(
            [send_ids.reshape(shards, token_cap), send_rows.reshape(shards, label_cap)], axis=1
        ),
        "shard",
    )
    got_rows = asked[:, token_cap:].reshape(shards * label_cap)

    digits = jnp.concatenate(
        [positives & 255, (positives >> 8) & 255, positives >> 16], axis=1
    ).astype(BF16)
    own_block = jnp.concatenate(
        [docs, digits, jnp.zeros((own_docs, 128 - 3 * pos_count), BF16)], axis=1
    )
    all_blocks = exchange(
        jnp.broadcast_to(own_block[None], (devices, own_docs, width + 128)), ALL
    ).reshape(devices * own_docs, width + 128)
    all_docs = all_blocks[:, :width]
    d = all_blocks[:, width : width + 3 * pos_count].astype(I32)
    all_positives = d[:, :pos_count] + 256 * d[:, pos_count : 2 * pos_count] + 65536 * d[:, 2 * pos_count :]

    found = token_table[jnp.maximum(asked[:, :token_cap], 0)]
    token_found = exchange(found, "shard").reshape(shards * token_cap, width)
    pick_tokens = jnp.zeros((labels, shards * token_cap), F32)
    for j in range(length):
        pick_tokens += (
            token_dest[:, j : j + 1] == jnp.arange(shards * token_cap, dtype=I32)[None, :]
        ).astype(F32)
    pooled = jnp.dot(
        (pick_tokens / length).astype(BF16), token_found, preferred_element_type=F32
    ).astype(BF16)
    projected = jnp.dot(pooled, enc_weight, preferred_element_type=F32)
    norm_scale = lax.rsqrt(jnp.mean(projected * projected, axis=1, keepdims=True) + 1e-06)
    encoded = (projected * norm_scale * enc_gain * width ** (-0.5)).astype(BF16)

    to_slots = (
        jnp.arange(shards * label_cap, dtype=I32)[:, None] == label_dest[None, :]
    ).astype(BF16)
    send_vectors = jnp.dot(to_slots, encoded, preferred_element_type=F32).astype(BF16)
    got_vectors = exchange(send_vectors.reshape(shards, label_cap, width), "shard").reshape(
        shards * label_cap, width
    )
    to_rows = (jnp.arange(slab_rows, dtype=I32)[:, None] == got_rows[None, :]).astype(BF16)
    delta = jnp.dot(to_rows, got_vectors, preferred_element_type=F32)
    head = (free_rows.astype(F32) + delta).astype(BF16)

    label_columns = lax.axis_index(ALL) * slab_rows + jnp.arange(slab_rows, dtype=I32)
    logits = lax.dot_general(all_docs, head, (((1,), (1,)), ((), ())), preferred_element_type=F32)
    hits = jnp.zeros(logits.shape, jnp.bool_)
    for column in range(pos_count):
        hits = hits | (all_positives[:, column : column + 1] == label_columns[None, :])
    errors = (jax.nn.sigmoid(logits) - hits.astype(F32)).astype(BF16)
    doc_terms = jnp.dot(errors, head, preferred_element_type=F32)
    free_grad = lax.dot_general(
        errors, all_docs, (((0,), (0,)), ((), ())), preferred_element_type=F32
    ).astype(BF16)
    picked = lax.dot_general(
        to_rows, errors, (((0,), (1,)), ((), ())), preferred_element_type=F32
    ).astype(BF16)
    returned = exchange(picked.reshape(shards, label_cap, devices * own_docs), "shard").reshape(
        shards * label_cap, devices * own_docs
    )
    ref_errors = lax.dot_general(
        to_slots, returned, (((0,), (0,)), ((), ())), preferred_element_type=F32
    ).astype(BF16)
    ref_grad = jnp.dot(ref_errors, all_docs, preferred_element_type=F32).astype(BF16)
    doc_grad = jnp.sum(exchange(doc_terms.reshape(devices, own_docs, width), ALL), axis=0)
    return (free_grad, doc_grad, ref_grad)


def solution(mesh):
    in_specs = (
        P("shard", None),
        P(),
        P(),
        P(ALL, None),
        P(ALL, None),
        P(ALL),
        P(ALL, None),
        P(ALL, None),
        P(ALL, None),
    )
    out_specs = (P(ALL, None), P(ALL, None), P(ALL, None))
    return jax.shard_map(
        on_device, mesh=mesh, in_specs=in_specs, out_specs=out_specs, check_vma=False
    )
```

time: 349 us -> 132 us (0.38)
  blocking collectives: 129 us -> 11.1 us
  waiting for transfers between devices: 126 us -> 67 us
  local copies, waits for them, and re-layouts: 32.9 us -> 14.6 us
  other arithmetic: 19.7 us -> 4.66 us
  between operations: 14.3 us -> 0.93 us
  matrix products: 8.25 us -> 14 us
    unnamed x2 -> x0, waiting for transfers between devices: 126 us -> none
    all_gather x2 -> x0, blocking collectives: 118 us -> none  [the longest x1 73 us: on_device(): lax.all_gather(positives, ('grp', 'shard'), axis=0, tiled=True)]
    all_to_all x4 -> x5, waiting for transfers between devices: 0.01 us -> 67 us  [exchange(): return lax.all_to_all(blocks, axes, split_axis=0, concat_axis=0, tiled=True)]
    gather x4 -> x1, local copies, waits for them, and re-layouts: 16.5 us -> 9.22 us  [on_device(): found = token_table[jnp.maximum(asked[:, :token_cap], 0)]]
    unnamed x26 -> x33, local copies, waits for them, and re-layouts: 8.03 us -> 1.66 us
    scatter-add x1 -> x0, other arithmetic: 6.21 us -> none  [on_device(): delta = jnp.zeros((slab_rows, width), jnp.float32).at[target].add(got_vec...]
    dot_general x4 -> x10, matrix products: 8.25 us -> 14 us  [the longest x1 2.9 us: on_device(): lax.dot_general(errors, all_docs, (((0,), (0,)), ((), ())), preferred_ele...]
    scatter x2 -> x0, local copies, waits for them, and re-layouts: 5.43 us -> none  [the longest x1 4.32 us: on_device(): send_ids = jnp.full((shards * token_cap,), -1, jnp.int32).at[token_dest]....]
  transfers between devices with their start and end apart: 5 -> 5, of which waited for: 1 -> 5; matrix products, arithmetic and copies ran while one was open for 8% -> 9% of each run, Pallas kernels for 0% -> 0%
where the time goes in v1:
time: 132 us; the launch traced here: 131 us
  waiting for transfers between devices  67 us (51%)
  starting transfers between devices  19.1 us (14%)
  local copies, waits for them, and re-layouts  14.6 us (11%)
  matrix products  14 us (11%)
  blocking collectives  11.1 us (8%)
  other arithmetic  4.66 us (4%)
    all_to_all x5, waiting for transfers between devices, exchange(): return lax.all_to_all(blocks, axes, split_axis=0, concat_axis=0, tiled=True)  67 us
    all_to_all x5, starting transfers between devices, exchange(): return lax.all_to_all(blocks, axes, split_axis=0, concat_axis=0, tiled=True)  19.1 us
    all_to_all x1, blocking collectives, exchange(): return lax.all_to_all(blocks, axes, split_axis=0, concat_axis=0, tiled=True)  11.1 us
    gather x1, local copies, waits for them, and re-layouts, on_device(): found = token_table[jnp.maximum(asked[:, :token_cap], 0)]  9.22 us
    dot_general x1, matrix products, on_device(): lax.dot_general(errors, all_docs, (((0,), (0,)), ((), ())), preferred_ele...  2.9 us
  transfers between devices with their start and end apart: 5, of which 5 were waited for; matrix products, arithmetic and copies ran while one was open for 9% of the time, Pallas kernels for 0%

profile of v1, /device:TPU:1, one launch (start us, length us, event | category | flops | bytes accessed | tf_op | source)
XLA Modules:
  0.0 131.4 jit_solution(5127001775098684940)
XLA Ops:
  0.6 0.8 add_select_fusion
  1.4 0.1 eq.290
  1.5 0.2 convolution_convert_fusion.4
  1.7 0.2 slice_reduce_fusion.5
  1.9 0.1 reduce_window_sum.13
  2.0 0.1 fusion.45
  2.1 0.7 multiply_add_fusion
  2.8 0.1 copy.22
  2.9 0.1 eq.293
  3.0 0.1 copy.23
  3.1 0.1 add.112
  3.2 0.7 select_reduce_fusion
  4.0 0.9 fusion.11
  4.9 0.7 fusion.50
  5.6 0.7 broadcast_add_fusion.2
  6.2 0.1 select_reduce_fusion.1
  6.4 0.1 sub.47
  6.4 0.1 pad_add_fusion
  6.5 11.1 %all_to_all.37 = s32[8,1,192]{2,1,0:T(1,128)S(1)} all-to-all(s32[8,1,192]{2,1,0:T(1,128)S(1)} %all_to_all.24), channel_id=1, replica_groups=mesh['grp'=4,'shard'=8] {'shard'}, dimensions={0} | all-to-all | bytes 12288 | tf_op jit(solution)/shard_map/all_to_all | solution.py:13
  17.7 9.2 %gather_fusion = bf16[1280,768]{1,0:T(8,128)(2,1)} fusion(bf16[3840,768]{1,0:T(8,128)(2,1)} %param.9, s32[2048]{0:T(1024)S(1)} %pad_clamp_fusion), kind=kCustom, calls=%fused_computation | custom fusion | bytes 3937280 | tf_op jit(solution)/shard_map/gather | solution.py:88
  26.9 4.4 %all-to-all-start.2 = ((bf16[8,160,768]{2,1,0:T(8,128)(2,1)}), bf16[8,160,768]{2,1,0:T(8,128)(2,1)S(1)}, u32[]{:S(2)}, u32[]{:S(2)}) async-start(bf16[8,160,768]{2,1,0:T(8,128)(2,1)} %bitcast.13), calls=%async_computation.2 | async-start | bytes 3932160 | tf_op jit(solution)/shard_map/all_to_all | solution.py:13
  31.3 0.1 concatenate.9
  31.4 45.3 %all-to-all-done.2 = bf16[8,160,768]{2,1,0:T(8,128)(2,1)S(1)} async-done(((bf16[8,160,768]{2,1,0:T(8,128)(2,1)}), bf16[8,160,768]{2,1,0:T(8,128)(2,1)S(1)}, u32[]{:S(2)}, u32[]{:S(2)}) %all-to-all-start.2) | async-done | bytes 1966112 | tf_op jit(solution)/shard_map/all_to_all | solution.py:13
  76.7 0.7 broadcast_in_dim.31
  77.4 4.1 %all-to-all-start = ((bf16[32,2,896]{2,1,0:T(2,128)(2,1)}), bf16[32,2,896]{2,1,0:T(2,128)(2,1)S(1)}, u32[]{:S(2)}, u32[]{:S(2)}) async-start(bf16[32,2,896]{2,1,0:T(2,128)(2,1)} %broadcast_in_dim.31), calls=%async_computation | async-start | bytes 229376 | tf_op jit(solution)/shard_map/all_to_all | solution.py:13
  81.5 2.0 %multiply_reduce_fusion = (f32[128]{0:T(128)S(1)}, f32[128,768]{1,0:T(8,128)}) fusion(bf16[768,768]{1,0:T(8,128)(2,1)S(1)} %copy-done, bf16[1280,768]{1,0:T(8,128)(2,1)S(1)} %bitcast.55, s32[128]{0:T(128)S(1)} %get-tuple-element.9, s32[128]{0:T(128)S(1)} %get-tuple-element.10, s32[128]{0:T(128)S(1)} %get-tuple-element.11, s32[128]{0:T(128)S(1)} %get-tuple-element.12, ...), kind=kOutput, calls=%fused_computation.37 | convolution fusion | flops 407043968 | bytes 3543552 | tf_op jit(solution)/shard_map/dot_general | solution.py:98
  83.5 2.1 %convolution_convert_fusion.1 = bf16[256,768]{1,0:T(8,128)(2,1)} fusion(f32[128,768]{1,0:T(8,128)} %get-tuple-element.22, f32[768]{0:T(1024)S(1)} %copy-done.6, f32[128]{0:T(128)S(1)} %add_rsqrt_fusion, s32[128]{0:T(128)S(1)} %multiply_add_fusion.1), kind=kOutput, calls=%fused_computation.14 | convolution fusion | flops 50954240 | bytes 790528 | tf_op jit(solution)/shard_map/dot_general | solution.py:105
  85.6 3.9 %all-to-all-done = bf16[32,2,896]{2,1,0:T(2,128)(2,1)S(1)} async-done(((bf16[32,2,896]{2,1,0:T(2,128)(2,1)}), bf16[32,2,896]{2,1,0:T(2,128)(2,1)S(1)}, u32[]{:S(2)}, u32[]{:S(2)}) %all-to-all-start) | async-done | bytes 114720 | tf_op jit(solution)/shard_map/all_to_all | solution.py:13
  89.5 3.6 %all-to-all-start.3 = ((bf16[8,32,768]{2,1,0:T(8,128)(2,1)}), bf16[8,32,768]{2,1,0:T(8,128)(2,1)S(1)}, u32[]{:S(2)}, u32[]{:S(2)}) async-start(bf16[8,32,768]{2,1,0:T(8,128)(2,1)} %bitcast.15), calls=%async_computation.3 | async-start | bytes 786432 | tf_op jit(solution)/shard_map/all_to_all | solution.py:13
  93.2 0.1 eq.305
  93.3 0.1 fusion.41
  93.4 0.8 slice_reduce_fusion.4
  94.2 10.5 %all-to-all-done.3 = bf16[8,32,768]{2,1,0:T(8,128)(2,1)S(1)} async-done(((bf16[8,32,768]{2,1,0:T(8,128)(2,1)}), bf16[8,32,768]{2,1,0:T(8,128)(2,1)S(1)}, u32[]{:S(2)}, u32[]{:S(2)}) %all-to-all-start.3) | async-done | bytes 393248 | tf_op jit(solution)/shard_map/all_to_all | solution.py:13
  104.8 2.3 %fusion = bf16[1280,768]{1,0:T(8,128)(2,1)S(1)} fusion(bf16[256,768]{1,0:T(8,128)(2,1)S(1)} %bitcast.56, bf16[1280,768]{1,0:T(8,128)(2,1)} %param.15, s32[256]{0:T(256)S(1)} %eq.305), kind=kOutput, calls=%fused_computation.5 | convolution fusion | flops 506593280 | bytes 4326400 | tf_op jit(solution)/shard_map/dot_general | solution.py:110
  107.2 0.8 fusion.5
  108.0 0.3 fusion.8
  108.4 0.1 copy.24
  108.5 0.7 reshape.118
  109.2 4.1 %all-to-all-start.5 = ((bf16[8,2,1024]{2,1,0:T(2,128)(2,1)}), bf16[8,2,1024]{2,1,0:T(2,128)(2,1)S(1)}, u32[]{:S(2)}, u32[]{:S(2)}) async-start(bf16[8,2,1024]{2,1,0:T(2,128)(2,1)} %reshape.118), calls=%async_computation.5 | async-start | bytes 65536 | tf_op jit(solution)/shard_map/all_to_all | solution.py:13
  113.3 1.4 %fusion.54 = f32[64,768]{1,0:T(8,128)S(1)} fusion(bf16[64,1280]{1,0:T(8,128)(2,1)} %copy-done.4, bf16[1280,768]{1,0:T(8,128)(2,1)S(1)} %fusion), kind=kOutput, calls=%fused_computation.113 | convolution fusion | flops 125829120 | bytes 2326528 | tf_op jit(solution)/shard_map/dot_general | solution.py:119
  114.7 0.8 reshape.99
  115.5 2.8 %all-to-all-done.5 = bf16[8,2,1024]{2,1,0:T(2,128)(2,1)S(1)} async-done(((bf16[8,2,1024]{2,1,0:T(2,128)(2,1)}), bf16[8,2,1024]{2,1,0:T(2,128)(2,1)S(1)}, u32[]{:S(2)}, u32[]{:S(2)}) %all-to-all-start.5) | async-done | bytes 32800 | tf_op jit(solution)/shard_map/all_to_all | solution.py:13
  118.3 3.0 %all-to-all-start.4 = ((f32[32,2,768]{2,1,0:T(2,128)}), f32[32,2,768]{2,1,0:T(2,128)S(1)}, u32[]{:S(2)}, u32[]{:S(2)}) async-start(f32[32,2,768]{2,1,0:T(2,128)} %reshape.99), calls=%async_computation.4 | async-start | bytes 393216 | tf_op jit(solution)/shard_map/all_to_all | solution.py:13
  121.3 2.9 %convolution_convert_fusion = bf16[1280,768]{1,0:T(8,128)(2,1)} fusion(bf16[64,1280]{1,0:T(8,128)(2,1)} %copy-done.4, bf16[64,896]{1,0:T(8,128)(2,1)S(1)} %copy-done.3), kind=kOutput, calls=%fused_computation.4 | convolution fusion | flops 126812160 | bytes 2228224 | tf_op jit(solution)/shard_map/dot_general | solution.py:120
  124.2 0.9 reshape.119
  125.1 1.1 convolution_convert_fusion.2
  126.2 4.5 %all-to-all-done.4 = f32[32,2,768]{2,1,0:T(2,128)S(1)} async-done(((f32[32,2,768]{2,1,0:T(2,128)}), f32[32,2,768]{2,1,0:T(2,128)S(1)}, u32[]{:S(2)}, u32[]{:S(2)}) %all-to-all-start.4) | async-done | bytes 196640 | tf_op jit(solution)/shard_map/all_to_all | solution.py:13
  130.7 0.7 reduce_sum.62
  (50 shorter events, 0.4 us)
Async XLA Ops:
  0.6 80.9 %copy-start = (bf16[768,768]{1,0:T(8,128)(2,1)S(1)}, bf16[768,768]{1,0:T(8,128)(2,1)}, u32[]{:S(2)}) copy-start(bf16[768,768]{1,0:T(8,128)(2,1)} %param.10) | copy-start | bytes 3538948
  26.9 4.4 %copy-start.8 = (s32[2,5]{1,0:T(2,128)S(1)}, s32[2,5]{1,0:T(2,128)}, u32[]{:S(2)}) copy-start(s32[2,5]{1,0:T(2,128)} %param.17) | copy-start | bytes 124
  26.9 4.4 %copy-start.7 = (bf16[2,768]{1,0:T(2,128)(2,1)S(1)}, bf16[2,768]{1,0:T(2,128)(2,1)}, u32[]{:S(2)}) copy-start(bf16[2,768]{1,0:T(2,128)(2,1)} %param.16) | copy-start | bytes 9220
  26.9 4.5 %copy-start.14 = (s32[128,1]{0,1:T(1,128)S(1)}, s32[128,1]{0,1:T(1,128)}, u32[]{:S(2)}) copy-start(s32[128,1]{0,1:T(1,128)} %param.13) | copy-start | bytes 1540
  26.9 49.8 %all-to-all-start.2 = ((bf16[8,160,768]{2,1,0:T(8,128)(2,1)}), bf16[8,160,768]{2,1,0:T(8,128)(2,1)S(1)}, u32[]{:S(2)}, u32[]{:S(2)}) async-start(bf16[8,160,768]{2,1,0:T(8,128)(2,1)} %bitcast.13), calls=%async_computation.2 | async-start | bytes 3932160 | tf_op jit(solution)/shard_map/all_to_all | solution.py:13
  77.4 12.1 %all-to-all-start = ((bf16[32,2,896]{2,1,0:T(2,128)(2,1)}), bf16[32,2,896]{2,1,0:T(2,128)(2,1)S(1)}, u32[]{:S(2)}, u32[]{:S(2)}) async-start(bf16[32,2,896]{2,1,0:T(2,128)(2,1)} %broadcast_in_dim.31), calls=%async_computation | async-start | bytes 229376 | tf_op jit(solution)/shard_map/all_to_all | solution.py:13
  81.5 2.0 %copy-start.6 = (f32[768]{0:T(1024)S(1)}, f32[768]{0:T(1024)}, u32[]{:S(2)}) copy-start(f32[768]{0:T(1024)} %param.11) | copy-start | bytes 9220
  89.5 15.3 %all-to-all-start.3 = ((bf16[8,32,768]{2,1,0:T(8,128)(2,1)}), bf16[8,32,768]{2,1,0:T(8,128)(2,1)S(1)}, u32[]{:S(2)}, u32[]{:S(2)}) async-start(bf16[8,32,768]{2,1,0:T(8,128)(2,1)} %bitcast.15), calls=%async_computation.3 | async-start | bytes 786432 | tf_op jit(solution)/shard_map/all_to_all | solution.py:13
  93.3 11.5 %copy-start.1 = (bf16[64,896]{1,0:T(8,128)(2,1)}, bf16[64,896]{1,0:T(8,128)(2,1)S(1)}, u32[]{:S(2)}) copy-start(bf16[64,896]{1,0:T(8,128)(2,1)S(1)} %reshape.94) | copy-start | bytes 344068
  104.8 2.4 %copy-start.2 = (bf16[64,896]{1,0:T(8,128)(2,1)S(1)}, bf16[64,896]{1,0:T(8,128)(2,1)}, u32[]{:S(2)}) copy-start(bf16[64,896]{1,0:T(8,128)(2,1)} %copy-done.1) | copy-start | bytes 344068
  104.8 2.4 %copy-start.9 = (s32[64]{0:T(128)S(1)}, s32[64]{0:T(128)}, u32[]{:S(2)}) copy-start(s32[64]{0:T(128)} %get-tuple-element.3) | copy-start | bytes 772
  104.8 2.4 %copy-start.10 = (s32[64]{0:T(128)S(1)}, s32[64]{0:T(128)}, u32[]{:S(2)}) copy-start(s32[64]{0:T(128)} %get-tuple-element.4) | copy-start | bytes 772
  104.8 2.4 %copy-start.11 = (s32[64]{0:T(128)S(1)}, s32[64]{0:T(128)}, u32[]{:S(2)}) copy-start(s32[64]{0:T(128)} %get-tuple-element.5) | copy-start | bytes 772
  104.8 2.4 %copy-start.12 = (s32[64]{0:T(128)S(1)}, s32[64]{0:T(128)}, u32[]{:S(2)}) copy-start(s32[64]{0:T(128)} %get-tuple-element.6) | copy-start | bytes 772
  104.8 2.4 %copy-start.13 = (s32[64]{0:T(128)S(1)}, s32[64]{0:T(128)}, u32[]{:S(2)}) copy-start(s32[64]{0:T(128)} %get-tuple-element.7) | copy-start | bytes 772
  108.0 1.2 copy-start.4
  108.0 13.3 %copy-start.3 = (bf16[64,896]{1,0:T(8,128)(2,1)S(1)}, bf16[64,896]{1,0:T(8,128)(2,1)}, u32[]{:S(2)}) copy-start(bf16[64,896]{1,0:T(8,128)(2,1)} %copy-done.1) | copy-start | bytes 344068
  109.2 9.1 %all-to-all-start.5 = ((bf16[8,2,1024]{2,1,0:T(2,128)(2,1)}), bf16[8,2,1024]{2,1,0:T(2,128)(2,1)S(1)}, u32[]{:S(2)}, u32[]{:S(2)}) async-start(bf16[8,2,1024]{2,1,0:T(2,128)(2,1)} %reshape.118), calls=%async_computation.5 | async-start | bytes 65536 | tf_op jit(solution)/shard_map/all_to_all | solution.py:13
  118.3 3.0 %copy-start.5 = (bf16[8,2,1024]{2,1,0:T(2,128)(2,1)}, bf16[8,2,1024]{2,1,0:T(2,128)(2,1)S(1)}, u32[]{:S(2)}) copy-start(bf16[8,2,1024]{2,1,0:T(2,128)(2,1)S(1)} %all-to-all-done.5) | copy-start | bytes 98308
  118.3 12.4 %all-to-all-start.4 = ((f32[32,2,768]{2,1,0:T(2,128)}), f32[32,2,768]{2,1,0:T(2,128)S(1)}, u32[]{:S(2)}, u32[]{:S(2)}) async-start(f32[32,2,768]{2,1,0:T(2,128)} %reshape.99), calls=%async_computation.4 | async-start | bytes 393216 | tf_op jit(solution)/shard_map/all_to_all | solution.py:13

commit v2 on v1

--- a/solution.py
+++ b/solution.py
@@ -41,7 +41,15 @@
     return jnp.sum(jnp.where(hit, values[:, None] + 1, 0), axis=0) - 1
 
 
-def on_device(
+def swap_cores(x):
+    return lax.ppermute(x, "shard", [(i, i ^ 1) for i in range(lax.axis_size("shard"))])
+
+
+def to_chip(x, k):
+    return lax.ppermute(x, "shard", [(i, i ^ (2 * k)) for i in range(lax.axis_size("shard"))])
+
+
+def by_rows(
     token_table, enc_weight, enc_gain, label_tokens, ref_owner, ref_row, free_rows, docs, positives
 ):
     shards = lax.axis_size("shard")
@@ -134,6 +142,131 @@
     return (free_grad, doc_grad, ref_grad)
 
 
+def by_sums(
+    token_table, enc_weight, enc_gain, label_tokens, ref_owner, ref_row, free_rows, docs, positives
+):
+    shards = lax.axis_size("shard")
+    chips = shards // 2
+    devices = shards * lax.axis_size("grp")
+    me = lax.axis_index("shard")
+    vocab_rows, width = token_table.shape
+    labels, length = label_tokens.shape
+    own_docs = docs.shape[0]
+    all_count = devices * own_docs
+    pos_count = positives.shape[1]
+    slab_rows = free_rows.shape[0]
+    tokens = labels * length
+    token_cap = 5 * tokens // (4 * shards)
+    label_cap = 2 * labels // shards
+    others = [k for k in range(chips - 1, 0, -1)]
+    stride = 2 * labels
+
+    other_table = swap_cores(token_table)
+
+    token_owner = label_tokens // vocab_rows
+    token_dest = token_places(token_owner ^ me, shards, token_cap)
+    codes = (label_tokens - token_owner * vocab_rows) * stride + jnp.arange(labels, dtype=I32)[:, None]
+    hit = token_dest.reshape(tokens)[:, None] == jnp.arange(shards * token_cap, dtype=I32)[None, :]
+    asks = labels + jnp.sum(jnp.where(hit, codes.reshape(tokens)[:, None] - labels, 0), axis=0)
+    asks = asks.reshape(chips, 2 * token_cap)
+    asked = {k: to_chip(asks[k : k + 1], k) for k in others}
+    asked[0] = asks[0:1]
+
+    label_dest = label_places(ref_owner[:, 0] ^ me, shards, label_cap)
+    mine = jnp.stack([label_dest, ref_row])
+    theirs = swap_cores(mine)
+    own_rel = label_dest // label_cap
+    other_rel = theirs[0] // label_cap
+    places = jnp.concatenate(
+        [
+            jnp.where(own_rel % 2 == 0, label_dest, -1),
+            jnp.where(other_rel % 2 == 1, theirs[0], -1),
+        ]
+    )
+    slots = shards * label_cap
+    to_slots = jnp.arange(slots, dtype=I32)[:, None] == places[None, :]
+    chip_rows = jnp.concatenate([ref_row, theirs[1]])
+    send_rows = jnp.sum(jnp.where(to_slots, chip_rows[None, :] + 1, 0), axis=1) - 1
+    send_rows = send_rows.reshape(chips, 2 * label_cap)
+    to_slots = to_slots.astype(BF16)
+    got_rows = jnp.concatenate(
+        [send_rows[0:1]] + [to_chip(send_rows[k : k + 1], k) for k in range(1, chips)]
+    ).reshape(slots)
+
+    digits = jnp.concatenate(
+        [positives & 255, (positives >> 8) & 255, positives >> 16], axis=1
+    ).astype(BF16)
+    own_block = jnp.concatenate(
+        [docs, digits, jnp.zeros((own_docs, 128 - 3 * pos_count), BF16)], axis=1
+    )
+    all_blocks = exchange(
+        jnp.broadcast_to(own_block[None], (devices, own_docs, width + 128)), ALL
+    ).reshape(all_count, width + 128)
+    all_docs = all_blocks[:, :width]
+    d = all_blocks[:, width : width + 3 * pos_count].astype(I32)
+    all_positives = d[:, :pos_count] + 256 * d[:, pos_count : 2 * pos_count] + 65536 * d[:, 2 * pos_count :]
+
+    def partial(code):
+        ids = code[0] // stride
+        which = code[0] - ids * stride
+        pick = (jnp.arange(labels, dtype=I32)[:, None] == which[None, :]).astype(BF16) / length
+        near = token_table[ids[:token_cap]]
+        far = other_table[ids[token_cap:]]
+        return jnp.dot(pick[:, :token_cap], near, preferred_element_type=F32) + jnp.dot(
+            pick[:, token_cap:], far, preferred_element_type=F32
+        )
+
+    arrived = [to_chip(partial(asked[k]).astype(BF16), k) for k in others]
+    pooled = partial(asked[0])
+    for term in arrived:
+        pooled = pooled + term.astype(F32)
+    pooled = pooled.astype(BF16)
+    projected = jnp.dot(pooled, enc_weight, preferred_element_type=F32)
+    norm_scale = lax.rsqrt(jnp.mean(projected * projected, axis=1, keepdims=True) + 1e-06)
+    encoded = (projected * norm_scale * enc_gain * width ** (-0.5)).astype(BF16)
+
+    both = jnp.concatenate([encoded, swap_cores(encoded)])
+    send_vectors = jnp.dot(to_slots, both, preferred_element_type=F32).astype(BF16)
+    send_vectors = send_vectors.reshape(chips, 2 * label_cap, width)
+    arrived = {k: to_chip(send_vectors[k], k) for k in others}
+    got_vectors = jnp.concatenate([send_vectors[0]] + [arrived[k] for k in range(1, chips)])
+    to_rows = (jnp.arange(slab_rows, dtype=I32)[:, None] == got_rows[None, :]).astype(BF16)
+    delta = jnp.dot(to_rows, got_vectors, preferred_element_type=F32)
+    head = (free_rows.astype(F32) + delta).astype(BF16)
+
+    label_columns = lax.axis_index(ALL) * slab_rows + jnp.arange(slab_rows, dtype=I32)
+    logits = lax.dot_general(all_docs, head, (((1,), (1,)), ((), ())), preferred_element_type=F32)
+    hits = jnp.zeros(logits.shape, jnp.bool_)
+    for column in range(pos_count):
+        hits = hits | (all_positives[:, column : column + 1] == label_columns[None, :])
+    errors = (jax.nn.sigmoid(logits) - hits.astype(F32)).astype(BF16)
+    doc_terms = jnp.dot(errors, head, preferred_element_type=F32)
+    doc_grad = jnp.sum(exchange(doc_terms.reshape(devices, own_docs, width), ALL), axis=0)
+    picked = lax.dot_general(
+        to_rows, errors, (((0,), (1,)), ((), ())), preferred_element_type=F32
+    ).astype(BF16)
+    picked = picked.reshape(chips, 2 * label_cap, all_count)
+    arrived = {k: to_chip(picked[k], k) for k in others}
+    returned = jnp.concatenate([picked[0]] + [arrived[k] for k in range(1, chips)])
+    chip_errors = lax.dot_general(
+        to_slots, returned, (((0,), (0,)), ((), ())), preferred_element_type=F32
+    ).astype(BF16)
+    ref_errors = chip_errors[:labels] + swap_cores(chip_errors[labels:])
+    free_grad = lax.dot_general(
+        errors, all_docs, (((0,), (0,)), ((), ())), preferred_element_type=F32
+    ).astype(BF16)
+    ref_grad = jnp.dot(ref_errors, all_docs, preferred_element_type=F32).astype(BF16)
+    return (free_grad, doc_grad, ref_grad)
+
+
+def on_device(token_table, enc_weight, enc_gain, label_tokens, *rest):
+    shards = lax.axis_size("shard")
+    labels, length = label_tokens.shape
+    row_count = 5 * labels * length // 4
+    plan = by_sums if shards % 2 == 0 and shards // 2 * labels < row_count else by_rows
+    return plan(token_table, enc_weight, enc_gain, label_tokens, *rest)
+
+
 def solution(mesh):
     in_specs = (
         P("shard", None),

time: 132 us -> 112 us (0.85)
  waiting for transfers between devices: 67 us -> 15.4 us
  local copies, waits for them, and re-layouts: 14.6 us -> 42 us
  starting transfers between devices: 19.1 us -> 36.6 us
  blocking collectives: 11.1 us -> 0 us
  matrix products: 14 us -> 9.51 us
  other arithmetic: 4.66 us -> 7.16 us
    all_to_all x5 -> x2, waiting for transfers between devices: 67 us -> 5.83 us  [exchange(): return lax.all_to_all(blocks, axes, split_axis=0, concat_axis=0, tiled=True)]
    gather x1 -> x8, local copies, waits for them, and re-layouts: 9.22 us -> 36.5 us  [the longest x4 18.5 us: partial(): far = other_table[ids[token_cap:]]]
    ppermute x0 -> x19, starting transfers between devices: none -> 25.2 us  [the longest x15 20.7 us: to_chip(): lax.ppermute(x, 'shard', [(i, i ^ 2 * k) for i in range(lax.axis_size('sh...]
    all_to_all x1 -> x0, blocking collectives: 11.1 us -> none  [exchange(): return lax.all_to_all(blocks, axes, split_axis=0, concat_axis=0, tiled=True)]
    ppermute x0 -> x19, waiting for transfers between devices: none -> 9.54 us  [the longest x15 8.55 us: to_chip(): lax.ppermute(x, 'shard', [(i, i ^ 2 * k) for i in range(lax.axis_size('sh...]
    all_to_all x5 -> x2, starting transfers between devices: 19.1 us -> 11.4 us  [exchange(): return lax.all_to_all(blocks, axes, split_axis=0, concat_axis=0, tiled=True)]
    dot_general x8 -> x16, matrix products: 12.9 us -> 9.19 us  [the longest x3 2.12 us: partial(): jnp.dot(pick[:, token_cap:], far, preferred_element_type=F32)]
    another operation x1 -> x2, other arithmetic: 0.01 us -> 1.35 us
  transfers between devices with their start and end apart: 5 -> 21, of which waited for: 5 -> 5; matrix products, arithmetic and copies ran while one was open for 9% -> 42% of each run, Pallas kernels for 0% -> 0%
where the time goes in v2:
time: 112 us
  local copies, waits for them, and re-layouts  42 us (38%)
  starting transfers between devices  36.6 us (33%)
  waiting for transfers between devices  15.4 us (14%)
  matrix products  9.51 us (8%)
  other arithmetic  7.16 us (6%)
  between operations  1.17 us (1%)
    ppermute x15, starting transfers between devices, to_chip(): lax.ppermute(x, 'shard', [(i, i ^ 2 * k) for i in range(lax.axis_size('sh...  20.7 us
    gather x4, local copies, waits for them, and re-layouts, partial(): far = other_table[ids[token_cap:]]  18.5 us
    gather x4, local copies, waits for them, and re-layouts, partial(): near = token_table[ids[:token_cap]]  18 us
    all_to_all x2, starting transfers between devices, exchange(): return lax.all_to_all(blocks, axes, split_axis=0, concat_axis=0, tiled=True)  11.4 us
    ppermute x15, waiting for transfers between devices, to_chip(): lax.ppermute(x, 'shard', [(i, i ^ 2 * k) for i in range(lax.axis_size('sh...  8.55 us
    all_to_all x2, waiting for transfers between devices, exchange(): return lax.all_to_all(blocks, axes, split_axis=0, concat_axis=0, tiled=True)  5.83 us
    ppermute x4, starting transfers between devices, swap_cores(): lax.ppermute(x, 'shard', [(i, i ^ 1) for i in range(lax.axis_size('shard'...  4.49 us
  transfers between devices with their start and end apart: 21, of which 5 were waited for; matrix products, arithmetic and copies ran while one was open for 42% of the time, Pallas kernels for 0%

profile of v2, /device:TPU:1, one launch (start us, length us, event | category | flops | bytes accessed | tf_op | source)
XLA Modules:
  0.0 111.8 jit_solution(11187068727432905530)
XLA Ops:
  0.8 0.8 broadcast_xor_fusion
  2.5 0.7 select_reduce_fusion
  3.3 3.2 %collective-permute-start.7 = (s32[1,320]{1,0:T(1,128)S(1)}, s32[1,320]{1,0:T(1,128)S(1)}, u32[]{:S(2)}, u32[]{:S(2)}) collective-permute-start(s32[1,320]{1,0:T(1,128)S(1)} %slice.197), channel_id=1, source_target_pairs={{0,4},{1,5},{2,6},{3,7},{4,0},{5,1},{6,2},{7,3},{8,12},{9,13},{10,... | collective-permute-start | bytes 3848 | tf_op jit(solution)/shard_map/ppermute | solution.py:49
  6.5 1.3 %collective-permute-start.9 = (s32[1,320]{1,0:T(1,128)S(1)}, s32[1,320]{1,0:T(1,128)S(1)}, u32[]{:S(2)}, u32[]{:S(2)}) collective-permute-start(s32[1,320]{1,0:T(1,128)S(1)} %slice.203), channel_id=1, source_target_pairs={{0,2},{1,3},{2,0},{3,1},{4,6},{5,7},{6,4},{7,5},{8,10},{9,11},{10,... | collective-permute-start | bytes 3848 | tf_op jit(solution)/shard_map/ppermute | solution.py:49
  7.8 1.2 %collective-permute-start.4 = (bf16[3840,768]{1,0:T(8,128)(2,1)}, bf16[3840,768]{1,0:T(8,128)(2,1)}, u32[]{:S(2)}, u32[]{:S(2)}) collective-permute-start(bf16[3840,768]{1,0:T(8,128)(2,1)} %param.9), channel_id=1, source_target_pairs={{0,1},{1,0},{2,3},{3,2},{4,5},{5,4},{6,7},{7,6},{8,9},{9,8},{10,11... | collective-permute-start | bytes 17694728 | tf_op jit(solution)/shard_map/ppermute | solution.py:45
  9.0 0.7 fusion.85
  9.8 0.7 bitcast_add_fusion.1
  10.5 0.7 pad_add_fusion.1
  11.2 0.7 shift-right-arithmetic_convert_fusion
  11.9 0.8 concatenate.30
  12.7 0.7 broadcast_in_dim.48
  13.4 6.1 %all-to-all-start = ((bf16[32,2,896]{2,1,0:T(2,128)(2,1)}), bf16[32,2,896]{2,1,0:T(2,128)(2,1)}, u32[]{:S(2)}, u32[]{:S(2)}) async-start(bf16[32,2,896]{2,1,0:T(2,128)(2,1)} %broadcast_in_dim.48), calls=%async_computation | async-start | bytes 229376 | tf_op jit(solution)/shard_map/all_to_all | solution.py:13
  19.5 4.5 %gather_fusion = bf16[160,768]{1,0:T(8,128)(2,1)S(1)} fusion(bf16[3840,768]{1,0:T(8,128)(2,1)} %param.9, s32[1024]{0:T(1024)S(1)} %pad_clamp_fusion.7), kind=kCustom, calls=%fused_computation | custom fusion | bytes 492160 | tf_op jit(solution)/shard_map/gather | solution.py:213
  24.6 1.4 %collective-permute-start.1 = (s32[1,64]{1,0:T(1,128)S(1)}, s32[1,64]{1,0:T(1,128)S(1)}, u32[]{:S(2)}, u32[]{:S(2)}) collective-permute-start(s32[1,64]{1,0:T(1,128)S(1)} %get-tuple-element.45), channel_id=1, source_target_pairs={{0,2},{1,3},{2,0},{3,1},{4,6},{5,7},{6,4},{7,5},{8,10},{9,11},{10,... | collective-permute-start | bytes 776 | tf_op jit(solution)/shard_map/ppermute | solution.py:49
  26.0 2.1 %collective-permute-start.2 = (s32[1,64]{1,0:T(1,128)S(1)}, s32[1,64]{1,0:T(1,128)S(1)}, u32[]{:S(2)}, u32[]{:S(2)}) collective-permute-start(s32[1,64]{1,0:T(1,128)S(1)} %get-tuple-element.44), channel_id=1, source_target_pairs={{0,4},{1,5},{2,6},{3,7},{4,0},{5,1},{6,2},{7,3},{8,12},{9,13},{10,... | collective-permute-start | bytes 776 | tf_op jit(solution)/shard_map/ppermute | solution.py:49
  28.6 4.5 %gather_fusion.4 = bf16[160,768]{1,0:T(8,128)(2,1)S(1)} fusion(bf16[3840,768]{1,0:T(8,128)(2,1)} %param.9, s32[1024]{0:T(1024)S(1)} %pad_clamp_fusion.3), kind=kCustom, calls=%fused_computation.4 | custom fusion | bytes 492160 | tf_op jit(solution)/shard_map/gather | solution.py:213
  33.1 4.5 %gather_fusion.6 = bf16[160,768]{1,0:T(8,128)(2,1)S(1)} fusion(bf16[3840,768]{1,0:T(8,128)(2,1)} %param.9, s32[1024]{0:T(1024)S(1)} %pad_clamp_fusion.1), kind=kCustom, calls=%fused_computation.6 | custom fusion | bytes 492160 | tf_op jit(solution)/shard_map/gather | solution.py:213
  37.7 4.5 %gather_fusion.2 = bf16[160,768]{1,0:T(8,128)(2,1)S(1)} fusion(bf16[3840,768]{1,0:T(8,128)(2,1)} %param.9, s32[1024]{0:T(1024)S(1)} %pad_clamp_fusion.5), kind=kCustom, calls=%fused_computation.2 | custom fusion | bytes 492160 | tf_op jit(solution)/shard_map/gather | solution.py:213
  42.2 0.6 eq.228
  42.8 0.6 pad_clamp_fusion.2
  43.4 0.6 pad_clamp_fusion
  45.1 1.0 reshape.133
  46.1 4.6 %gather_fusion.5 = bf16[160,768]{1,0:T(8,128)(2,1)S(1)} fusion(bf16[3840,768]{1,0:T(8,128)(2,1)} %collective-permute-done.4, s32[1024]{0:T(1024)} %pad_clamp_fusion.2), kind=kCustom, calls=%fused_computation.5 | custom fusion | bytes 492160 | tf_op jit(solution)/shard_map/gather | solution.py:214
  50.8 0.9 fusion.12
  51.7 1.4 %collective-permute-start.8 = (bf16[128,768]{1,0:T(8,128)(2,1)}, bf16[128,768]{1,0:T(8,128)(2,1)S(1)}, u32[]{:S(2)}, u32[]{:S(2)}) collective-permute-start(bf16[128,768]{1,0:T(8,128)(2,1)} %fusion.12), channel_id=1, source_target_pairs={{0,4},{1,5},{2,6},{3,7},{4,0},{5,1},{6,2},{7,3},{8,12},{9,13},{10,... | collective-permute-start | bytes 589832 | tf_op jit(solution)/shard_map/ppermute | solution.py:49
  53.1 4.6 %gather_fusion.7 = bf16[160,768]{1,0:T(8,128)(2,1)S(1)} fusion(bf16[3840,768]{1,0:T(8,128)(2,1)} %collective-permute-done.4, s32[1024]{0:T(1024)} %pad_clamp_fusion), kind=kCustom, calls=%fused_computation.7 | custom fusion | bytes 492160 | tf_op jit(solution)/shard_map/gather | solution.py:214
  57.7 0.9 fusion.13
  58.6 2.1 %collective-permute-start.10 = (bf16[128,768]{1,0:T(8,128)(2,1)}, bf16[128,768]{1,0:T(8,128)(2,1)S(1)}, u32[]{:S(2)}, u32[]{:S(2)}) collective-permute-start(bf16[128,768]{1,0:T(8,128)(2,1)} %fusion.13), channel_id=1, source_target_pairs={{0,2},{1,3},{2,0},{3,1},{4,6},{5,7},{6,4},{7,5},{8,10},{9,11},{10,... | collective-permute-start | bytes 589832 | tf_op jit(solution)/shard_map/ppermute | solution.py:49
  60.8 4.5 %gather_fusion.3 = bf16[160,768]{1,0:T(8,128)(2,1)S(1)} fusion(bf16[3840,768]{1,0:T(8,128)(2,1)} %collective-permute-done.4, s32[1024]{0:T(1024)S(1)} %pad_clamp_fusion.4), kind=kCustom, calls=%fused_computation.3 | custom fusion | bytes 492160 | tf_op jit(solution)/shard_map/gather | solution.py:214
  65.7 4.7 %gather_fusion.1 = bf16[160,768]{1,0:T(8,128)(2,1)S(1)} fusion(bf16[3840,768]{1,0:T(8,128)(2,1)} %collective-permute-done.4, s32[1024]{0:T(1024)S(1)} %pad_clamp_fusion.6), kind=kCustom, calls=%fused_computation.1 | custom fusion | bytes 492160 | tf_op jit(solution)/shard_map/gather | solution.py:214
  70.4 1.6 %collective-permute-done.6 = bf16[128,768]{1,0:T(8,128)(2,1)S(1)} collective-permute-done((bf16[128,768]{1,0:T(8,128)(2,1)S(1)}, bf16[128,768]{1,0:T(8,128)(2,1)S(1)}, u32[]{:S(2)}, u32[]{:S(2)}) %collective-permute-start.6) | collective-permute-done | bytes 196640 | tf_op jit(solution)/shard_map/ppermute | solution.py:49
  72.0 0.6 multiply_reduce_fusion
  72.8 2.9 %collective-permute-start.11 = (bf16[128,768]{1,0:T(8,128)(2,1)S(1)}, bf16[128,768]{1,0:T(8,128)(2,1)S(1)}, u32[]{:S(2)}, u32[]{:S(2)}) collective-permute-start(bf16[128,768]{1,0:T(8,128)(2,1)S(1)} %multiply_convert_fusion), channel_id=1, source_target_pairs={{0,1},{1,0},{2,3},{3,2},{4,5},{5,4},{6,7},{7,6},{8,9},{9,8},{10,11... | collective-permute-start | bytes 589832 | tf_op jit(solution)/shard_map/ppermute | solution.py:45
  75.8 1.0 collective-permute-done.11
  77.1 2.3 %collective-permute-start.12 = (bf16[64,768]{1,0:T(8,128)(2,1)S(1)}, bf16[64,768]{1,0:T(8,128)(2,1)S(1)}, u32[]{:S(2)}, u32[]{:S(2)}) collective-permute-start(bf16[64,768]{1,0:T(8,128)(2,1)S(1)} %get-tuple-element.19), channel_id=1, source_target_pairs={{0,2},{1,3},{2,0},{3,1},{4,6},{5,7},{6,4},{7,5},{8,10},{9,11},{10,... | collective-permute-start | bytes 294920 | tf_op jit(solution)/shard_map/ppermute | solution.py:49
  79.5 2.1 %collective-permute-start.14 = (bf16[64,768]{1,0:T(8,128)(2,1)S(1)}, bf16[64,768]{1,0:T(8,128)(2,1)S(1)}, u32[]{:S(2)}, u32[]{:S(2)}) collective-permute-start(bf16[64,768]{1,0:T(8,128)(2,1)S(1)} %get-tuple-element.17), channel_id=1, source_target_pairs={{0,6},{1,7},{2,4},{3,5},{4,2},{5,3},{6,0},{7,1},{8,14},{9,15},{10,... | collective-permute-start | bytes 294920 | tf_op jit(solution)/shard_map/ppermute | solution.py:49
  81.8 0.5 collective-permute-done.12
  82.3 6.4 %collective-permute-done.13 = bf16[64,768]{1,0:T(8,128)(2,1)S(1)} collective-permute-done((bf16[64,768]{1,0:T(8,128)(2,1)S(1)}, bf16[64,768]{1,0:T(8,128)(2,1)S(1)}, u32[]{:S(2)}, u32[]{:S(2)}) %collective-permute-start.13) | collective-permute-done | bytes 98336 | tf_op jit(solution)/shard_map/ppermute | solution.py:49
  88.7 0.7 fusion
  89.5 0.8 fusion.5
  90.7 2.4 %collective-permute-start.15 = (bf16[64,64]{0,1:T(8,128)(2,1)S(1)}, bf16[64,64]{0,1:T(8,128)(2,1)S(1)}, u32[]{:S(2)}, u32[]{:S(2)}) collective-permute-start(bf16[64,64]{0,1:T(8,128)(2,1)S(1)} %get-tuple-element.23), channel_id=1, source_target_pairs={{0,2},{1,3},{2,0},{3,1},{4,6},{5,7},{6,4},{7,5},{8,10},{9,11},{10,... | collective-permute-start | bytes 24584 | tf_op jit(solution)/shard_map/ppermute | solution.py:49
  93.1 2.2 %collective-permute-start.17 = (bf16[64,64]{0,1:T(8,128)(2,1)S(1)}, bf16[64,64]{0,1:T(8,128)(2,1)S(1)}, u32[]{:S(2)}, u32[]{:S(2)}) collective-permute-start(bf16[64,64]{0,1:T(8,128)(2,1)S(1)} %get-tuple-element.21), channel_id=1, source_target_pairs={{0,6},{1,7},{2,4},{3,5},{4,2},{5,3},{6,0},{7,1},{8,14},{9,15},{10,... | collective-permute-start | bytes 24584 | tf_op jit(solution)/shard_map/ppermute | solution.py:49
  95.7 0.8 reshape.135
  96.5 5.3 %all-to-all-start.1 = ((f32[32,2,768]{2,1,0:T(2,128)}), f32[32,2,768]{2,1,0:T(2,128)S(1)}, u32[]{:S(2)}, u32[]{:S(2)}) async-start(f32[32,2,768]{2,1,0:T(2,128)} %reshape.135), calls=%async_computation.1 | async-start | bytes 393216 | tf_op jit(solution)/shard_map/all_to_all | solution.py:13
  102.4 2.0 %convolution_convert_fusion = bf16[1280,768]{1,0:T(8,128)(2,1)} fusion(bf16[64,1280]{1,0:T(8,128)(2,1)S(1)} %fusion.5, bf16[64,896]{1,0:T(8,128)(2,1)S(1)} %reshape.133), kind=kOutput, calls=%fused_computation.11 | convolution fusion | flops 126812160 | bytes 2228224 | tf_op jit(solution)/shard_map/dot_general | solution.py:255
  104.4 0.9 convolution_convert_fusion.2
  105.3 5.8 %all-to-all-done.1 = f32[32,2,768]{2,1,0:T(2,128)S(1)} async-done(((f32[32,2,768]{2,1,0:T(2,128)}), f32[32,2,768]{2,1,0:T(2,128)S(1)}, u32[]{:S(2)}, u32[]{:S(2)}) %all-to-all-start.1) | async-done | bytes 196640 | tf_op jit(solution)/shard_map/all_to_all | solution.py:13
  111.1 0.7 reduce_sum.62
  (109 shorter events, 6.0 us)
Async XLA Ops:
  0.6 71.4 %copy-start = (bf16[768,768]{1,0:T(8,128)(2,1)S(1)}, bf16[768,768]{1,0:T(8,128)(2,1)}, u32[]{:S(2)}) copy-start(bf16[768,768]{1,0:T(8,128)(2,1)} %param.10) | copy-start | bytes 3538948
  0.6 23.4 %copy-start.6 = (s32[128,1]{0,1:T(1,128)S(1)}, s32[128,1]{0,1:T(1,128)}, u32[]{:S(2)}) copy-start(s32[128,1]{0,1:T(1,128)} %param.13) | copy-start | bytes 1540
  1.7 22.7 %copy-start.7 = (s32[128]{0:T(128)S(1)}, s32[128]{0:T(128)}, u32[]{:S(2)}) copy-start(s32[128]{0:T(128)} %param.14) | copy-start | bytes 1540
  3.3 22.7 %collective-permute-start.7 = (s32[1,320]{1,0:T(1,128)S(1)}, s32[1,320]{1,0:T(1,128)S(1)}, u32[]{:S(2)}, u32[]{:S(2)}) collective-permute-start(s32[1,320]{1,0:T(1,128)S(1)} %slice.197), channel_id=1, source_target_pairs={{0,4},{1,5},{2,6},{3,7},{4,0},{5,1},{6,2},{7,3},{8,12},{9,13},{10,... | collective-permute-start | bytes 3848 | tf_op jit(solution)/shard_map/ppermute | solution.py:49
  6.5 21.7 %collective-permute-start.9 = (s32[1,320]{1,0:T(1,128)S(1)}, s32[1,320]{1,0:T(1,128)S(1)}, u32[]{:S(2)}, u32[]{:S(2)}) collective-permute-start(s32[1,320]{1,0:T(1,128)S(1)} %slice.203), channel_id=1, source_target_pairs={{0,2},{1,3},{2,0},{3,1},{4,6},{5,7},{6,4},{7,5},{8,10},{9,11},{10,... | collective-permute-start | bytes 3848 | tf_op jit(solution)/shard_map/ppermute | solution.py:49
  7.8 38.3 %collective-permute-start.4 = (bf16[3840,768]{1,0:T(8,128)(2,1)}, bf16[3840,768]{1,0:T(8,128)(2,1)}, u32[]{:S(2)}, u32[]{:S(2)}) collective-permute-start(bf16[3840,768]{1,0:T(8,128)(2,1)} %param.9), channel_id=1, source_target_pairs={{0,1},{1,0},{2,3},{3,2},{4,5},{5,4},{6,7},{7,6},{8,9},{9,8},{10,11... | collective-permute-start | bytes 17694728 | tf_op jit(solution)/shard_map/ppermute | solution.py:45
  9.0 19.5 %collective-permute-start.5 = (s32[1,320]{1,0:T(1,128)S(1)}, s32[1,320]{1,0:T(1,128)S(1)}, u32[]{:S(2)}, u32[]{:S(2)}) collective-permute-start(s32[1,320]{1,0:T(1,128)S(1)} %slice.191), channel_id=1, source_target_pairs={{0,6},{1,7},{2,4},{3,5},{4,2},{5,3},{6,0},{7,1},{8,14},{9,15},{10,... | collective-permute-start | bytes 3848 | tf_op jit(solution)/shard_map/ppermute | solution.py:49
  11.2 13.2 %collective-permute-start = (s32[2,128]{1,0:T(2,128)S(1)}, s32[2,128]{1,0:T(2,128)S(1)}, u32[]{:S(2)}, u32[]{:S(2)}) collective-permute-start(s32[2,128]{1,0:T(2,128)S(1)} %pad_add_fusion.1), channel_id=1, source_target_pairs={{0,1},{1,0},{2,3},{3,2},{4,5},{5,4},{6,7},{7,6},{8,9},{9,8},{10,11... | collective-permute-start | bytes 3080 | tf_op jit(solution)/shard_map/ppermute | solution.py:45
  13.4 31.7 %all-to-all-start = ((bf16[32,2,896]{2,1,0:T(2,128)(2,1)}), bf16[32,2,896]{2,1,0:T(2,128)(2,1)}, u32[]{:S(2)}, u32[]{:S(2)}) async-start(bf16[32,2,896]{2,1,0:T(2,128)(2,1)} %broadcast_in_dim.48), calls=%async_computation | async-start | bytes 229376 | tf_op jit(solution)/shard_map/all_to_all | solution.py:13
  24.4 3.7 %copy-start.4 = (s32[256]{0:T(256)}, s32[256]{0:T(256)S(1)}, u32[]{:S(2)}) copy-start(s32[256]{0:T(256)S(1)} %pad_add_fusion.2) | copy-start | bytes 3076
  24.6 17.5 %collective-permute-start.1 = (s32[1,64]{1,0:T(1,128)S(1)}, s32[1,64]{1,0:T(1,128)S(1)}, u32[]{:S(2)}, u32[]{:S(2)}) collective-permute-start(s32[1,64]{1,0:T(1,128)S(1)} %get-tuple-element.45), channel_id=1, source_target_pairs={{0,2},{1,3},{2,0},{3,1},{4,6},{5,7},{6,4},{7,5},{8,10},{9,11},{10,... | collective-permute-start | bytes 776 | tf_op jit(solution)/shard_map/ppermute | solution.py:49
  26.0 16.1 %collective-permute-start.2 = (s32[1,64]{1,0:T(1,128)S(1)}, s32[1,64]{1,0:T(1,128)S(1)}, u32[]{:S(2)}, u32[]{:S(2)}) collective-permute-start(s32[1,64]{1,0:T(1,128)S(1)} %get-tuple-element.44), channel_id=1, source_target_pairs={{0,4},{1,5},{2,6},{3,7},{4,0},{5,1},{6,2},{7,3},{8,12},{9,13},{10,... | collective-permute-start | bytes 776 | tf_op jit(solution)/shard_map/ppermute | solution.py:49
  28.2 14.0 %collective-permute-start.3 = (s32[1,64]{1,0:T(1,128)S(1)}, s32[1,64]{1,0:T(1,128)S(1)}, u32[]{:S(2)}, u32[]{:S(2)}) collective-permute-start(s32[1,64]{1,0:T(1,128)S(1)} %get-tuple-element.43), channel_id=1, source_target_pairs={{0,6},{1,7},{2,4},{3,5},{4,2},{5,3},{6,0},{7,1},{8,14},{9,15},{10,... | collective-permute-start | bytes 776 | tf_op jit(solution)/shard_map/ppermute | solution.py:49
  44.0 0.6 copy-start.1
  45.1 5.7 %copy-start.2 = (bf16[128,320]{1,0:T(8,128)(2,1)S(1)}, bf16[128,320]{1,0:T(8,128)(2,1)}, u32[]{:S(2)}) copy-start(bf16[128,320]{1,0:T(8,128)(2,1)} %copy-done.1) | copy-start | bytes 245764
  51.7 18.7 %collective-permute-start.8 = (bf16[128,768]{1,0:T(8,128)(2,1)}, bf16[128,768]{1,0:T(8,128)(2,1)S(1)}, u32[]{:S(2)}, u32[]{:S(2)}) collective-permute-start(bf16[128,768]{1,0:T(8,128)(2,1)} %fusion.12), channel_id=1, source_target_pairs={{0,4},{1,5},{2,6},{3,7},{4,0},{5,1},{6,2},{7,3},{8,12},{9,13},{10,... | collective-permute-start | bytes 589832 | tf_op jit(solution)/shard_map/ppermute | solution.py:49
  58.6 11.8 %collective-permute-start.10 = (bf16[128,768]{1,0:T(8,128)(2,1)}, bf16[128,768]{1,0:T(8,128)(2,1)S(1)}, u32[]{:S(2)}, u32[]{:S(2)}) collective-permute-start(bf16[128,768]{1,0:T(8,128)(2,1)} %fusion.13), channel_id=1, source_target_pairs={{0,2},{1,3},{2,0},{3,1},{4,6},{5,7},{6,4},{7,5},{8,10},{9,11},{10,... | collective-permute-start | bytes 589832 | tf_op jit(solution)/shard_map/ppermute | solution.py:49
  65.6 6.5 %collective-permute-start.6 = (bf16[128,768]{1,0:T(8,128)(2,1)S(1)}, bf16[128,768]{1,0:T(8,128)(2,1)S(1)}, u32[]{:S(2)}, u32[]{:S(2)}) collective-permute-start(bf16[128,768]{1,0:T(8,128)(2,1)S(1)} %fusion.11), channel_id=1, source_target_pairs={{0,6},{1,7},{2,4},{3,5},{4,2},{5,3},{6,0},{7,1},{8,14},{9,15},{10,... | collective-permute-start | bytes 589832 | tf_op jit(solution)/shard_map/ppermute | solution.py:49
  70.4 2.3 %copy-start.3 = (f32[768]{0:T(1024)S(1)}, f32[768]{0:T(1024)}, u32[]{:S(2)}) copy-start(f32[768]{0:T(1024)} %param.11) | copy-start | bytes 9220
  70.4 6.4 %copy-start.5 = (s32[256]{0:T(256)S(1)}, s32[256]{0:T(256)}, u32[]{:S(2)}) copy-start(s32[256]{0:T(256)} %copy-done.4) | copy-start | bytes 3076
  72.6 16.1 %copy-start.8 = (s32[256]{0:T(256)S(1)}, s32[256]{0:T(256)}, u32[]{:S(2)}) copy-start(s32[256]{0:T(256)} %eq.228) | copy-start | bytes 3076
  72.7 16.1 %copy-start.9 = (bf16[1280,768]{1,0:T(8,128)(2,1)S(1)}, bf16[1280,768]{1,0:T(8,128)(2,1)}, u32[]{:S(2)}) copy-start(bf16[1280,768]{1,0:T(8,128)(2,1)} %param.15) | copy-start | bytes 5898244
  72.8 4.0 %collective-permute-start.11 = (bf16[128,768]{1,0:T(8,128)(2,1)S(1)}, bf16[128,768]{1,0:T(8,128)(2,1)S(1)}, u32[]{:S(2)}, u32[]{:S(2)}) collective-permute-start(bf16[128,768]{1,0:T(8,128)(2,1)S(1)} %multiply_convert_fusion), channel_id=1, source_target_pairs={{0,1},{1,0},{2,3},{3,2},{4,5},{5,4},{6,7},{7,6},{8,9},{9,8},{10,11... | collective-permute-start | bytes 589832 | tf_op jit(solution)/shard_map/ppermute | solution.py:45
  77.1 5.2 %collective-permute-start.12 = (bf16[64,768]{1,0:T(8,128)(2,1)S(1)}, bf16[64,768]{1,0:T(8,128)(2,1)S(1)}, u32[]{:S(2)}, u32[]{:S(2)}) collective-permute-start(bf16[64,768]{1,0:T(8,128)(2,1)S(1)} %get-tuple-element.19), channel_id=1, source_target_pairs={{0,2},{1,3},{2,0},{3,1},{4,6},{5,7},{6,4},{7,5},{8,10},{9,11},{10,... | collective-permute-start | bytes 294920 | tf_op jit(solution)/shard_map/ppermute | solution.py:49
  79.4 9.3 %collective-permute-start.13 = (bf16[64,768]{1,0:T(8,128)(2,1)S(1)}, bf16[64,768]{1,0:T(8,128)(2,1)S(1)}, u32[]{:S(2)}, u32[]{:S(2)}) collective-permute-start(bf16[64,768]{1,0:T(8,128)(2,1)S(1)} %get-tuple-element.18), channel_id=1, source_target_pairs={{0,4},{1,5},{2,6},{3,7},{4,0},{5,1},{6,2},{7,3},{8,12},{9,13},{10,... | collective-permute-start | bytes 294920 | tf_op jit(solution)/shard_map/ppermute | solution.py:49
  79.5 9.2 %collective-permute-start.14 = (bf16[64,768]{1,0:T(8,128)(2,1)S(1)}, bf16[64,768]{1,0:T(8,128)(2,1)S(1)}, u32[]{:S(2)}, u32[]{:S(2)}) collective-permute-start(bf16[64,768]{1,0:T(8,128)(2,1)S(1)} %get-tuple-element.17), channel_id=1, source_target_pairs={{0,6},{1,7},{2,4},{3,5},{4,2},{5,3},{6,0},{7,1},{8,14},{9,15},{10,... | collective-permute-start | bytes 294920 | tf_op jit(solution)/shard_map/ppermute | solution.py:49
  90.7 11.1 %collective-permute-start.15 = (bf16[64,64]{0,1:T(8,128)(2,1)S(1)}, bf16[64,64]{0,1:T(8,128)(2,1)S(1)}, u32[]{:S(2)}, u32[]{:S(2)}) collective-permute-start(bf16[64,64]{0,1:T(8,128)(2,1)S(1)} %get-tuple-element.23), channel_id=1, source_target_pairs={{0,2},{1,3},{2,0},{3,1},{4,6},{5,7},{6,4},{7,5},{8,10},{9,11},{10,... | collective-permute-start | bytes 24584 | tf_op jit(solution)/shard_map/ppermute | solution.py:49
  93.1 8.7 %collective-permute-start.16 = (bf16[64,64]{0,1:T(8,128)(2,1)S(1)}, bf16[64,64]{0,1:T(8,128)(2,1)S(1)}, u32[]{:S(2)}, u32[]{:S(2)}) collective-permute-start(bf16[64,64]{0,1:T(8,128)(2,1)S(1)} %get-tuple-element.22), channel_id=1, source_target_pairs={{0,4},{1,5},{2,6},{3,7},{4,0},{5,1},{6,2},{7,3},{8,12},{9,13},{10,... | collective-permute-start | bytes 24584 | tf_op jit(solution)/shard_map/ppermute | solution.py:49
  93.1 8.8 %collective-permute-start.17 = (bf16[64,64]{0,1:T(8,128)(2,1)S(1)}, bf16[64,64]{0,1:T(8,128)(2,1)S(1)}, u32[]{:S(2)}, u32[]{:S(2)}) collective-permute-start(bf16[64,64]{0,1:T(8,128)(2,1)S(1)} %get-tuple-element.21), channel_id=1, source_target_pairs={{0,6},{1,7},{2,4},{3,5},{4,2},{5,3},{6,0},{7,1},{8,14},{9,15},{10,... | collective-permute-start | bytes 24584 | tf_op jit(solution)/shard_map/ppermute | solution.py:49
  96.5 14.6 %all-to-all-start.1 = ((f32[32,2,768]{2,1,0:T(2,128)}), f32[32,2,768]{2,1,0:T(2,128)S(1)}, u32[]{:S(2)}, u32[]{:S(2)}) async-start(f32[32,2,768]{2,1,0:T(2,128)} %reshape.135), calls=%async_computation.1 | async-start | bytes 393216 | tf_op jit(solution)/shard_map/all_to_all | solution.py:13
  102.1 2.3 %collective-permute-start.18 = (bf16[128,64]{0,1:T(8,128)(2,1)S(1)}, bf16[128,64]{0,1:T(8,128)(2,1)S(1)}, u32[]{:S(2)}, u32[]{:S(2)}) collective-permute-start(bf16[128,64]{0,1:T(8,128)(2,1)S(1)} %slice.275), channel_id=1, source_target_pairs={{0,1},{1,0},{2,3},{3,2},{4,5},{5,4},{6,7},{7,6},{8,9},{9,8},{10,11... | collective-permute-start | bytes 49160 | tf_op jit(solution)/shard_map/ppermute | solution.py:45

commit v3 on v2

--- a/solution.py
+++ b/solution.py
@@ -1,6 +1,9 @@
+import functools
 import jax
 import jax.numpy as jnp
 from jax import lax
+from jax.experimental import pallas as pl
+from jax.experimental.pallas import tpu as pltpu
 from jax.sharding import PartitionSpec as P
 
 BF16 = jnp.bfloat16
@@ -140,6 +143,92 @@
     ref_grad = jnp.dot(ref_errors, all_docs, preferred_element_type=F32).astype(BF16)
     doc_grad = jnp.sum(exchange(doc_terms.reshape(devices, own_docs, width), ALL), axis=0)
     return (free_grad, doc_grad, ref_grad)
+
+
+LANES = 128
+SUBLANES = 8
+PIECES = 4
+
+
+def sum_kernel(length, starts_ref, near_ref, far_ref, *refs):
+    outs, (stage, rows, sums, sems) = refs[:-4], refs[-4:]
+    vocab_rows, width = near_ref.shape
+    chunks = width // LANES
+    tile = SUBLANES * chunks
+    labels = outs[0].shape[0]
+    piece = vocab_rows // PIECES
+
+    copies = []
+    for half, table in enumerate((near_ref, far_ref)):
+        for p in range(PIECES):
+            at = half * PIECES + p
+            copies.append(
+                pltpu.make_async_copy(
+                    table.at[pl.ds(p * piece, piece)], stage.at[pl.ds(at * piece, piece)], sems.at[at]
+                )
+            )
+    for copy in copies:
+        copy.start()
+    rows[pl.ds(2 * vocab_rows * chunks, tile), :] = jnp.zeros((tile, LANES), F32)
+    for at, copy in enumerate(copies):
+        copy.wait()
+
+        @pl.loop(0, piece // 16, unroll=4)
+        def _(group):
+            first = pl.multiple_of(at * piece + group * 16, 16)
+            block = stage[pl.ds(first, 16), :].astype(F32)
+            to = pl.multiple_of(first * chunks, 16)
+            for h in range(2):
+                for c in range(chunks):
+                    rows[pl.ds(to + h * tile + c * SUBLANES, SUBLANES), :] = block[
+                        h * SUBLANES : (h + 1) * SUBLANES, c * LANES : (c + 1) * LANES
+                    ]
+
+    @pl.loop(0, len(outs) * labels // SUBLANES)
+    def _(group):
+        for q in range(SUBLANES):
+            first = (group * SUBLANES + q) * length
+            terms = [
+                rows[pl.ds(starts_ref[first + j], chunks, stride=SUBLANES), :] for j in range(length)
+            ]
+            while len(terms) > 1:
+                terms = [a + b for a, b in zip(terms[::2], terms[1::2])] + terms[len(terms) // 2 * 2 :]
+            sums[pl.ds(group * tile + q, chunks, stride=SUBLANES), :] = terms[0] / length
+
+    for n, out in enumerate(outs):
+        for group in range(labels // 16):
+            for c in range(chunks):
+                at = ((n * labels) // SUBLANES + 2 * group) * tile + c * SUBLANES
+                out[16 * group : 16 * group + 16, c * LANES : (c + 1) * LANES] = jnp.concatenate(
+                    [sums[at : at + SUBLANES, :], sums[at + tile : at + tile + SUBLANES, :]]
+                ).astype(out.dtype)
+
+
+def partial_means(starts, near, far, labels, length, kinds):
+    vocab_rows, width = near.shape
+    chunks = width // LANES
+    return pl.pallas_call(
+        functools.partial(sum_kernel, length),
+        out_shape=[jax.ShapeDtypeStruct((labels, width), kind) for kind in kinds],
+        in_specs=[
+            pl.BlockSpec(memory_space=pltpu.SMEM),
+            pl.BlockSpec(memory_space=pl.ANY),
+            pl.BlockSpec(memory_space=pl.ANY),
+        ],
+        out_specs=[pl.BlockSpec(memory_space=pltpu.VMEM) for _ in kinds],
+        scratch_shapes=[
+            pltpu.VMEM((2 * vocab_rows, width), BF16),
+            pltpu.VMEM(((2 * vocab_rows + 2 * SUBLANES) * chunks, LANES), F32),
+            pltpu.VMEM(((len(kinds) * labels + SUBLANES) * chunks, LANES), F32),
+            pltpu.SemaphoreType.DMA((2 * PIECES,)),
+        ],
+        compiler_params=pltpu.CompilerParams(vmem_limit_bytes=56 * 1024 * 1024),
+        cost_estimate=pl.CostEstimate(
+            flops=len(kinds) * labels * length * width,
+            bytes_accessed=4 * vocab_rows * width,
+            transcendentals=0,
+        ),
+    )(starts, near, far)
 
 
 def by_sums(
@@ -156,21 +245,13 @@
     pos_count = positives.shape[1]
     slab_rows = free_rows.shape[0]
     tokens = labels * length
-    token_cap = 5 * tokens // (4 * shards)
     label_cap = 2 * labels // shards
     others = [k for k in range(chips - 1, 0, -1)]
-    stride = 2 * labels
 
     other_table = swap_cores(token_table)
 
-    token_owner = label_tokens // vocab_rows
-    token_dest = token_places(token_owner ^ me, shards, token_cap)
-    codes = (label_tokens - token_owner * vocab_rows) * stride + jnp.arange(labels, dtype=I32)[:, None]
-    hit = token_dest.reshape(tokens)[:, None] == jnp.arange(shards * token_cap, dtype=I32)[None, :]
-    asks = labels + jnp.sum(jnp.where(hit, codes.reshape(tokens)[:, None] - labels, 0), axis=0)
-    asks = asks.reshape(chips, 2 * token_cap)
-    asked = {k: to_chip(asks[k : k + 1], k) for k in others}
-    asked[0] = asks[0:1]
+    asked = {k: to_chip(label_tokens, k) for k in others}
+    asked[0] = label_tokens
 
     label_dest = label_places(ref_owner[:, 0] ^ me, shards, label_cap)
     mine = jnp.stack([label_dest, ref_row])
@@ -206,18 +287,26 @@
     d = all_blocks[:, width : width + 3 * pos_count].astype(I32)
     all_positives = d[:, :pos_count] + 256 * d[:, pos_count : 2 * pos_count] + 65536 * d[:, 2 * pos_count :]
 
-    def partial(code):
-        ids = code[0] // stride
-        which = code[0] - ids * stride
-        pick = (jnp.arange(labels, dtype=I32)[:, None] == which[None, :]).astype(BF16) / length
-        near = token_table[ids[:token_cap]]
-        far = other_table[ids[token_cap:]]
-        return jnp.dot(pick[:, :token_cap], near, preferred_element_type=F32) + jnp.dot(
-            pick[:, token_cap:], far, preferred_element_type=F32
+    def starts(ks):
+        ids = jnp.concatenate([asked[k] for k in ks])
+        near = ids - me * vocab_rows
+        far = ids - (me ^ 1) * vocab_rows
+        row = jnp.where(
+            (near >= 0) & (near < vocab_rows),
+            near,
+            jnp.where((far >= 0) & (far < vocab_rows), far + vocab_rows, 2 * vocab_rows),
         )
-
-    arrived = [to_chip(partial(asked[k]).astype(BF16), k) for k in others]
-    pooled = partial(asked[0])
+        first = (row // SUBLANES) * (SUBLANES * (width // LANES)) + row % SUBLANES
+        return first.reshape(len(ks) * tokens)
+
+    sent = []
+    half = len(others) - len(others) // 3
+    for ks in (others[:half], others[half:] + [0]):
+        sent += partial_means(
+            starts(ks), token_table, other_table, labels, length, [BF16 if k else F32 for k in ks]
+        )
+    arrived = [to_chip(term, k) for term, k in zip(sent, others)]
+    pooled = sent[-1]
     for term in arrived:
         pooled = pooled + term.astype(F32)
     pooled = pooled.astype(BF16)

time: 112 us -> 101 us (0.902)
  local copies, waits for them, and re-layouts: 42 us -> 4.5 us
  Pallas kernels: 0 us -> 17.9 us
  waiting for transfers between devices: 15.4 us -> 31.9 us
  starting transfers between devices: 36.6 us -> 32.8 us
  matrix products: 9.51 us -> 6.24 us
    gather x8 -> x0, local copies, waits for them, and re-layouts: 36.5 us -> none  [the longest x4 18.5 us: partial(): far = other_table[ids[token_cap:]]]
    pallas_call x0 -> x2, Pallas kernels: none -> 17.9 us  [partial_means(): pl.pallas_call(functools.partial(sum_kernel, length), out_shape=[jax.Shap...]
    ppermute x15, waiting for transfers between devices: 8.55 us -> 25.1 us  [to_chip(): lax.ppermute(x, 'shard', [(i, i ^ 2 * k) for i in range(lax.axis_size('sh...]
    dot_general x7 -> x0, matrix products: 2.91 us -> none  [the longest x3 2.12 us: partial(): jnp.dot(pick[:, token_cap:], far, preferred_element_type=F32)]
    ppermute x4, starting transfers between devices: 4.49 us -> 2.18 us  [swap_cores(): lax.ppermute(x, 'shard', [(i, i ^ 1) for i in range(lax.axis_size('shard'...]
    gather x8 -> x0, other arithmetic: 1.22 us -> none  [the longest x4 1.19 us: partial(): far = other_table[ids[token_cap:]]]
    add x2, other arithmetic: 0.01 us -> 1.22 us  [starts(): first = row // SUBLANES * (SUBLANES * (width // LANES)) + row % SUBLANES]
    all_to_all x2, starting transfers between devices: 11.4 us -> 10.2 us  [exchange(): return lax.all_to_all(blocks, axes, split_axis=0, concat_axis=0, tiled=True)]
  transfers between devices with their start and end apart: 21 -> 21, of which waited for: 5 -> 8; matrix products, arithmetic and copies ran while one was open for 42% -> 14% of each run, Pallas kernels for 0% -> 9%
where the time goes in v3:
time: 101 us
  starting transfers between devices  32.8 us (32%)
  waiting for transfers between devices  31.9 us (32%)
  Pallas kernels  17.9 us (18%)
  other arithmetic  6.31 us (6%)
  matrix products  6.24 us (6%)
  local copies, waits for them, and re-layouts  4.5 us (4%)
    ppermute x15, waiting for transfers between devices, to_chip(): lax.ppermute(x, 'shard', [(i, i ^ 2 * k) for i in range(lax.axis_size('sh...  25.1 us
    ppermute x15, starting transfers between devices, to_chip(): lax.ppermute(x, 'shard', [(i, i ^ 2 * k) for i in range(lax.axis_size('sh...  20.4 us
    pallas_call x2, Pallas kernels, partial_means(): pl.pallas_call(functools.partial(sum_kernel, length), out_shape=[jax.Shap...  17.9 us
    all_to_all x2, starting transfers between devices, exchange(): return lax.all_to_all(blocks, axes, split_axis=0, concat_axis=0, tiled=True)  10.2 us
    all_to_all x2, waiting for transfers between devices, exchange(): return lax.all_to_all(blocks, axes, split_axis=0, concat_axis=0, tiled=True)  5.83 us
    ppermute x4, starting transfers between devices, swap_cores(): lax.ppermute(x, 'shard', [(i, i ^ 1) for i in range(lax.axis_size('shard'...  2.18 us
  transfers between devices with their start and end apart: 21, of which 8 were waited for; matrix products, arithmetic and copies ran while one was open for 14% of the time, Pallas kernels for 9%

profile of v3, /device:TPU:1, one launch (start us, length us, event | category | flops | bytes accessed | tf_op | source)
XLA Modules:
  0.0 100.6 jit_solution(8901985994918776878)
XLA Ops:
  0.8 2.8 %collective-permute-start.4 = (s32[128,8]{0,1:T(8,128)}, s32[128,8]{0,1:T(8,128)S(1)}, u32[]{:S(2)}, u32[]{:S(2)}) collective-permute-start(s32[128,8]{0,1:T(8,128)} %param.12), channel_id=1, source_target_pairs={{0,2},{1,3},{2,0},{3,1},{4,6},{5,7},{6,4},{7,5},{8,10},{9,11},{10,... | collective-permute-start | bytes 12296 | tf_op jit(solution)/shard_map/ppermute | solution.py:52
  3.5 0.7 fusion.56
  4.3 0.7 bitcast_add_fusion
  5.0 0.7 pad_add_fusion.1
  5.7 0.3 collective-permute-start
  6.0 0.7 shift-right-arithmetic_convert_fusion
  6.7 0.8 concatenate.36
  7.5 0.7 broadcast_in_dim.25
  8.2 4.7 %all-to-all-start = ((bf16[32,2,896]{2,1,0:T(2,128)(2,1)}), bf16[32,2,896]{2,1,0:T(2,128)(2,1)S(1)}, u32[]{:S(2)}, u32[]{:S(2)}) async-start(bf16[32,2,896]{2,1,0:T(2,128)(2,1)} %broadcast_in_dim.25), calls=%async_computation | async-start | bytes 229376 | tf_op jit(solution)/shard_map/all_to_all | solution.py:16
  13.0 0.7 compare_select_fusion.5
  13.7 0.7 add_add_fusion
  14.6 1.4 %collective-permute-start.1 = (s32[1,64]{1,0:T(1,128)S(1)}, s32[1,64]{1,0:T(1,128)S(1)}, u32[]{:S(2)}, u32[]{:S(2)}) collective-permute-start(s32[1,64]{1,0:T(1,128)S(1)} %get-tuple-element.34), channel_id=1, source_target_pairs={{0,2},{1,3},{2,0},{3,1},{4,6},{5,7},{6,4},{7,5},{8,10},{9,11},{10,... | collective-permute-start | bytes 776 | tf_op jit(solution)/shard_map/ppermute | solution.py:52
  16.0 2.1 %collective-permute-start.2 = (s32[1,64]{1,0:T(1,128)S(1)}, s32[1,64]{1,0:T(1,128)S(1)}, u32[]{:S(2)}, u32[]{:S(2)}) collective-permute-start(s32[1,64]{1,0:T(1,128)S(1)} %get-tuple-element.33), channel_id=1, source_target_pairs={{0,4},{1,5},{2,6},{3,7},{4,0},{5,1},{6,2},{7,3},{8,12},{9,13},{10,... | collective-permute-start | bytes 776 | tf_op jit(solution)/shard_map/ppermute | solution.py:52
  18.1 3.2 %collective-permute-start.6 = (s32[128,8]{0,1:T(8,128)}, s32[128,8]{0,1:T(8,128)S(1)}, u32[]{:S(2)}, u32[]{:S(2)}) collective-permute-start(s32[128,8]{0,1:T(8,128)} %param.12), channel_id=1, source_target_pairs={{0,6},{1,7},{2,4},{3,5},{4,2},{5,3},{6,0},{7,1},{8,14},{9,15},{10,... | collective-permute-start | bytes 12296 | tf_op jit(solution)/shard_map/ppermute | solution.py:52
  21.4 0.9 collective-permute-done.3
  22.4 0.7 constant_dynamic-update-slice_fusion
  23.6 1.3 %collective-permute-done.7 = s32[128,8]{0,1:T(8,128)S(1)} collective-permute-done((s32[128,8]{0,1:T(8,128)}, s32[128,8]{0,1:T(8,128)S(1)}, u32[]{:S(2)}, u32[]{:S(2)}) %collective-permute-start.7) | collective-permute-done | bytes 4128 | tf_op jit(solution)/shard_map/ppermute | solution.py:52
  25.4 0.6 fusion.39.starts_ref
  26.1 0.6 fusion.41.starts_ref
  26.7 8.9 %shard_map.112 = (bf16[128,768]{1,0:T(8,128)(2,1)}, f32[128,768]{1,0:T(8,128)}) custom-call(s32[2048]{0:T(1024)} %fusion.39.starts_ref, bf16[3840,768]{1,0:T(8,128)(2,1)} %near_ref.3, bf16[3840,768]{1,0:T(8,128)(2,1)} %collective-permute-done.5.far_ref), custom_call_target="tpu_custom_call" | custom-call | flops 1572864 | bytes 11796480 | tf_op jit(solution)/shard_map/pallas_call | solution.py:210
  35.7 9.0 %shard_map.113 = (bf16[128,768]{1,0:T(8,128)(2,1)}, bf16[128,768]{1,0:T(8,128)(2,1)}) custom-call(s32[2048]{0:T(1024)} %fusion.41.starts_ref, bf16[3840,768]{1,0:T(8,128)(2,1)} %near_ref.3, bf16[3840,768]{1,0:T(8,128)(2,1)} %collective-permute-done.5.far_ref), custom_call_target="tpu_custom_call" | custom-call | flops 1572864 | bytes 11796480 | tf_op jit(solution)/shard_map/pallas_call | solution.py:210
  44.8 1.5 %collective-permute-start.8 = (bf16[128,768]{1,0:T(8,128)(2,1)}, bf16[128,768]{1,0:T(8,128)(2,1)S(1)}, u32[]{:S(2)}, u32[]{:S(2)}) collective-permute-start(bf16[128,768]{1,0:T(8,128)(2,1)} %get-tuple-element.8), channel_id=1, source_target_pairs={{0,6},{1,7},{2,4},{3,5},{4,2},{5,3},{6,0},{7,1},{8,14},{9,15},{10,... | collective-permute-start | bytes 589832 | tf_op jit(solution)/shard_map/ppermute | solution.py:52
  46.2 1.1 %collective-permute-start.9 = (bf16[128,768]{1,0:T(8,128)(2,1)}, bf16[128,768]{1,0:T(8,128)(2,1)S(1)}, u32[]{:S(2)}, u32[]{:S(2)}) collective-permute-start(bf16[128,768]{1,0:T(8,128)(2,1)} %get-tuple-element.9), channel_id=1, source_target_pairs={{0,4},{1,5},{2,6},{3,7},{4,0},{5,1},{6,2},{7,3},{8,12},{9,13},{10,... | collective-permute-start | bytes 589832 | tf_op jit(solution)/shard_map/ppermute | solution.py:52
  47.3 4.1 %collective-permute-done.8 = bf16[128,768]{1,0:T(8,128)(2,1)S(1)} collective-permute-done((bf16[128,768]{1,0:T(8,128)(2,1)}, bf16[128,768]{1,0:T(8,128)(2,1)S(1)}, u32[]{:S(2)}, u32[]{:S(2)}) %collective-permute-start.8) | collective-permute-done | bytes 196640 | tf_op jit(solution)/shard_map/ppermute | solution.py:52
  51.5 13.3 %collective-permute-done.9 = bf16[128,768]{1,0:T(8,128)(2,1)S(1)} collective-permute-done((bf16[128,768]{1,0:T(8,128)(2,1)}, bf16[128,768]{1,0:T(8,128)(2,1)S(1)}, u32[]{:S(2)}, u32[]{:S(2)}) %collective-permute-start.9) | collective-permute-done | bytes 196640 | tf_op jit(solution)/shard_map/ppermute | solution.py:52
  64.7 0.4 multiply_reduce_fusion
  65.3 1.4 %collective-permute-start.11 = (bf16[128,768]{1,0:T(8,128)(2,1)S(1)}, bf16[128,768]{1,0:T(8,128)(2,1)S(1)}, u32[]{:S(2)}, u32[]{:S(2)}) collective-permute-start(bf16[128,768]{1,0:T(8,128)(2,1)S(1)} %multiply_convert_fusion), channel_id=1, source_target_pairs={{0,1},{1,0},{2,3},{3,2},{4,5},{5,4},{6,7},{7,6},{8,9},{9,8},{10,11... | collective-permute-start | bytes 589832 | tf_op jit(solution)/shard_map/ppermute | solution.py:48
  66.8 1.0 collective-permute-done.11
  67.7 0.3 convolution_convert_fusion.1
  68.1 1.7 %collective-permute-start.13 = (bf16[64,768]{1,0:T(8,128)(2,1)S(1)}, bf16[64,768]{1,0:T(8,128)(2,1)S(1)}, u32[]{:S(2)}, u32[]{:S(2)}) collective-permute-start(bf16[64,768]{1,0:T(8,128)(2,1)S(1)} %get-tuple-element.18), channel_id=1, source_target_pairs={{0,4},{1,5},{2,6},{3,7},{4,0},{5,1},{6,2},{7,3},{8,12},{9,13},{10,... | collective-permute-start | bytes 294920 | tf_op jit(solution)/shard_map/ppermute | solution.py:52
  69.8 1.9 %collective-permute-start.14 = (bf16[64,768]{1,0:T(8,128)(2,1)S(1)}, bf16[64,768]{1,0:T(8,128)(2,1)S(1)}, u32[]{:S(2)}, u32[]{:S(2)}) collective-permute-start(bf16[64,768]{1,0:T(8,128)(2,1)S(1)} %get-tuple-element.17), channel_id=1, source_target_pairs={{0,6},{1,7},{2,4},{3,5},{4,2},{5,3},{6,0},{7,1},{8,14},{9,15},{10,... | collective-permute-start | bytes 294920 | tf_op jit(solution)/shard_map/ppermute | solution.py:52
  71.7 0.2 slice_reduce_fusion.4
  71.9 1.4 %collective-permute-done.12 = bf16[64,768]{1,0:T(8,128)(2,1)S(1)} collective-permute-done((bf16[64,768]{1,0:T(8,128)(2,1)S(1)}, bf16[64,768]{1,0:T(8,128)(2,1)S(1)}, u32[]{:S(2)}, u32[]{:S(2)}) %collective-permute-start.12) | collective-permute-done | bytes 98336 | tf_op jit(solution)/shard_map/ppermute | solution.py:52
  73.3 4.1 %collective-permute-done.13 = bf16[64,768]{1,0:T(8,128)(2,1)S(1)} collective-permute-done((bf16[64,768]{1,0:T(8,128)(2,1)S(1)}, bf16[64,768]{1,0:T(8,128)(2,1)S(1)}, u32[]{:S(2)}, u32[]{:S(2)}) %collective-permute-start.13) | collective-permute-done | bytes 98336 | tf_op jit(solution)/shard_map/ppermute | solution.py:52
  77.4 0.7 fusion
  78.1 0.8 fusion.5
  78.9 0.3 fusion.7
  79.3 2.4 %collective-permute-start.15 = (bf16[64,64]{0,1:T(8,128)(2,1)S(1)}, bf16[64,64]{0,1:T(8,128)(2,1)S(1)}, u32[]{:S(2)}, u32[]{:S(2)}) collective-permute-start(bf16[64,64]{0,1:T(8,128)(2,1)S(1)} %get-tuple-element.23), channel_id=1, source_target_pairs={{0,2},{1,3},{2,0},{3,1},{4,6},{5,7},{6,4},{7,5},{8,10},{9,11},{10,... | collective-permute-start | bytes 24584 | tf_op jit(solution)/shard_map/ppermute | solution.py:52
  81.7 0.3 collective-permute-start.16
  82.0 1.9 %collective-permute-start.17 = (bf16[64,64]{0,1:T(8,128)(2,1)S(1)}, bf16[64,64]{0,1:T(8,128)(2,1)S(1)}, u32[]{:S(2)}, u32[]{:S(2)}) collective-permute-start(bf16[64,64]{0,1:T(8,128)(2,1)S(1)} %get-tuple-element.21), channel_id=1, source_target_pairs={{0,6},{1,7},{2,4},{3,5},{4,2},{5,3},{6,0},{7,1},{8,14},{9,15},{10,... | collective-permute-start | bytes 24584 | tf_op jit(solution)/shard_map/ppermute | solution.py:52
  83.9 0.5 fusion.59
  84.3 0.8 reshape.126
  85.1 5.5 %all-to-all-start.1 = ((f32[32,2,768]{2,1,0:T(2,128)}), f32[32,2,768]{2,1,0:T(2,128)S(1)}, u32[]{:S(2)}, u32[]{:S(2)}) async-start(f32[32,2,768]{2,1,0:T(2,128)} %reshape.126), calls=%async_computation.1 | async-start | bytes 393216 | tf_op jit(solution)/shard_map/all_to_all | solution.py:16
  90.9 0.3 collective-permute-start.18
  91.2 2.0 %convolution_convert_fusion = bf16[1280,768]{1,0:T(8,128)(2,1)} fusion(bf16[64,1280]{1,0:T(8,128)(2,1)S(1)} %fusion.5, bf16[64,896]{1,0:T(8,128)(2,1)S(1)} %reshape.125), kind=kOutput, calls=%fused_computation.1 | convolution fusion | flops 126812160 | bytes 2228224 | tf_op jit(solution)/shard_map/dot_general | solution.py:344
  93.2 0.9 convolution_convert_fusion.2
  94.1 5.8 %all-to-all-done.1 = f32[32,2,768]{2,1,0:T(2,128)S(1)} async-done(((f32[32,2,768]{2,1,0:T(2,128)}), f32[32,2,768]{2,1,0:T(2,128)S(1)}, u32[]{:S(2)}, u32[]{:S(2)}) %all-to-all-start.1) | async-done | bytes 196640 | tf_op jit(solution)/shard_map/all_to_all | solution.py:16
  99.9 0.7 reduce_sum.42
  (59 shorter events, 2.4 us)
Async XLA Ops:
  0.6 64.1 %copy-start = (bf16[768,768]{1,0:T(8,128)(2,1)S(1)}, bf16[768,768]{1,0:T(8,128)(2,1)}, u32[]{:S(2)}) copy-start(bf16[768,768]{1,0:T(8,128)(2,1)} %param.10) | copy-start | bytes 3538948
  0.6 26.1 %collective-permute-start.5 = (bf16[3840,768]{1,0:T(8,128)(2,1)}, bf16[3840,768]{1,0:T(8,128)(2,1)}, u32[]{:S(2)}, u32[]{:S(2)}) collective-permute-start(bf16[3840,768]{1,0:T(8,128)(2,1)} %near_ref.3), channel_id=1, source_target_pairs={{0,1},{1,0},{2,3},{3,2},{4,5},{5,4},{6,7},{7,6},{8,9},{9,8},{10,11... | collective-permute-start | bytes 17694728 | tf_op jit(solution)/shard_map/ppermute | solution.py:48
  0.8 21.6 %collective-permute-start.4 = (s32[128,8]{0,1:T(8,128)}, s32[128,8]{0,1:T(8,128)S(1)}, u32[]{:S(2)}, u32[]{:S(2)}) collective-permute-start(s32[128,8]{0,1:T(8,128)} %param.12), channel_id=1, source_target_pairs={{0,2},{1,3},{2,0},{3,1},{4,6},{5,7},{6,4},{7,5},{8,10},{9,11},{10,... | collective-permute-start | bytes 12296 | tf_op jit(solution)/shard_map/ppermute | solution.py:52
  5.7 8.0 %collective-permute-start = (s32[2,128]{1,0:T(2,128)S(1)}, s32[2,128]{1,0:T(2,128)S(1)}, u32[]{:S(2)}, u32[]{:S(2)}) collective-permute-start(s32[2,128]{1,0:T(2,128)S(1)} %pad_add_fusion.1), channel_id=1, source_target_pairs={{0,1},{1,0},{2,3},{3,2},{4,5},{5,4},{6,7},{7,6},{8,9},{9,8},{10,11... | collective-permute-start | bytes 3080 | tf_op jit(solution)/shard_map/ppermute | solution.py:48
  8.2 18.5 %all-to-all-start = ((bf16[32,2,896]{2,1,0:T(2,128)(2,1)}), bf16[32,2,896]{2,1,0:T(2,128)(2,1)S(1)}, u32[]{:S(2)}, u32[]{:S(2)}) async-start(bf16[32,2,896]{2,1,0:T(2,128)(2,1)} %broadcast_in_dim.25), calls=%async_computation | async-start | bytes 229376 | tf_op jit(solution)/shard_map/all_to_all | solution.py:16
  14.6 3.6 %collective-permute-start.1 = (s32[1,64]{1,0:T(1,128)S(1)}, s32[1,64]{1,0:T(1,128)S(1)}, u32[]{:S(2)}, u32[]{:S(2)}) collective-permute-start(s32[1,64]{1,0:T(1,128)S(1)} %get-tuple-element.34), channel_id=1, source_target_pairs={{0,2},{1,3},{2,0},{3,1},{4,6},{5,7},{6,4},{7,5},{8,10},{9,11},{10,... | collective-permute-start | bytes 776 | tf_op jit(solution)/shard_map/ppermute | solution.py:52
  16.0 5.4 %collective-permute-start.2 = (s32[1,64]{1,0:T(1,128)S(1)}, s32[1,64]{1,0:T(1,128)S(1)}, u32[]{:S(2)}, u32[]{:S(2)}) collective-permute-start(s32[1,64]{1,0:T(1,128)S(1)} %get-tuple-element.33), channel_id=1, source_target_pairs={{0,4},{1,5},{2,6},{3,7},{4,0},{5,1},{6,2},{7,3},{8,12},{9,13},{10,... | collective-permute-start | bytes 776 | tf_op jit(solution)/shard_map/ppermute | solution.py:52
  18.1 4.2 %collective-permute-start.3 = (s32[1,64]{1,0:T(1,128)S(1)}, s32[1,64]{1,0:T(1,128)S(1)}, u32[]{:S(2)}, u32[]{:S(2)}) collective-permute-start(s32[1,64]{1,0:T(1,128)S(1)} %get-tuple-element.32), channel_id=1, source_target_pairs={{0,6},{1,7},{2,4},{3,5},{4,2},{5,3},{6,0},{7,1},{8,14},{9,15},{10,... | collective-permute-start | bytes 776 | tf_op jit(solution)/shard_map/ppermute | solution.py:52
  18.1 5.0 %collective-permute-start.6 = (s32[128,8]{0,1:T(8,128)}, s32[128,8]{0,1:T(8,128)S(1)}, u32[]{:S(2)}, u32[]{:S(2)}) collective-permute-start(s32[128,8]{0,1:T(8,128)} %param.12), channel_id=1, source_target_pairs={{0,6},{1,7},{2,4},{3,5},{4,2},{5,3},{6,0},{7,1},{8,14},{9,15},{10,... | collective-permute-start | bytes 12296 | tf_op jit(solution)/shard_map/ppermute | solution.py:52
  21.4 3.6 %collective-permute-start.7 = (s32[128,8]{0,1:T(8,128)}, s32[128,8]{0,1:T(8,128)S(1)}, u32[]{:S(2)}, u32[]{:S(2)}) collective-permute-start(s32[128,8]{0,1:T(8,128)} %param.12), channel_id=1, source_target_pairs={{0,4},{1,5},{2,6},{3,7},{4,0},{5,1},{6,2},{7,3},{8,12},{9,13},{10,... | collective-permute-start | bytes 12296 | tf_op jit(solution)/shard_map/ppermute | solution.py:52
  35.7 29.1 %copy-start.1 = (f32[128,768]{1,0:T(8,128)S(1)}, f32[128,768]{1,0:T(8,128)}, u32[]{:S(2)}) copy-start(f32[128,768]{1,0:T(8,128)} %get-tuple-element.7) | copy-start | bytes 1179652
  35.7 11.7 %collective-permute-start.10 = (bf16[128,768]{1,0:T(8,128)(2,1)}, bf16[128,768]{1,0:T(8,128)(2,1)S(1)}, u32[]{:S(2)}, u32[]{:S(2)}) collective-permute-start(bf16[128,768]{1,0:T(8,128)(2,1)} %get-tuple-element.10), channel_id=1, source_target_pairs={{0,2},{1,3},{2,0},{3,1},{4,6},{5,7},{6,4},{7,5},{8,10},{9,11},{10,... | collective-permute-start | bytes 589832 | tf_op jit(solution)/shard_map/ppermute | solution.py:52
  44.7 20.4 %copy-start.2 = (f32[768]{0:T(1024)S(1)}, f32[768]{0:T(1024)}, u32[]{:S(2)}) copy-start(f32[768]{0:T(1024)} %param.11) | copy-start | bytes 9220
  44.8 6.7 %collective-permute-start.8 = (bf16[128,768]{1,0:T(8,128)(2,1)}, bf16[128,768]{1,0:T(8,128)(2,1)S(1)}, u32[]{:S(2)}, u32[]{:S(2)}) collective-permute-start(bf16[128,768]{1,0:T(8,128)(2,1)} %get-tuple-element.8), channel_id=1, source_target_pairs={{0,6},{1,7},{2,4},{3,5},{4,2},{5,3},{6,0},{7,1},{8,14},{9,15},{10,... | collective-permute-start | bytes 589832 | tf_op jit(solution)/shard_map/ppermute | solution.py:52
  46.2 18.5 %collective-permute-start.9 = (bf16[128,768]{1,0:T(8,128)(2,1)}, bf16[128,768]{1,0:T(8,128)(2,1)S(1)}, u32[]{:S(2)}, u32[]{:S(2)}) collective-permute-start(bf16[128,768]{1,0:T(8,128)(2,1)} %get-tuple-element.9), channel_id=1, source_target_pairs={{0,4},{1,5},{2,6},{3,7},{4,0},{5,1},{6,2},{7,3},{8,12},{9,13},{10,... | collective-permute-start | bytes 589832 | tf_op jit(solution)/shard_map/ppermute | solution.py:52
  64.7 12.7 %copy-start.3 = (bf16[1280,768]{1,0:T(8,128)(2,1)S(1)}, bf16[1280,768]{1,0:T(8,128)(2,1)}, u32[]{:S(2)}) copy-start(bf16[1280,768]{1,0:T(8,128)(2,1)} %param.15) | copy-start | bytes 5898244
  65.3 2.5 %collective-permute-start.11 = (bf16[128,768]{1,0:T(8,128)(2,1)S(1)}, bf16[128,768]{1,0:T(8,128)(2,1)S(1)}, u32[]{:S(2)}, u32[]{:S(2)}) collective-permute-start(bf16[128,768]{1,0:T(8,128)(2,1)S(1)} %multiply_convert_fusion), channel_id=1, source_target_pairs={{0,1},{1,0},{2,3},{3,2},{4,5},{5,4},{6,7},{7,6},{8,9},{9,8},{10,11... | collective-permute-start | bytes 589832 | tf_op jit(solution)/shard_map/ppermute | solution.py:48
  68.0 5.2 %collective-permute-start.12 = (bf16[64,768]{1,0:T(8,128)(2,1)S(1)}, bf16[64,768]{1,0:T(8,128)(2,1)S(1)}, u32[]{:S(2)}, u32[]{:S(2)}) collective-permute-start(bf16[64,768]{1,0:T(8,128)(2,1)S(1)} %get-tuple-element.19), channel_id=1, source_target_pairs={{0,2},{1,3},{2,0},{3,1},{4,6},{5,7},{6,4},{7,5},{8,10},{9,11},{10,... | collective-permute-start | bytes 294920 | tf_op jit(solution)/shard_map/ppermute | solution.py:52
  68.1 9.2 %collective-permute-start.13 = (bf16[64,768]{1,0:T(8,128)(2,1)S(1)}, bf16[64,768]{1,0:T(8,128)(2,1)S(1)}, u32[]{:S(2)}, u32[]{:S(2)}) collective-permute-start(bf16[64,768]{1,0:T(8,128)(2,1)S(1)} %get-tuple-element.18), channel_id=1, source_target_pairs={{0,4},{1,5},{2,6},{3,7},{4,0},{5,1},{6,2},{7,3},{8,12},{9,13},{10,... | collective-permute-start | bytes 294920 | tf_op jit(solution)/shard_map/ppermute | solution.py:52
  69.8 7.6 %collective-permute-start.14 = (bf16[64,768]{1,0:T(8,128)(2,1)S(1)}, bf16[64,768]{1,0:T(8,128)(2,1)S(1)}, u32[]{:S(2)}, u32[]{:S(2)}) collective-permute-start(bf16[64,768]{1,0:T(8,128)(2,1)S(1)} %get-tuple-element.17), channel_id=1, source_target_pairs={{0,6},{1,7},{2,4},{3,5},{4,2},{5,3},{6,0},{7,1},{8,14},{9,15},{10,... | collective-permute-start | bytes 294920 | tf_op jit(solution)/shard_map/ppermute | solution.py:52
  79.3 11.3 %collective-permute-start.15 = (bf16[64,64]{0,1:T(8,128)(2,1)S(1)}, bf16[64,64]{0,1:T(8,128)(2,1)S(1)}, u32[]{:S(2)}, u32[]{:S(2)}) collective-permute-start(bf16[64,64]{0,1:T(8,128)(2,1)S(1)} %get-tuple-element.23), channel_id=1, source_target_pairs={{0,2},{1,3},{2,0},{3,1},{4,6},{5,7},{6,4},{7,5},{8,10},{9,11},{10,... | collective-permute-start | bytes 24584 | tf_op jit(solution)/shard_map/ppermute | solution.py:52
  81.7 8.9 %collective-permute-start.16 = (bf16[64,64]{0,1:T(8,128)(2,1)S(1)}, bf16[64,64]{0,1:T(8,128)(2,1)S(1)}, u32[]{:S(2)}, u32[]{:S(2)}) collective-permute-start(bf16[64,64]{0,1:T(8,128)(2,1)S(1)} %get-tuple-element.22), channel_id=1, source_target_pairs={{0,4},{1,5},{2,6},{3,7},{4,0},{5,1},{6,2},{7,3},{8,12},{9,13},{10,... | collective-permute-start | bytes 24584 | tf_op jit(solution)/shard_map/ppermute | solution.py:52
  82.0 8.6 %collective-permute-start.17 = (bf16[64,64]{0,1:T(8,128)(2,1)S(1)}, bf16[64,64]{0,1:T(8,128)(2,1)S(1)}, u32[]{:S(2)}, u32[]{:S(2)}) collective-permute-start(bf16[64,64]{0,1:T(8,128)(2,1)S(1)} %get-tuple-element.21), channel_id=1, source_target_pairs={{0,6},{1,7},{2,4},{3,5},{4,2},{5,3},{6,0},{7,1},{8,14},{9,15},{10,... | collective-permute-start | bytes 24584 | tf_op jit(solution)/shard_map/ppermute | solution.py:52
  85.1 14.8 %all-to-all-start.1 = ((f32[32,2,768]{2,1,0:T(2,128)}), f32[32,2,768]{2,1,0:T(2,128)S(1)}, u32[]{:S(2)}, u32[]{:S(2)}) async-start(f32[32,2,768]{2,1,0:T(2,128)} %reshape.126), calls=%async_computation.1 | async-start | bytes 393216 | tf_op jit(solution)/shard_map/all_to_all | solution.py:16
  90.9 2.3 %collective-permute-start.18 = (bf16[128,64]{0,1:T(8,128)(2,1)S(1)}, bf16[128,64]{0,1:T(8,128)(2,1)S(1)}, u32[]{:S(2)}, u32[]{:S(2)}) collective-permute-start(bf16[128,64]{0,1:T(8,128)(2,1)S(1)} %slice.148), channel_id=1, source_target_pairs={{0,1},{1,0},{2,3},{3,2},{4,5},{5,4},{6,7},{7,6},{8,9},{9,8},{10,11... | collective-permute-start | bytes 49160 | tf_op jit(solution)/shard_map/ppermute | solution.py:48

commit v4 on v3

--- a/solution.py
+++ b/solution.py
@@ -253,40 +253,6 @@
     asked = {k: to_chip(label_tokens, k) for k in others}
     asked[0] = label_tokens
 
-    label_dest = label_places(ref_owner[:, 0] ^ me, shards, label_cap)
-    mine = jnp.stack([label_dest, ref_row])
-    theirs = swap_cores(mine)
-    own_rel = label_dest // label_cap
-    other_rel = theirs[0] // label_cap
-    places = jnp.concatenate(
-        [
-            jnp.where(own_rel % 2 == 0, label_dest, -1),
-            jnp.where(other_rel % 2 == 1, theirs[0], -1),
-        ]
-    )
-    slots = shards * label_cap
-    to_slots = jnp.arange(slots, dtype=I32)[:, None] == places[None, :]
-    chip_rows = jnp.concatenate([ref_row, theirs[1]])
-    send_rows = jnp.sum(jnp.where(to_slots, chip_rows[None, :] + 1, 0), axis=1) - 1
-    send_rows = send_rows.reshape(chips, 2 * label_cap)
-    to_slots = to_slots.astype(BF16)
-    got_rows = jnp.concatenate(
-        [send_rows[0:1]] + [to_chip(send_rows[k : k + 1], k) for k in range(1, chips)]
-    ).reshape(slots)
-
-    digits = jnp.concatenate(
-        [positives & 255, (positives >> 8) & 255, positives >> 16], axis=1
-    ).astype(BF16)
-    own_block = jnp.concatenate(
-        [docs, digits, jnp.zeros((own_docs, 128 - 3 * pos_count), BF16)], axis=1
-    )
-    all_blocks = exchange(
-        jnp.broadcast_to(own_block[None], (devices, own_docs, width + 128)), ALL
-    ).reshape(all_count, width + 128)
-    all_docs = all_blocks[:, :width]
-    d = all_blocks[:, width : width + 3 * pos_count].astype(I32)
-    all_positives = d[:, :pos_count] + 256 * d[:, pos_count : 2 * pos_count] + 65536 * d[:, 2 * pos_count :]
-
     def starts(ks):
         ids = jnp.concatenate([asked[k] for k in ks])
         near = ids - me * vocab_rows
@@ -299,14 +265,50 @@
         first = (row // SUBLANES) * (SUBLANES * (width // LANES)) + row % SUBLANES
         return first.reshape(len(ks) * tokens)
 
-    sent = []
-    half = len(others) - len(others) // 3
-    for ks in (others[:half], others[half:] + [0]):
-        sent += partial_means(
-            starts(ks), token_table, other_table, labels, length, [BF16 if k else F32 for k in ks]
-        )
+    ks = others + [0]
+    sent = partial_means(
+        starts(ks), token_table, other_table, labels, length, [BF16 if k else F32 for k in ks]
+    )
     arrived = [to_chip(term, k) for term, k in zip(sent, others)]
-    pooled = sent[-1]
+    docs, positives, ref_owner, ref_row, own = lax.optimization_barrier(
+        (docs, positives, ref_owner, ref_row, sent[-1])
+    )
+
+    label_dest = label_places(ref_owner[:, 0] ^ me, shards, label_cap)
+    mine = jnp.stack([label_dest, ref_row])
+    theirs = swap_cores(mine)
+    own_rel = label_dest // label_cap
+    other_rel = theirs[0] // label_cap
+    places = jnp.concatenate(
+        [
+            jnp.where(own_rel % 2 == 0, label_dest, -1),
+            jnp.where(other_rel % 2 == 1, theirs[0], -1),
+        ]
+    )
+    slots = shards * label_cap
+    to_slots = jnp.arange(slots, dtype=I32)[:, None] == places[None, :]
+    chip_rows = jnp.concatenate([ref_row, theirs[1]])
+    send_rows = jnp.sum(jnp.where(to_slots, chip_rows[None, :] + 1, 0), axis=1) - 1
+    send_rows = send_rows.reshape(chips, 2 * label_cap)
+    to_slots = to_slots.astype(BF16)
+    got_rows = jnp.concatenate(
+        [send_rows[0:1]] + [to_chip(send_rows[k : k + 1], k) for k in range(1, chips)]
+    ).reshape(slots)
+
+    digits = jnp.concatenate(
+        [positives & 255, (positives >> 8) & 255, positives >> 16], axis=1
+    ).astype(BF16)
+    own_block = jnp.concatenate(
+        [docs, digits, jnp.zeros((own_docs, 128 - 3 * pos_count), BF16)], axis=1
+    )
+    all_blocks = exchange(
+        jnp.broadcast_to(own_block[None], (devices, own_docs, width + 128)), ALL
+    ).reshape(all_count, width + 128)
+    all_docs = all_blocks[:, :width]
+    d = all_blocks[:, width : width + 3 * pos_count].astype(I32)
+    all_positives = d[:, :pos_count] + 256 * d[:, pos_count : 2 * pos_count] + 65536 * d[:, 2 * pos_count :]
+
+    pooled = own
     for term in arrived:
         pooled = pooled + term.astype(F32)
     pooled = pooled.astype(BF16)
@@ -330,9 +332,11 @@
         hits = hits | (all_positives[:, column : column + 1] == label_columns[None, :])
     errors = (jax.nn.sigmoid(logits) - hits.astype(F32)).astype(BF16)
     doc_terms = jnp.dot(errors, head, preferred_element_type=F32)
-    doc_grad = jnp.sum(exchange(doc_terms.reshape(devices, own_docs, width), ALL), axis=0)
+    doc_terms = doc_terms.reshape(devices, own_docs, width)
+    doc_terms, late_errors = lax.optimization_barrier((doc_terms, errors))
+    doc_grad = jnp.sum(exchange(doc_terms, ALL), axis=0)
     picked = lax.dot_general(
-        to_rows, errors, (((0,), (1,)), ((), ())), preferred_element_type=F32
+        to_rows, late_errors, (((0,), (1,)), ((), ())), preferred_element_type=F32
     ).astype(BF16)
     picked = picked.reshape(chips, 2 * label_cap, all_count)
     arrived = {k: to_chip(picked[k], k) for k in others}

time: 101 us -> 86.6 us (0.86)
  Pallas kernels: 17.9 us -> 11.9 us
  waiting for transfers between devices: 31.9 us -> 26.6 us
  other arithmetic: 6.31 us -> 1.73 us
  starting transfers between devices: 32.8 us -> 34.4 us
  local copies, waits for them, and re-layouts: 4.5 us -> 3.43 us
  matrix products: 6.24 us -> 7.26 us
    ppermute x15, waiting for transfers between devices: 25.1 us -> 15.3 us  [to_chip(): lax.ppermute(x, 'shard', [(i, i ^ 2 * k) for i in range(lax.axis_size('sh...]
    pallas_call x2 -> x1, Pallas kernels: 17.9 us -> 11.9 us  [partial_means(): pl.pallas_call(functools.partial(sum_kernel, length), out_shape=[jax.Shap...]
    all_to_all x2, waiting for transfers between devices: 5.83 us -> 11.2 us  [exchange(): return lax.all_to_all(blocks, axes, split_axis=0, concat_axis=0, tiled=True)]
    ppermute x15, starting transfers between devices: 20.4 us -> 21.8 us  [to_chip(): lax.ppermute(x, 'shard', [(i, i ^ 2 * k) for i in range(lax.axis_size('sh...]
  transfers between devices with their start and end apart: 21 -> 21, of which waited for: 8 -> 7; matrix products, arithmetic and copies ran while one was open for 14% -> 9% of each run, Pallas kernels for 9% -> 0%
where the time goes in v4:
time: 86.6 us; the launch traced here: 86.2 us
  starting transfers between devices  34.4 us (40%)
  waiting for transfers between devices  26.6 us (31%)
  Pallas kernels  11.9 us (14%)
  matrix products  7.26 us (8%)
  local copies, waits for them, and re-layouts  3.43 us (4%)
  other arithmetic  1.73 us (2%)
  between operations  0.94 us (1%)
    ppermute x15, starting transfers between devices, to_chip(): lax.ppermute(x, 'shard', [(i, i ^ 2 * k) for i in range(lax.axis_size('sh...  21.8 us
    ppermute x15, waiting for transfers between devices, to_chip(): lax.ppermute(x, 'shard', [(i, i ^ 2 * k) for i in range(lax.axis_size('sh...  15.3 us
    pallas_call x1, Pallas kernels, partial_means(): pl.pallas_call(functools.partial(sum_kernel, length), out_shape=[jax.Shap...  11.9 us
    all_to_all x2, waiting for transfers between devices, exchange(): return lax.all_to_all(blocks, axes, split_axis=0, concat_axis=0, tiled=True)  11.2 us
    all_to_all x2, starting transfers between devices, exchange(): return lax.all_to_all(blocks, axes, split_axis=0, concat_axis=0, tiled=True)  9.55 us
    ppermute x4, starting transfers between devices, swap_cores(): lax.ppermute(x, 'shard', [(i, i ^ 1) for i in range(lax.axis_size('shard'...  3.02 us
    dot_general x1, matrix products, by_sums(): lax.dot_general(errors, all_docs, (((0,), (0,)), ((), ())), preferred_ele...  1.99 us
  transfers between devices with their start and end apart: 21, of which 7 were waited for; matrix products, arithmetic and copies ran while one was open for 9% of the time, Pallas kernels for 0%

profile of v4, /device:TPU:1, one launch (start us, length us, event | category | flops | bytes accessed | tf_op | source)
XLA Modules:
  0.0 86.2 jit_solution(1843323374139323343)
XLA Ops:
  0.6 0.1 collective-permute-start.3
  0.8 4.8 %collective-permute-start = (s32[128,8]{0,1:T(8,128)}, s32[128,8]{0,1:T(8,128)S(1)}, u32[]{:S(2)}, u32[]{:S(2)}) collective-permute-start(s32[128,8]{0,1:T(8,128)} %param.12), channel_id=1, source_target_pairs={{0,6},{1,7},{2,4},{3,5},{4,2},{5,3},{6,0},{7,1},{8,14},{9,15},{10,... | collective-permute-start | bytes 12296 | tf_op jit(solution)/shard_map/ppermute | solution.py:52
  5.6 0.3 collective-permute-start.2
  5.8 0.9 %collective-permute-done = s32[128,8]{0,1:T(8,128)S(1)} collective-permute-done((s32[128,8]{0,1:T(8,128)}, s32[128,8]{0,1:T(8,128)S(1)}, u32[]{:S(2)}, u32[]{:S(2)}) %collective-permute-start) | collective-permute-done | bytes 4128 | tf_op jit(solution)/shard_map/ppermute | solution.py:52
  6.7 2.4 %collective-permute-done.1 = s32[128,8]{0,1:T(8,128)S(1)} collective-permute-done((s32[128,8]{0,1:T(8,128)}, s32[128,8]{0,1:T(8,128)S(1)}, u32[]{:S(2)}, u32[]{:S(2)}) %collective-permute-start.1) | collective-permute-done | bytes 4128 | tf_op jit(solution)/shard_map/ppermute | solution.py:52
  9.1 0.7 constant_dynamic-update-slice_fusion
  9.8 0.1 copy.18
  10.0 0.2 select_n.56
  10.1 0.1 copy.17
  10.2 0.2 sub.47
  10.4 0.6 fusion.39.starts_ref
  11.0 11.9 %shard_map.112 = (bf16[128,768]{1,0:T(8,128)(2,1)}, bf16[128,768]{1,0:T(8,128)(2,1)}, bf16[128,768]{1,0:T(8,128)(2,1)}, f32[128,768]{1,0:T(8,128)}) custom-call(s32[4096]{0:T(1024)} %fusion.39.starts_ref, bf16[3840,768]{1,0:T(8,128)(2,1)} %near_ref.1, bf16[3840,768]{1,0:T(8,128)(2,1)} %collective-permute-done.3.far_ref), custom_call_target="tpu_custom_call" | custom-call | flops 3145728 | bytes 11796480 | tf_op jit(solution)/shard_map/pallas_call | solution.py:210
  23.0 0.2 fusion.10
  23.1 1.6 %collective-permute-start.4 = (s32[2,128]{1,0:T(2,128)S(1)}, s32[2,128]{1,0:T(2,128)S(1)}, u32[]{:S(2)}, u32[]{:S(2)}) collective-permute-start(s32[2,128]{1,0:T(2,128)S(1)} %pad_add_fusion.1), channel_id=1, source_target_pairs={{0,1},{1,0},{2,3},{3,2},{4,5},{5,4},{6,7},{7,6},{8,9},{9,8},{10,11... | collective-permute-start | bytes 3080 | tf_op jit(solution)/shard_map/ppermute | solution.py:48
  24.7 0.8 collective-permute-start.10
  25.6 2.2 %collective-permute-start.8 = (bf16[128,768]{1,0:T(8,128)(2,1)}, bf16[128,768]{1,0:T(8,128)(2,1)S(1)}, u32[]{:S(2)}, u32[]{:S(2)}) collective-permute-start(bf16[128,768]{1,0:T(8,128)(2,1)} %get-tuple-element.20), channel_id=1, source_target_pairs={{0,6},{1,7},{2,4},{3,5},{4,2},{5,3},{6,0},{7,1},{8,14},{9,15},{10,... | collective-permute-start | bytes 589832 | tf_op jit(solution)/shard_map/ppermute | solution.py:52
  27.8 0.1 collective-permute-start.9
  28.1 1.2 %collective-permute-start.5 = (s32[1,64]{1,0:T(1,128)S(1)}, s32[1,64]{1,0:T(1,128)S(1)}, u32[]{:S(2)}, u32[]{:S(2)}) collective-permute-start(s32[1,64]{1,0:T(1,128)S(1)} %get-tuple-element.46), channel_id=1, source_target_pairs={{0,2},{1,3},{2,0},{3,1},{4,6},{5,7},{6,4},{7,5},{8,10},{9,11},{10,... | collective-permute-start | bytes 776 | tf_op jit(solution)/shard_map/ppermute | solution.py:52
  29.4 1.4 %collective-permute-start.6 = (s32[1,64]{1,0:T(1,128)S(1)}, s32[1,64]{1,0:T(1,128)S(1)}, u32[]{:S(2)}, u32[]{:S(2)}) collective-permute-start(s32[1,64]{1,0:T(1,128)S(1)} %get-tuple-element.45), channel_id=1, source_target_pairs={{0,4},{1,5},{2,6},{3,7},{4,0},{5,1},{6,2},{7,3},{8,12},{9,13},{10,... | collective-permute-start | bytes 776 | tf_op jit(solution)/shard_map/ppermute | solution.py:52
  30.8 7.7 %collective-permute-done.5 = s32[1,64]{1,0:T(1,128)S(1)} collective-permute-done((s32[1,64]{1,0:T(1,128)S(1)}, s32[1,64]{1,0:T(1,128)S(1)}, u32[]{:S(2)}, u32[]{:S(2)}) %collective-permute-start.5) | collective-permute-done | bytes 288 | tf_op jit(solution)/shard_map/ppermute | solution.py:52
  38.5 2.2 %collective-permute-start.7 = (s32[1,64]{1,0:T(1,128)S(1)}, s32[1,64]{1,0:T(1,128)S(1)}, u32[]{:S(2)}, u32[]{:S(2)}) collective-permute-start(s32[1,64]{1,0:T(1,128)S(1)} %get-tuple-element.44), channel_id=1, source_target_pairs={{0,6},{1,7},{2,4},{3,5},{4,2},{5,3},{6,0},{7,1},{8,14},{9,15},{10,... | collective-permute-start | bytes 776 | tf_op jit(solution)/shard_map/ppermute | solution.py:52
  40.8 0.7 broadcast_in_dim.25
  41.5 4.7 %all-to-all-start = ((bf16[32,2,896]{2,1,0:T(2,128)(2,1)}), bf16[32,2,896]{2,1,0:T(2,128)(2,1)S(1)}, u32[]{:S(2)}, u32[]{:S(2)}) async-start(bf16[32,2,896]{2,1,0:T(2,128)(2,1)} %broadcast_in_dim.25), calls=%async_computation | async-start | bytes 229376 | tf_op jit(solution)/shard_map/all_to_all | solution.py:16
  46.4 1.4 %multiply_reduce_fusion = (f32[128]{0:T(128)S(1)}, f32[128,768]{1,0:T(8,128)S(1)}) fusion(bf16[768,768]{1,0:T(8,128)(2,1)S(1)} %copy-done, bf16[128,768]{1,0:T(8,128)(2,1)S(1)} %collective-permute-done.10, bf16[128,768]{1,0:T(8,128)(2,1)S(1)} %collective-permute-done.9, f32[128,768]{1,0:T(8,128)} %get-tuple-element.19, ...), kind=kOutput, calls=%fused_computation.32 | convolution fusion | flops 151879552 | bytes 2556416 | tf_op jit(solution)/shard_map/dot_general | solution.py:315
  47.9 0.5 collective-permute-start.11
  48.4 5.8 %all-to-all-done = bf16[32,2,896]{2,1,0:T(2,128)(2,1)S(1)} async-done(((bf16[32,2,896]{2,1,0:T(2,128)(2,1)}), bf16[32,2,896]{2,1,0:T(2,128)(2,1)S(1)}, u32[]{:S(2)}, u32[]{:S(2)}) %all-to-all-start) | async-done | bytes 114720 | tf_op jit(solution)/shard_map/all_to_all | solution.py:16
  54.4 0.3 convolution_convert_fusion.1
  54.7 0.2 collective-permute-start.12
  54.9 0.9 %collective-permute-start.13 = (bf16[64,768]{1,0:T(8,128)(2,1)S(1)}, bf16[64,768]{1,0:T(8,128)(2,1)S(1)}, u32[]{:S(2)}, u32[]{:S(2)}) collective-permute-start(bf16[64,768]{1,0:T(8,128)(2,1)S(1)} %get-tuple-element.32), channel_id=1, source_target_pairs={{0,4},{1,5},{2,6},{3,7},{4,0},{5,1},{6,2},{7,3},{8,12},{9,13},{10,... | collective-permute-start | bytes 294920 | tf_op jit(solution)/shard_map/ppermute | solution.py:52
  55.7 2.6 %collective-permute-start.14 = (bf16[64,768]{1,0:T(8,128)(2,1)S(1)}, bf16[64,768]{1,0:T(8,128)(2,1)S(1)}, u32[]{:S(2)}, u32[]{:S(2)}) collective-permute-start(bf16[64,768]{1,0:T(8,128)(2,1)S(1)} %get-tuple-element.31), channel_id=1, source_target_pairs={{0,6},{1,7},{2,4},{3,5},{4,2},{5,3},{6,0},{7,1},{8,14},{9,15},{10,... | collective-permute-start | bytes 294920 | tf_op jit(solution)/shard_map/ppermute | solution.py:52
  58.3 0.2 slice_reduce_fusion.4
  58.5 1.4 %collective-permute-done.12 = bf16[64,768]{1,0:T(8,128)(2,1)S(1)} collective-permute-done((bf16[64,768]{1,0:T(8,128)(2,1)S(1)}, bf16[64,768]{1,0:T(8,128)(2,1)S(1)}, u32[]{:S(2)}, u32[]{:S(2)}) %collective-permute-start.12) | collective-permute-done | bytes 98336 | tf_op jit(solution)/shard_map/ppermute | solution.py:52
  60.0 2.9 %collective-permute-done.14 = bf16[64,768]{1,0:T(8,128)(2,1)S(1)} collective-permute-done((bf16[64,768]{1,0:T(8,128)(2,1)S(1)}, bf16[64,768]{1,0:T(8,128)(2,1)S(1)}, u32[]{:S(2)}, u32[]{:S(2)}) %collective-permute-start.14) | collective-permute-done | bytes 98336 | tf_op jit(solution)/shard_map/ppermute | solution.py:52
  62.8 0.7 fusion
  63.6 0.8 fusion.5
  64.4 0.5 fusion.53
  64.8 0.8 reshape.111
  65.6 0.3 fusion.7
  66.1 3.0 %collective-permute-start.15 = (bf16[64,64]{0,1:T(8,128)(2,1)S(1)}, bf16[64,64]{0,1:T(8,128)(2,1)S(1)}, u32[]{:S(2)}, u32[]{:S(2)}) collective-permute-start(bf16[64,64]{0,1:T(8,128)(2,1)S(1)} %get-tuple-element.37), channel_id=1, source_target_pairs={{0,2},{1,3},{2,0},{3,1},{4,6},{5,7},{6,4},{7,5},{8,10},{9,11},{10,... | collective-permute-start | bytes 24584 | tf_op jit(solution)/shard_map/ppermute | solution.py:52
  69.1 0.4 collective-permute-start.16
  69.5 1.8 %collective-permute-start.17 = (bf16[64,64]{0,1:T(8,128)(2,1)S(1)}, bf16[64,64]{0,1:T(8,128)(2,1)S(1)}, u32[]{:S(2)}, u32[]{:S(2)}) collective-permute-start(bf16[64,64]{0,1:T(8,128)(2,1)S(1)} %get-tuple-element.35), channel_id=1, source_target_pairs={{0,6},{1,7},{2,4},{3,5},{4,2},{5,3},{6,0},{7,1},{8,14},{9,15},{10,... | collective-permute-start | bytes 24584 | tf_op jit(solution)/shard_map/ppermute | solution.py:52
  71.2 4.9 %all-to-all-start.1 = ((f32[32,2,768]{2,1,0:T(2,128)}), f32[32,2,768]{2,1,0:T(2,128)S(1)}, u32[]{:S(2)}, u32[]{:S(2)}) async-start(f32[32,2,768]{2,1,0:T(2,128)} %reshape.111), calls=%async_computation.1 | async-start | bytes 393216 | tf_op jit(solution)/shard_map/all_to_all | solution.py:16
  76.1 0.2 convolution_convert_fusion.3
  76.3 0.8 collective-permute-start.18
  77.2 2.0 %convolution_convert_fusion = bf16[1280,768]{1,0:T(8,128)(2,1)} fusion(bf16[64,1280]{1,0:T(8,128)(2,1)S(1)} %fusion.5, bf16[64,896]{1,0:T(8,128)(2,1)S(1)} %reshape.110), kind=kOutput, calls=%fused_computation.1 | convolution fusion | flops 126812160 | bytes 2228224 | tf_op jit(solution)/shard_map/dot_general | solution.py:348
  79.1 0.9 %convolution_convert_fusion.2 = bf16[128,768]{1,0:T(8,128)(2,1)} fusion(bf16[64,896]{1,0:T(8,128)(2,1)S(1)} %reshape.110, bf16[128,64]{0,1:T(8,128)(2,1)S(1)} %collective-permute-done.18, bf16[256,64]{0,1:T(8,128)(2,1)S(1)} %convolution_convert_fusion.3), kind=kOutput, calls=%fused_computation.12 | convolution fusion | flops 12689408 | bytes 327680 | tf_op jit(solution)/shard_map/dot_general | solution.py:351
  80.1 5.5 %all-to-all-done.1 = f32[32,2,768]{2,1,0:T(2,128)S(1)} async-done(((f32[32,2,768]{2,1,0:T(2,128)}), f32[32,2,768]{2,1,0:T(2,128)S(1)}, u32[]{:S(2)}, u32[]{:S(2)}) %all-to-all-start.1) | async-done | bytes 196640 | tf_op jit(solution)/shard_map/all_to_all | solution.py:16
  85.5 0.7 reduce_sum.42
  (58 shorter events, 1.0 us)
Async XLA Ops:
  0.6 45.7 %copy-start = (bf16[768,768]{1,0:T(8,128)(2,1)S(1)}, bf16[768,768]{1,0:T(8,128)(2,1)}, u32[]{:S(2)}) copy-start(bf16[768,768]{1,0:T(8,128)(2,1)} %param.10) | copy-start | bytes 3538948
  0.6 10.4 %collective-permute-start.3 = (bf16[3840,768]{1,0:T(8,128)(2,1)}, bf16[3840,768]{1,0:T(8,128)(2,1)}, u32[]{:S(2)}, u32[]{:S(2)}) collective-permute-start(bf16[3840,768]{1,0:T(8,128)(2,1)} %near_ref.1), channel_id=1, source_target_pairs={{0,1},{1,0},{2,3},{3,2},{4,5},{5,4},{6,7},{7,6},{8,9},{9,8},{10,11... | collective-permute-start | bytes 17694728 | tf_op jit(solution)/shard_map/ppermute | solution.py:48
  0.8 6.0 %collective-permute-start = (s32[128,8]{0,1:T(8,128)}, s32[128,8]{0,1:T(8,128)S(1)}, u32[]{:S(2)}, u32[]{:S(2)}) collective-permute-start(s32[128,8]{0,1:T(8,128)} %param.12), channel_id=1, source_target_pairs={{0,6},{1,7},{2,4},{3,5},{4,2},{5,3},{6,0},{7,1},{8,14},{9,15},{10,... | collective-permute-start | bytes 12296 | tf_op jit(solution)/shard_map/ppermute | solution.py:52
  5.6 3.6 %collective-permute-start.1 = (s32[128,8]{0,1:T(8,128)}, s32[128,8]{0,1:T(8,128)S(1)}, u32[]{:S(2)}, u32[]{:S(2)}) collective-permute-start(s32[128,8]{0,1:T(8,128)} %param.12), channel_id=1, source_target_pairs={{0,4},{1,5},{2,6},{3,7},{4,0},{5,1},{6,2},{7,3},{8,12},{9,13},{10,... | collective-permute-start | bytes 12296 | tf_op jit(solution)/shard_map/ppermute | solution.py:52
  5.6 3.6 %collective-permute-start.2 = (s32[128,8]{0,1:T(8,128)}, s32[128,8]{0,1:T(8,128)S(1)}, u32[]{:S(2)}, u32[]{:S(2)}) collective-permute-start(s32[128,8]{0,1:T(8,128)} %param.12), channel_id=1, source_target_pairs={{0,2},{1,3},{2,0},{3,1},{4,6},{5,7},{6,4},{7,5},{8,10},{9,11},{10,... | collective-permute-start | bytes 12296 | tf_op jit(solution)/shard_map/ppermute | solution.py:52
  11.0 11.9 %copy-start.3 = (s32[128,1]{0,1:T(1,128)S(1)}, s32[128,1]{0,1:T(1,128)}, u32[]{:S(2)}) copy-start(s32[128,1]{0,1:T(1,128)} %param.13) | copy-start | bytes 1540
  11.0 12.1 %copy-start.4 = (s32[128]{0:T(128)S(1)}, s32[128]{0:T(128)}, u32[]{:S(2)}) copy-start(s32[128]{0:T(128)} %param.14) | copy-start | bytes 1540
  11.0 18.4 %copy-start.5 = (s32[2,5]{1,0:T(2,128)S(1)}, s32[2,5]{1,0:T(2,128)}, u32[]{:S(2)}) copy-start(s32[2,5]{1,0:T(2,128)} %param.17) | copy-start | bytes 124
  11.0 29.7 %copy-start.2 = (bf16[2,768]{1,0:T(2,128)(2,1)S(1)}, bf16[2,768]{1,0:T(2,128)(2,1)}, u32[]{:S(2)}) copy-start(bf16[2,768]{1,0:T(2,128)(2,1)} %param.16) | copy-start | bytes 9220
  22.9 24.9 %copy-start.1 = (f32[768]{0:T(1024)S(1)}, f32[768]{0:T(1024)}, u32[]{:S(2)}) copy-start(f32[768]{0:T(1024)} %param.11) | copy-start | bytes 9220
  23.1 4.7 %collective-permute-start.4 = (s32[2,128]{1,0:T(2,128)S(1)}, s32[2,128]{1,0:T(2,128)S(1)}, u32[]{:S(2)}, u32[]{:S(2)}) collective-permute-start(s32[2,128]{1,0:T(2,128)S(1)} %pad_add_fusion.1), channel_id=1, source_target_pairs={{0,1},{1,0},{2,3},{3,2},{4,5},{5,4},{6,7},{7,6},{8,9},{9,8},{10,11... | collective-permute-start | bytes 3080 | tf_op jit(solution)/shard_map/ppermute | solution.py:48
  24.7 21.6 %collective-permute-start.10 = (bf16[128,768]{1,0:T(8,128)(2,1)}, bf16[128,768]{1,0:T(8,128)(2,1)S(1)}, u32[]{:S(2)}, u32[]{:S(2)}) collective-permute-start(bf16[128,768]{1,0:T(8,128)(2,1)} %get-tuple-element.22), channel_id=1, source_target_pairs={{0,2},{1,3},{2,0},{3,1},{4,6},{5,7},{6,4},{7,5},{8,10},{9,11},{10,... | collective-permute-start | bytes 589832 | tf_op jit(solution)/shard_map/ppermute | solution.py:52
  25.6 20.8 %collective-permute-start.8 = (bf16[128,768]{1,0:T(8,128)(2,1)}, bf16[128,768]{1,0:T(8,128)(2,1)S(1)}, u32[]{:S(2)}, u32[]{:S(2)}) collective-permute-start(bf16[128,768]{1,0:T(8,128)(2,1)} %get-tuple-element.20), channel_id=1, source_target_pairs={{0,6},{1,7},{2,4},{3,5},{4,2},{5,3},{6,0},{7,1},{8,14},{9,15},{10,... | collective-permute-start | bytes 589832 | tf_op jit(solution)/shard_map/ppermute | solution.py:52
  27.8 18.6 %collective-permute-start.9 = (bf16[128,768]{1,0:T(8,128)(2,1)}, bf16[128,768]{1,0:T(8,128)(2,1)S(1)}, u32[]{:S(2)}, u32[]{:S(2)}) collective-permute-start(bf16[128,768]{1,0:T(8,128)(2,1)} %get-tuple-element.21), channel_id=1, source_target_pairs={{0,4},{1,5},{2,6},{3,7},{4,0},{5,1},{6,2},{7,3},{8,12},{9,13},{10,... | collective-permute-start | bytes 589832 | tf_op jit(solution)/shard_map/ppermute | solution.py:52
  28.1 10.4 %collective-permute-start.5 = (s32[1,64]{1,0:T(1,128)S(1)}, s32[1,64]{1,0:T(1,128)S(1)}, u32[]{:S(2)}, u32[]{:S(2)}) collective-permute-start(s32[1,64]{1,0:T(1,128)S(1)} %get-tuple-element.46), channel_id=1, source_target_pairs={{0,2},{1,3},{2,0},{3,1},{4,6},{5,7},{6,4},{7,5},{8,10},{9,11},{10,... | collective-permute-start | bytes 776 | tf_op jit(solution)/shard_map/ppermute | solution.py:52
  29.4 16.8 %collective-permute-start.6 = (s32[1,64]{1,0:T(1,128)S(1)}, s32[1,64]{1,0:T(1,128)S(1)}, u32[]{:S(2)}, u32[]{:S(2)}) collective-permute-start(s32[1,64]{1,0:T(1,128)S(1)} %get-tuple-element.45), channel_id=1, source_target_pairs={{0,4},{1,5},{2,6},{3,7},{4,0},{5,1},{6,2},{7,3},{8,12},{9,13},{10,... | collective-permute-start | bytes 776 | tf_op jit(solution)/shard_map/ppermute | solution.py:52
  38.5 7.7 %collective-permute-start.7 = (s32[1,64]{1,0:T(1,128)S(1)}, s32[1,64]{1,0:T(1,128)S(1)}, u32[]{:S(2)}, u32[]{:S(2)}) collective-permute-start(s32[1,64]{1,0:T(1,128)S(1)} %get-tuple-element.44), channel_id=1, source_target_pairs={{0,6},{1,7},{2,4},{3,5},{4,2},{5,3},{6,0},{7,1},{8,14},{9,15},{10,... | collective-permute-start | bytes 776 | tf_op jit(solution)/shard_map/ppermute | solution.py:52
  41.5 12.7 %all-to-all-start = ((bf16[32,2,896]{2,1,0:T(2,128)(2,1)}), bf16[32,2,896]{2,1,0:T(2,128)(2,1)S(1)}, u32[]{:S(2)}, u32[]{:S(2)}) async-start(bf16[32,2,896]{2,1,0:T(2,128)(2,1)} %broadcast_in_dim.25), calls=%async_computation | async-start | bytes 229376 | tf_op jit(solution)/shard_map/all_to_all | solution.py:16
  47.9 6.4 %collective-permute-start.11 = (bf16[128,768]{1,0:T(8,128)(2,1)S(1)}, bf16[128,768]{1,0:T(8,128)(2,1)S(1)}, u32[]{:S(2)}, u32[]{:S(2)}) collective-permute-start(bf16[128,768]{1,0:T(8,128)(2,1)S(1)} %multiply_convert_fusion), channel_id=1, source_target_pairs={{0,1},{1,0},{2,3},{3,2},{4,5},{5,4},{6,7},{7,6},{8,9},{9,8},{10,11... | collective-permute-start | bytes 589832 | tf_op jit(solution)/shard_map/ppermute | solution.py:48
  54.2 8.6 %copy-start.6 = (bf16[1280,768]{1,0:T(8,128)(2,1)S(1)}, bf16[1280,768]{1,0:T(8,128)(2,1)}, u32[]{:S(2)}) copy-start(bf16[1280,768]{1,0:T(8,128)(2,1)} %param.15) | copy-start | bytes 5898244
  54.7 5.3 %collective-permute-start.12 = (bf16[64,768]{1,0:T(8,128)(2,1)S(1)}, bf16[64,768]{1,0:T(8,128)(2,1)S(1)}, u32[]{:S(2)}, u32[]{:S(2)}) collective-permute-start(bf16[64,768]{1,0:T(8,128)(2,1)S(1)} %get-tuple-element.33), channel_id=1, source_target_pairs={{0,2},{1,3},{2,0},{3,1},{4,6},{5,7},{6,4},{7,5},{8,10},{9,11},{10,... | collective-permute-start | bytes 294920 | tf_op jit(solution)/shard_map/ppermute | solution.py:52
  54.9 5.1 %collective-permute-start.13 = (bf16[64,768]{1,0:T(8,128)(2,1)S(1)}, bf16[64,768]{1,0:T(8,128)(2,1)S(1)}, u32[]{:S(2)}, u32[]{:S(2)}) collective-permute-start(bf16[64,768]{1,0:T(8,128)(2,1)S(1)} %get-tuple-element.32), channel_id=1, source_target_pairs={{0,4},{1,5},{2,6},{3,7},{4,0},{5,1},{6,2},{7,3},{8,12},{9,13},{10,... | collective-permute-start | bytes 294920 | tf_op jit(solution)/shard_map/ppermute | solution.py:52
  55.7 7.1 %collective-permute-start.14 = (bf16[64,768]{1,0:T(8,128)(2,1)S(1)}, bf16[64,768]{1,0:T(8,128)(2,1)S(1)}, u32[]{:S(2)}, u32[]{:S(2)}) collective-permute-start(bf16[64,768]{1,0:T(8,128)(2,1)S(1)} %get-tuple-element.31), channel_id=1, source_target_pairs={{0,6},{1,7},{2,4},{3,5},{4,2},{5,3},{6,0},{7,1},{8,14},{9,15},{10,... | collective-permute-start | bytes 294920 | tf_op jit(solution)/shard_map/ppermute | solution.py:52
  66.1 10.0 %collective-permute-start.15 = (bf16[64,64]{0,1:T(8,128)(2,1)S(1)}, bf16[64,64]{0,1:T(8,128)(2,1)S(1)}, u32[]{:S(2)}, u32[]{:S(2)}) collective-permute-start(bf16[64,64]{0,1:T(8,128)(2,1)S(1)} %get-tuple-element.37), channel_id=1, source_target_pairs={{0,2},{1,3},{2,0},{3,1},{4,6},{5,7},{6,4},{7,5},{8,10},{9,11},{10,... | collective-permute-start | bytes 24584 | tf_op jit(solution)/shard_map/ppermute | solution.py:52
  69.1 7.0 %collective-permute-start.16 = (bf16[64,64]{0,1:T(8,128)(2,1)S(1)}, bf16[64,64]{0,1:T(8,128)(2,1)S(1)}, u32[]{:S(2)}, u32[]{:S(2)}) collective-permute-start(bf16[64,64]{0,1:T(8,128)(2,1)S(1)} %get-tuple-element.36), channel_id=1, source_target_pairs={{0,4},{1,5},{2,6},{3,7},{4,0},{5,1},{6,2},{7,3},{8,12},{9,13},{10,... | collective-permute-start | bytes 24584 | tf_op jit(solution)/shard_map/ppermute | solution.py:52
  69.5 6.6 %collective-permute-start.17 = (bf16[64,64]{0,1:T(8,128)(2,1)S(1)}, bf16[64,64]{0,1:T(8,128)(2,1)S(1)}, u32[]{:S(2)}, u32[]{:S(2)}) collective-permute-start(bf16[64,64]{0,1:T(8,128)(2,1)S(1)} %get-tuple-element.35), channel_id=1, source_target_pairs={{0,6},{1,7},{2,4},{3,5},{4,2},{5,3},{6,0},{7,1},{8,14},{9,15},{10,... | collective-permute-start | bytes 24584 | tf_op jit(solution)/shard_map/ppermute | solution.py:52
  71.2 14.3 %all-to-all-start.1 = ((f32[32,2,768]{2,1,0:T(2,128)}), f32[32,2,768]{2,1,0:T(2,128)S(1)}, u32[]{:S(2)}, u32[]{:S(2)}) async-start(f32[32,2,768]{2,1,0:T(2,128)} %reshape.111), calls=%async_computation.1 | async-start | bytes 393216 | tf_op jit(solution)/shard_map/all_to_all | solution.py:16
  76.3 2.8 %collective-permute-start.18 = (bf16[128,64]{0,1:T(8,128)(2,1)S(1)}, bf16[128,64]{0,1:T(8,128)(2,1)S(1)}, u32[]{:S(2)}, u32[]{:S(2)}) collective-permute-start(bf16[128,64]{0,1:T(8,128)(2,1)S(1)} %slice.148), channel_id=1, source_target_pairs={{0,1},{1,0},{2,3},{3,2},{4,5},{5,4},{6,7},{7,6},{8,9},{9,8},{10,11... | collective-permute-start | bytes 49160 | tf_op jit(solution)/shard_map/ppermute | solution.py:48

commit v5 on v4

--- a/solution.py
+++ b/solution.py
@@ -150,8 +150,18 @@
 PIECES = 4
 
 
-def sum_kernel(length, starts_ref, near_ref, far_ref, *refs):
-    outs, (stage, rows, sums, sems) = refs[:-4], refs[-4:]
+def sum_kernel(length, held, starts_ref, near_ref, far_ref, *refs):
+    moved = held - 1 if held else 0
+    refs = refs[1:] if held else refs
+    sources, refs, targets, note, (stage, rows, sums, sems) = (
+        refs[:moved], refs[moved : -5 - moved], refs[len(refs) - 5 - moved : -5], refs[-5], refs[-4:]
+    )
+    outs = refs
+    note[...] = jnp.zeros(note.shape, F32)
+    moves = [
+        pltpu.make_async_copy(a, b, sems.at[2 * PIECES + n])
+        for n, (a, b) in enumerate(zip(sources, targets))
+    ]
     vocab_rows, width = near_ref.shape
     chunks = width // LANES
     tile = SUBLANES * chunks
@@ -167,7 +177,7 @@
                     table.at[pl.ds(p * piece, piece)], stage.at[pl.ds(at * piece, piece)], sems.at[at]
                 )
             )
-    for copy in copies:
+    for copy in copies + moves:
         copy.start()
     rows[pl.ds(2 * vocab_rows * chunks, tile), :] = jnp.zeros((tile, LANES), F32)
     for at, copy in enumerate(copies):
@@ -195,6 +205,8 @@
                 terms = [a + b for a, b in zip(terms[::2], terms[1::2])] + terms[len(terms) // 2 * 2 :]
             sums[pl.ds(group * tile + q, chunks, stride=SUBLANES), :] = terms[0] / length
 
+    for copy in moves:
+        copy.wait()
     for n, out in enumerate(outs):
         for group in range(labels // 16):
             for c in range(chunks):
@@ -204,23 +216,60 @@
                 ).astype(out.dtype)
 
 
-def partial_means(starts, near, far, labels, length, kinds):
+def block_kernel(docs_ref, positives_ref, owner_ref, row_ref, out):
+    count, width = docs_ref.shape
+    devices, labels = out.shape[0], owner_ref.shape[1]
+    positives, row = positives_ref[...], row_ref[...]
+
+    def spread(value):
+        return jnp.broadcast_to(value.astype(F32).astype(BF16)[None], (devices,) + value.shape)
+
+    out[:, :, width:] = jnp.zeros((devices, count, out.shape[2] - width), BF16)
+    out[:, :, :width] = jnp.broadcast_to(docs_ref[...][None], (devices, count, width))
+    for n in range(3):
+        at = width + n * LANES
+        out[:, :, at : at + positives.shape[1]] = spread((positives >> (8 * n)) & 255)
+    at = width + 3 * LANES
+    second = jnp.concatenate([row & 255] + [jnp.zeros_like(row)] * (count - 1))
+    first = jnp.concatenate([owner_ref[...], second[:-1]])
+    out[:, :, at : at + labels] = spread(first)
+    out[:, :, at + labels : at + 2 * labels] = spread(
+        jnp.concatenate([row >> 8] + [jnp.zeros_like(row)] * (count - 1))
+    )
+
+
+def docs_block(docs, positives, ref_owner, ref_row, devices):
+    count, width = docs.shape
+    labels = ref_row.shape[0]
+    return pl.pallas_call(
+        block_kernel,
+        out_shape=jax.ShapeDtypeStruct((devices, count, width + 3 * LANES + 2 * labels), BF16),
+        in_specs=[pl.BlockSpec(memory_space=pltpu.VMEM)] * 4,
+        out_specs=pl.BlockSpec(memory_space=pltpu.VMEM),
+    )(docs, positives, ref_owner.reshape(1, labels), ref_row.reshape(1, labels))
+
+
+def partial_means(starts, near, far, after, labels, length, kinds, later=()):
     vocab_rows, width = near.shape
     chunks = width // LANES
     return pl.pallas_call(
-        functools.partial(sum_kernel, length),
-        out_shape=[jax.ShapeDtypeStruct((labels, width), kind) for kind in kinds],
+        functools.partial(sum_kernel, length, 0 if after is None else 1 + len(later)),
+        out_shape=[jax.ShapeDtypeStruct((labels, width), kind) for kind in kinds]
+        + [jax.ShapeDtypeStruct(x.shape, x.dtype) for x in later]
+        + [jax.ShapeDtypeStruct((SUBLANES, LANES), F32)],
         in_specs=[
             pl.BlockSpec(memory_space=pltpu.SMEM),
             pl.BlockSpec(memory_space=pl.ANY),
             pl.BlockSpec(memory_space=pl.ANY),
-        ],
-        out_specs=[pl.BlockSpec(memory_space=pltpu.VMEM) for _ in kinds],
+        ]
+        + [pl.BlockSpec(memory_space=pltpu.VMEM)] * (after is not None)
+        + [pl.BlockSpec(memory_space=pl.ANY) for _ in later],
+        out_specs=[pl.BlockSpec(memory_space=pltpu.VMEM)] * (len(kinds) + len(later) + 1),
         scratch_shapes=[
             pltpu.VMEM((2 * vocab_rows, width), BF16),
             pltpu.VMEM(((2 * vocab_rows + 2 * SUBLANES) * chunks, LANES), F32),
             pltpu.VMEM(((len(kinds) * labels + SUBLANES) * chunks, LANES), F32),
-            pltpu.SemaphoreType.DMA((2 * PIECES,)),
+            pltpu.SemaphoreType.DMA((2 * PIECES + len(later),)),
         ],
         compiler_params=pltpu.CompilerParams(vmem_limit_bytes=56 * 1024 * 1024),
         cost_estimate=pl.CostEstimate(
@@ -228,7 +277,7 @@
             bytes_accessed=4 * vocab_rows * width,
             transcendentals=0,
         ),
-    )(starts, near, far)
+    )(starts, near, far, *([] if after is None else [after]), *later)
 
 
 def by_sums(
@@ -253,6 +302,10 @@
     asked = {k: to_chip(label_tokens, k) for k in others}
     asked[0] = label_tokens
 
+    own_blocks = docs_block(docs, positives, ref_owner, ref_row, devices)
+    own_blocks, asked[1] = lax.optimization_barrier((own_blocks, asked[1]))
+    all_blocks = exchange(own_blocks, ALL)
+
     def starts(ks):
         ids = jnp.concatenate([asked[k] for k in ks])
         near = ids - me * vocab_rows
@@ -265,50 +318,54 @@
         first = (row // SUBLANES) * (SUBLANES * (width // LANES)) + row % SUBLANES
         return first.reshape(len(ks) * tokens)
 
-    ks = others + [0]
-    sent = partial_means(
-        starts(ks), token_table, other_table, labels, length, [BF16 if k else F32 for k in ks]
-    )
+    sent, after = [], None
+    half = len(others) - len(others) // 3
+    for ks in (others[:half], others[half:] + [0]):
+        later = () if after is None else (free_rows,)
+        *terms, note = partial_means(
+            starts(ks), token_table, other_table, after, labels, length,
+            [BF16 if k else F32 for k in ks], later
+        )
+        if later:
+            *terms, free_rows = terms
+        sent += terms
+        after = swap_cores(note)
     arrived = [to_chip(term, k) for term, k in zip(sent, others)]
-    docs, positives, ref_owner, ref_row, own = lax.optimization_barrier(
-        (docs, positives, ref_owner, ref_row, sent[-1])
-    )
-
-    label_dest = label_places(ref_owner[:, 0] ^ me, shards, label_cap)
-    mine = jnp.stack([label_dest, ref_row])
-    theirs = swap_cores(mine)
-    own_rel = label_dest // label_cap
-    other_rel = theirs[0] // label_cap
+    all_blocks, pooled = lax.optimization_barrier((all_blocks, sent[-1]))
+    all_docs = all_blocks[:, :, :width].reshape(all_count, width)
+    low, middle, high = (
+        all_blocks[:, :, at : at + pos_count].reshape(all_count, pos_count).astype(I32)
+        for at in range(width, width + 3 * LANES, LANES)
+    )
+    all_positives = low + 256 * middle + 65536 * high
+
+    info = lax.dynamic_slice_in_dim(all_blocks, lax.axis_index("grp") * shards, shards, 0)
+    info = info[:, :, width + 3 * LANES :].astype(I32)
+    owners = info[:, 0, :labels]
+    rows = 256 * info[:, 0, labels:] + info[:, 1, :labels]
+    marks = owners[:, None, :] == jnp.arange(shards, dtype=I32)[None, :, None]
+    order = lax.broadcasted_iota(I32, (labels, labels), 0) < lax.broadcasted_iota(
+        I32, (labels, labels), 1
+    )
+    before = jnp.dot(
+        marks.reshape(shards * shards, labels).astype(BF16),
+        order.astype(BF16),
+        preferred_element_type=F32,
+    ).reshape(shards, shards, labels)
+    slot = jnp.sum(jnp.where(marks, before, 0.0), axis=1).astype(I32)
+    slots = shards * label_cap
+    source = jnp.arange(shards, dtype=I32)[:, None]
+    coming = jnp.where(owners == me, (source ^ me) * label_cap + slot, -1).reshape(shards * labels)
+    hit = jnp.arange(slots, dtype=I32)[:, None] == coming[None, :]
+    got_rows = jnp.sum(jnp.where(hit, rows.reshape(shards * labels)[None, :] + 1, 0), axis=1) - 1
+    going = jnp.where(
+        (owners ^ me) % 2 == 0, ((owners ^ me) + (source ^ me) % 2) * label_cap + slot, -1
+    )
     places = jnp.concatenate(
-        [
-            jnp.where(own_rel % 2 == 0, label_dest, -1),
-            jnp.where(other_rel % 2 == 1, theirs[0], -1),
-        ]
-    )
-    slots = shards * label_cap
-    to_slots = jnp.arange(slots, dtype=I32)[:, None] == places[None, :]
-    chip_rows = jnp.concatenate([ref_row, theirs[1]])
-    send_rows = jnp.sum(jnp.where(to_slots, chip_rows[None, :] + 1, 0), axis=1) - 1
-    send_rows = send_rows.reshape(chips, 2 * label_cap)
-    to_slots = to_slots.astype(BF16)
-    got_rows = jnp.concatenate(
-        [send_rows[0:1]] + [to_chip(send_rows[k : k + 1], k) for k in range(1, chips)]
-    ).reshape(slots)
-
-    digits = jnp.concatenate(
-        [positives & 255, (positives >> 8) & 255, positives >> 16], axis=1
-    ).astype(BF16)
-    own_block = jnp.concatenate(
-        [docs, digits, jnp.zeros((own_docs, 128 - 3 * pos_count), BF16)], axis=1
-    )
-    all_blocks = exchange(
-        jnp.broadcast_to(own_block[None], (devices, own_docs, width + 128)), ALL
-    ).reshape(all_count, width + 128)
-    all_docs = all_blocks[:, :width]
-    d = all_blocks[:, width : width + 3 * pos_count].astype(I32)
-    all_positives = d[:, :pos_count] + 256 * d[:, pos_count : 2 * pos_count] + 65536 * d[:, 2 * pos_count :]
-
-    pooled = own
+        [lax.dynamic_index_in_dim(going, me, 0, False), lax.dynamic_index_in_dim(going, me ^ 1, 0, False)]
+    )
+    to_slots = (jnp.arange(slots, dtype=I32)[:, None] == places[None, :]).astype(BF16)
+
     for term in arrived:
         pooled = pooled + term.astype(F32)
     pooled = pooled.astype(BF16)
@@ -333,6 +390,9 @@
     errors = (jax.nn.sigmoid(logits) - hits.astype(F32)).astype(BF16)
     doc_terms = jnp.dot(errors, head, preferred_element_type=F32)
     doc_terms = doc_terms.reshape(devices, own_docs, width)
+    free_grad = lax.dot_general(
+        errors, all_docs, (((0,), (0,)), ((), ())), preferred_element_type=F32
+    ).astype(BF16)
     doc_terms, late_errors = lax.optimization_barrier((doc_terms, errors))
     doc_grad = jnp.sum(exchange(doc_terms, ALL), axis=0)
     picked = lax.dot_general(
@@ -345,9 +405,6 @@
         to_slots, returned, (((0,), (0,)), ((), ())), preferred_element_type=F32
     ).astype(BF16)
     ref_errors = chip_errors[:labels] + swap_cores(chip_errors[labels:])
-    free_grad = lax.dot_general(
-        errors, all_docs, (((0,), (0,)), ((), ())), preferred_element_type=F32
-    ).astype(BF16)
     ref_grad = jnp.dot(ref_errors, all_docs, preferred_element_type=F32).astype(BF16)
     return (free_grad, doc_grad, ref_grad)
 

time: 86.6 us -> 85.8 us (level)
  Pallas kernels: 11.9 us -> 19.9 us
  waiting for transfers between devices: 26.6 us -> 19.4 us
  starting transfers between devices: 34.4 us -> 30.1 us
  matrix products: 7.26 us -> 8.77 us
    pallas_call x1 -> x3, Pallas kernels: 11.9 us -> 19.9 us  [the longest x2 18.4 us: partial_means(): pl.pallas_call(functools.partial(sum_kernel, length, 0 if after is None e...]
    ppermute x15 -> x12, starting transfers between devices: 21.8 us -> 15.9 us  [to_chip(): lax.ppermute(x, 'shard', [(i, i ^ 2 * k) for i in range(lax.axis_size('sh...]
    all_to_all x2, waiting for transfers between devices: 11.2 us -> 5.83 us  [exchange(): return lax.all_to_all(blocks, axes, split_axis=0, concat_axis=0, tiled=True)]
    ppermute x15 -> x12, waiting for transfers between devices: 15.3 us -> 12.5 us  [to_chip(): lax.ppermute(x, 'shard', [(i, i ^ 2 * k) for i in range(lax.axis_size('sh...]
    all_to_all x2, starting transfers between devices: 9.55 us -> 11.8 us  [exchange(): return lax.all_to_all(blocks, axes, split_axis=0, concat_axis=0, tiled=True)]
    dot_general x1, matrix products: 0.74 us -> 2.27 us  [by_sums(): delta = jnp.dot(to_rows, got_vectors, preferred_element_type=F32)]
    ppermute x4, waiting for transfers between devices: 0.01 us -> 0.98 us  [swap_cores(): lax.ppermute(x, 'shard', [(i, i ^ 1) for i in range(lax.axis_size('shard'...]
    unnamed x17 -> x13, local copies, waits for them, and re-layouts: 0.04 us -> 0.96 us
  transfers between devices with their start and end apart: 21 -> 18, of which waited for: 7 -> 6; matrix products, arithmetic and copies ran while one was open for 9% -> 8% of each run, Pallas kernels for 0% -> 23%
where the time goes in v5:
time: 85.8 us; the launch traced here: 85.3 us
  starting transfers between devices  30.1 us (35%)
  Pallas kernels  19.9 us (23%)
  waiting for transfers between devices  19.4 us (23%)
  matrix products  8.77 us (10%)
  local copies, waits for them, and re-layouts  3.71 us (4%)
  other arithmetic  2.52 us (3%)
  between operations  0.95 us (1%)
    pallas_call x2, Pallas kernels, partial_means(): pl.pallas_call(functools.partial(sum_kernel, length, 0 if after is None e...  18.4 us
    ppermute x12, starting transfers between devices, to_chip(): lax.ppermute(x, 'shard', [(i, i ^ 2 * k) for i in range(lax.axis_size('sh...  15.9 us
    ppermute x12, waiting for transfers between devices, to_chip(): lax.ppermute(x, 'shard', [(i, i ^ 2 * k) for i in range(lax.axis_size('sh...  12.5 us
    all_to_all x2, starting transfers between devices, exchange(): return lax.all_to_all(blocks, axes, split_axis=0, concat_axis=0, tiled=True)  11.8 us
    all_to_all x2, waiting for transfers between devices, exchange(): return lax.all_to_all(blocks, axes, split_axis=0, concat_axis=0, tiled=True)  5.83 us
    ppermute x4, starting transfers between devices, swap_cores(): lax.ppermute(x, 'shard', [(i, i ^ 1) for i in range(lax.axis_size('shard'...  2.37 us
    dot_general x1, matrix products, by_sums(): delta = jnp.dot(to_rows, got_vectors, preferred_element_type=F32)  2.27 us
    dot_general x1, matrix products, by_sums(): lax.dot_general(errors, all_docs, (((0,), (0,)), ((), ())), preferred_ele...  1.98 us
  transfers between devices with their start and end apart: 18, of which 6 were waited for; matrix products, arithmetic and copies ran while one was open for 8% of the time, Pallas kernels for 23%

profile of v5, /device:TPU:1, one launch (start us, length us, event | category | flops | bytes accessed | tf_op | source)
XLA Modules:
  0.0 85.3 jit_solution(10778187828669704863)
XLA Ops:
  0.6 0.1 collective-permute-start.1
  0.8 2.8 %collective-permute-start = (s32[128,8]{0,1:T(8,128)}, s32[128,8]{0,1:T(8,128)S(1)}, u32[]{:S(2)}, u32[]{:S(2)}) collective-permute-start(s32[128,8]{0,1:T(8,128)} %param.12), channel_id=1, source_target_pairs={{0,2},{1,3},{2,0},{3,1},{4,6},{5,7},{6,4},{7,5},{8,10},{9,11},{10,... | collective-permute-start | bytes 12296 | tf_op jit(solution)/shard_map/ppermute | solution.py:52
  3.5 2.2 %collective-permute-start.2 = (s32[128,8]{0,1:T(8,128)}, s32[128,8]{0,1:T(8,128)S(1)}, u32[]{:S(2)}, u32[]{:S(2)}) collective-permute-start(s32[128,8]{0,1:T(8,128)} %param.12), channel_id=1, source_target_pairs={{0,6},{1,7},{2,4},{3,5},{4,2},{5,3},{6,0},{7,1},{8,14},{9,15},{10,... | collective-permute-start | bytes 12296 | tf_op jit(solution)/shard_map/ppermute | solution.py:52
  5.7 0.1 collective-permute-start.3
  5.9 1.4 %shard_map.112 = bf16[32,2,1408]{2,1,0:T(2,128)(2,1)} custom-call(bf16[2,768]{1,0:T(2,128)(2,1)} %docs_ref.1, s32[2,5]{1,0:T(2,128)} %positives_ref.1, s32[1,128]{1,0:T(1,128)} %bitcast.34, s32[1,128]{1,0:T(1,128)} %bitcast.35), custom_call_target="tpu_custom_call" | custom-call | tf_op jit(solution)/shard_map/pallas_call | solution.py:244
  7.3 5.5 %all-to-all-start = ((bf16[32,2,1408]{2,1,0:T(2,128)(2,1)}), bf16[32,2,1408]{2,1,0:T(2,128)(2,1)S(1)}, u32[]{:S(2)}, u32[]{:S(2)}) async-start(bf16[32,2,1408]{2,1,0:T(2,128)(2,1)} %shard_map.112), calls=%async_computation | async-start | bytes 360448 | tf_op jit(solution)/shard_map/all_to_all | solution.py:16
  12.8 0.7 constant_dynamic-update-slice_fusion
  13.6 0.1 copy.35
  13.7 0.1 sub.51
  13.8 0.1 copy.36
  14.1 0.1 copy.37
  14.3 0.1 copy.38
  14.6 0.6 fusion.37.starts_ref
  15.2 8.9 %shard_map.113 = (bf16[128,768]{1,0:T(8,128)(2,1)}, bf16[128,768]{1,0:T(8,128)(2,1)}, f32[8,128]{1,0:T(8,128)}) custom-call(s32[2048]{0:T(1024)} %fusion.37.starts_ref, bf16[3840,768]{1,0:T(8,128)(2,1)} %near_ref.3, bf16[3840,768]{1,0:T(8,128)(2,1)} %collective-permute-done.1.far_ref), custom_call_target="tpu_custom_call" | custom-call | flops 1572864 | bytes 11796480 | tf_op jit(solution)/shard_map/pallas_call | solution.py:255
  24.1 0.3 collective-permute-start.4
  24.4 0.6 fusion.35.starts_ref
  25.0 2.4 %collective-permute-start.6 = (bf16[128,768]{1,0:T(8,128)(2,1)}, bf16[128,768]{1,0:T(8,128)(2,1)S(1)}, u32[]{:S(2)}, u32[]{:S(2)}) collective-permute-start(bf16[128,768]{1,0:T(8,128)(2,1)} %get-tuple-element.23), channel_id=1, source_target_pairs={{0,4},{1,5},{2,6},{3,7},{4,0},{5,1},{6,2},{7,3},{8,12},{9,13},{10,... | collective-permute-start | bytes 589832 | tf_op jit(solution)/shard_map/ppermute | solution.py:52
  27.4 1.2 %collective-permute-start.5 = (bf16[128,768]{1,0:T(8,128)(2,1)}, bf16[128,768]{1,0:T(8,128)(2,1)S(1)}, u32[]{:S(2)}, u32[]{:S(2)}) collective-permute-start(bf16[128,768]{1,0:T(8,128)(2,1)} %get-tuple-element.22), channel_id=1, source_target_pairs={{0,6},{1,7},{2,4},{3,5},{4,2},{5,3},{6,0},{7,1},{8,14},{9,15},{10,... | collective-permute-start | bytes 589832 | tf_op jit(solution)/shard_map/ppermute | solution.py:52
  28.6 0.6 copy-done.2
  29.2 9.6 %shard_map.114 = (bf16[128,768]{1,0:T(8,128)(2,1)}, f32[128,768]{1,0:T(8,128)}, bf16[1280,768]{1,0:T(8,128)(2,1)}, f32[8,128]{1,0:T(8,128)}) custom-call(s32[2048]{0:T(1024)} %fusion.35.starts_ref, bf16[3840,768]{1,0:T(8,128)(2,1)} %near_ref.3, bf16[3840,768]{1,0:T(8,128)(2,1)} %collective-permute-done.1.far_ref, f32[8,128]{1,0:T(8,128)} %copy-done.2, ...), custom_call_target="tpu_custom_call" | custom-call | flops 1572864 | bytes 11796480 | tf_op jit(solution)/shard_map/pallas_call | solution.py:255
  38.9 0.1 fusion.8
  39.0 0.1 collective-permute-start.7
  39.3 0.2 select_reduce_fusion
  39.6 1.3 %collective-permute-done.6 = bf16[128,768]{1,0:T(8,128)(2,1)S(1)} collective-permute-done((bf16[128,768]{1,0:T(8,128)(2,1)}, bf16[128,768]{1,0:T(8,128)(2,1)S(1)}, u32[]{:S(2)}, u32[]{:S(2)}) %collective-permute-start.6) | collective-permute-done | bytes 196640 | tf_op jit(solution)/shard_map/ppermute | solution.py:52
  40.9 4.3 %collective-permute-done.7 = bf16[128,768]{1,0:T(8,128)(2,1)S(1)} collective-permute-done((bf16[128,768]{1,0:T(8,128)(2,1)}, bf16[128,768]{1,0:T(8,128)(2,1)S(1)}, u32[]{:S(2)}, u32[]{:S(2)}) %collective-permute-start.7) | collective-permute-done | bytes 196640 | tf_op jit(solution)/shard_map/ppermute | solution.py:52
  45.1 1.4 %multiply_reduce_fusion = (f32[128]{0:T(128)S(1)}, f32[128,768]{1,0:T(8,128)S(1)}) fusion(bf16[768,768]{1,0:T(8,128)(2,1)S(1)} %copy-done, bf16[128,768]{1,0:T(8,128)(2,1)S(1)} %collective-permute-done.7, bf16[128,768]{1,0:T(8,128)(2,1)S(1)} %collective-permute-done.6, f32[128,768]{1,0:T(8,128)} %get-tuple-element.21, ...), kind=kOutput, calls=%fused_computation.32 | convolution fusion | flops 151879552 | bytes 2556416 | tf_op jit(solution)/shard_map/dot_general | solution.py:372
  46.6 0.1 multiply_convert_fusion
  46.7 1.6 %collective-permute-start.8 = (bf16[128,768]{1,0:T(8,128)(2,1)S(1)}, bf16[128,768]{1,0:T(8,128)(2,1)S(1)}, u32[]{:S(2)}, u32[]{:S(2)}) collective-permute-start(bf16[128,768]{1,0:T(8,128)(2,1)S(1)} %multiply_convert_fusion), channel_id=1, source_target_pairs={{0,1},{1,0},{2,3},{3,2},{4,5},{5,4},{6,7},{7,6},{8,9},{9,8},{10,11... | collective-permute-start | bytes 589832 | tf_op jit(solution)/shard_map/ppermute | solution.py:48
  48.4 1.0 %collective-permute-done.8 = bf16[128,768]{1,0:T(8,128)(2,1)S(1)} collective-permute-done((bf16[128,768]{1,0:T(8,128)(2,1)S(1)}, bf16[128,768]{1,0:T(8,128)(2,1)S(1)}, u32[]{:S(2)}, u32[]{:S(2)}) %collective-permute-start.8) | collective-permute-done | bytes 196640 | tf_op jit(solution)/shard_map/ppermute | solution.py:48
  49.4 0.3 convolution_convert_fusion.1
  49.7 2.8 %collective-permute-start.11 = (bf16[64,768]{1,0:T(8,128)(2,1)S(1)}, bf16[64,768]{1,0:T(8,128)(2,1)S(1)}, u32[]{:S(2)}, u32[]{:S(2)}) collective-permute-start(bf16[64,768]{1,0:T(8,128)(2,1)S(1)} %get-tuple-element.28), channel_id=1, source_target_pairs={{0,6},{1,7},{2,4},{3,5},{4,2},{5,3},{6,0},{7,1},{8,14},{9,15},{10,... | collective-permute-start | bytes 294920 | tf_op jit(solution)/shard_map/ppermute | solution.py:52
  52.5 0.8 collective-permute-start.9
  53.8 1.8 %collective-permute-done.11 = bf16[64,768]{1,0:T(8,128)(2,1)S(1)} collective-permute-done((bf16[64,768]{1,0:T(8,128)(2,1)S(1)}, bf16[64,768]{1,0:T(8,128)(2,1)S(1)}, u32[]{:S(2)}, u32[]{:S(2)}) %collective-permute-start.11) | collective-permute-done | bytes 98336 | tf_op jit(solution)/shard_map/ppermute | solution.py:52
  55.6 5.1 %collective-permute-done.10 = bf16[64,768]{1,0:T(8,128)(2,1)S(1)} collective-permute-done((bf16[64,768]{1,0:T(8,128)(2,1)S(1)}, bf16[64,768]{1,0:T(8,128)(2,1)S(1)}, u32[]{:S(2)}, u32[]{:S(2)}) %collective-permute-start.10) | collective-permute-done | bytes 98336 | tf_op jit(solution)/shard_map/ppermute | solution.py:52
  60.8 2.3 %add_convert_fusion = bf16[1280,768]{1,0:T(8,128)(2,1)S(1)} fusion(bf16[1280,768]{1,0:T(8,128)(2,1)} %get-tuple-element.20, s32[256]{0:T(256)S(1)} %broadcast_add_fusion, bf16[64,768]{1,0:T(8,128)(2,1)S(1)} %collective-permute-done.11, bf16[64,768]{1,0:T(8,128)(2,1)S(1)} %collective-permute-done.10, bf16[64,768]{1,0:T(8,128)(2,1)S(1)} %collective-permute-done.9, ...), kind=kOutput, calls=%fused_computation | convolution fusion | flops 508166144 | bytes 4326400 | tf_op jit(solution)/shard_map/dot_general | solution.py:382
  63.0 0.8 fusion.4
  63.8 0.5 fusion.61
  64.3 0.8 reshape.175
  65.1 0.3 fusion.7
  65.5 2.2 %collective-permute-start.14 = (bf16[64,64]{0,1:T(8,128)(2,1)S(1)}, bf16[64,64]{0,1:T(8,128)(2,1)S(1)}, u32[]{:S(2)}, u32[]{:S(2)}) collective-permute-start(bf16[64,64]{0,1:T(8,128)(2,1)S(1)} %get-tuple-element.32), channel_id=1, source_target_pairs={{0,6},{1,7},{2,4},{3,5},{4,2},{5,3},{6,0},{7,1},{8,14},{9,15},{10,... | collective-permute-start | bytes 24584 | tf_op jit(solution)/shard_map/ppermute | solution.py:52
  67.6 1.4 %collective-permute-start.12 = (bf16[64,64]{0,1:T(8,128)(2,1)S(1)}, bf16[64,64]{0,1:T(8,128)(2,1)S(1)}, u32[]{:S(2)}, u32[]{:S(2)}) collective-permute-start(bf16[64,64]{0,1:T(8,128)(2,1)S(1)} %get-tuple-element.34), channel_id=1, source_target_pairs={{0,2},{1,3},{2,0},{3,1},{4,6},{5,7},{6,4},{7,5},{8,10},{9,11},{10,... | collective-permute-start | bytes 24584 | tf_op jit(solution)/shard_map/ppermute | solution.py:52
  69.0 6.3 %all-to-all-start.1 = ((f32[32,2,768]{2,1,0:T(2,128)}), f32[32,2,768]{2,1,0:T(2,128)S(1)}, u32[]{:S(2)}, u32[]{:S(2)}) async-start(f32[32,2,768]{2,1,0:T(2,128)} %reshape.175), calls=%async_computation.1 | async-start | bytes 393216 | tf_op jit(solution)/shard_map/all_to_all | solution.py:16
  75.4 0.2 convolution_convert_fusion.3
  75.6 0.3 collective-permute-start.15
  75.9 2.0 %convolution_convert_fusion = bf16[1280,768]{1,0:T(8,128)(2,1)} fusion(bf16[64,1280]{1,0:T(8,128)(2,1)S(1)} %fusion.4, bf16[64,768]{1,0:T(8,128)(2,1)S(1)} %reshape.174), kind=kOutput, calls=%fused_computation.1 | convolution fusion | flops 126812160 | bytes 2228224 | tf_op jit(solution)/shard_map/dot_general | solution.py:393
  77.9 0.9 %convolution_convert_fusion.2 = bf16[128,768]{1,0:T(8,128)(2,1)} fusion(bf16[64,768]{1,0:T(8,128)(2,1)S(1)} %reshape.174, bf16[128,64]{0,1:T(8,128)(2,1)S(1)} %collective-permute-done.15, bf16[256,64]{0,1:T(8,128)(2,1)S(1)} %convolution_convert_fusion.3), kind=kOutput, calls=%fused_computation.12 | convolution fusion | flops 12689408 | bytes 327680 | tf_op jit(solution)/shard_map/dot_general | solution.py:408
  78.8 5.8 %all-to-all-done.1 = f32[32,2,768]{2,1,0:T(2,128)S(1)} async-done(((f32[32,2,768]{2,1,0:T(2,128)}), f32[32,2,768]{2,1,0:T(2,128)S(1)}, u32[]{:S(2)}, u32[]{:S(2)}) %all-to-all-start.1) | async-done | bytes 196640 | tf_op jit(solution)/shard_map/all_to_all | solution.py:16
  84.7 0.7 reduce_sum.39
  (50 shorter events, 1.4 us)
Async XLA Ops:
  0.6 44.5 %copy-start = (bf16[768,768]{1,0:T(8,128)(2,1)S(1)}, bf16[768,768]{1,0:T(8,128)(2,1)}, u32[]{:S(2)}) copy-start(bf16[768,768]{1,0:T(8,128)(2,1)} %param.10) | copy-start | bytes 3538948
  0.6 14.6 %collective-permute-start.1 = (bf16[3840,768]{1,0:T(8,128)(2,1)}, bf16[3840,768]{1,0:T(8,128)(2,1)}, u32[]{:S(2)}, u32[]{:S(2)}) collective-permute-start(bf16[3840,768]{1,0:T(8,128)(2,1)} %near_ref.3), channel_id=1, source_target_pairs={{0,1},{1,0},{2,3},{3,2},{4,5},{5,4},{6,7},{7,6},{8,9},{9,8},{10,11... | collective-permute-start | bytes 17694728 | tf_op jit(solution)/shard_map/ppermute | solution.py:48
  0.8 6.5 %collective-permute-start = (s32[128,8]{0,1:T(8,128)}, s32[128,8]{0,1:T(8,128)S(1)}, u32[]{:S(2)}, u32[]{:S(2)}) collective-permute-start(s32[128,8]{0,1:T(8,128)} %param.12), channel_id=1, source_target_pairs={{0,2},{1,3},{2,0},{3,1},{4,6},{5,7},{6,4},{7,5},{8,10},{9,11},{10,... | collective-permute-start | bytes 12296 | tf_op jit(solution)/shard_map/ppermute | solution.py:52
  3.5 10.0 %collective-permute-start.2 = (s32[128,8]{0,1:T(8,128)}, s32[128,8]{0,1:T(8,128)S(1)}, u32[]{:S(2)}, u32[]{:S(2)}) collective-permute-start(s32[128,8]{0,1:T(8,128)} %param.12), channel_id=1, source_target_pairs={{0,6},{1,7},{2,4},{3,5},{4,2},{5,3},{6,0},{7,1},{8,14},{9,15},{10,... | collective-permute-start | bytes 12296 | tf_op jit(solution)/shard_map/ppermute | solution.py:52
  5.7 8.3 %collective-permute-start.3 = (s32[128,8]{0,1:T(8,128)}, s32[128,8]{0,1:T(8,128)S(1)}, u32[]{:S(2)}, u32[]{:S(2)}) collective-permute-start(s32[128,8]{0,1:T(8,128)} %param.12), channel_id=1, source_target_pairs={{0,4},{1,5},{2,6},{3,7},{4,0},{5,1},{6,2},{7,3},{8,12},{9,13},{10,... | collective-permute-start | bytes 12296 | tf_op jit(solution)/shard_map/ppermute | solution.py:52
  7.3 31.5 %all-to-all-start = ((bf16[32,2,1408]{2,1,0:T(2,128)(2,1)}), bf16[32,2,1408]{2,1,0:T(2,128)(2,1)S(1)}, u32[]{:S(2)}, u32[]{:S(2)}) async-start(bf16[32,2,1408]{2,1,0:T(2,128)(2,1)} %shard_map.112), calls=%async_computation | async-start | bytes 360448 | tf_op jit(solution)/shard_map/all_to_all | solution.py:16
  24.1 4.5 %collective-permute-start.4 = (f32[8,128]{1,0:T(8,128)}, f32[8,128]{1,0:T(8,128)S(1)}, u32[]{:S(2)}, u32[]{:S(2)}) collective-permute-start(f32[8,128]{1,0:T(8,128)} %get-tuple-element.17), channel_id=1, source_target_pairs={{0,1},{1,0},{2,3},{3,2},{4,5},{5,4},{6,7},{7,6},{8,9},{9,8},{10,11... | collective-permute-start | bytes 12296 | tf_op jit(solution)/shard_map/ppermute | solution.py:48
  25.0 15.9 %collective-permute-start.6 = (bf16[128,768]{1,0:T(8,128)(2,1)}, bf16[128,768]{1,0:T(8,128)(2,1)S(1)}, u32[]{:S(2)}, u32[]{:S(2)}) collective-permute-start(bf16[128,768]{1,0:T(8,128)(2,1)} %get-tuple-element.23), channel_id=1, source_target_pairs={{0,4},{1,5},{2,6},{3,7},{4,0},{5,1},{6,2},{7,3},{8,12},{9,13},{10,... | collective-permute-start | bytes 589832 | tf_op jit(solution)/shard_map/ppermute | solution.py:52
  27.4 13.5 %collective-permute-start.5 = (bf16[128,768]{1,0:T(8,128)(2,1)}, bf16[128,768]{1,0:T(8,128)(2,1)S(1)}, u32[]{:S(2)}, u32[]{:S(2)}) collective-permute-start(bf16[128,768]{1,0:T(8,128)(2,1)} %get-tuple-element.22), channel_id=1, source_target_pairs={{0,6},{1,7},{2,4},{3,5},{4,2},{5,3},{6,0},{7,1},{8,14},{9,15},{10,... | collective-permute-start | bytes 589832 | tf_op jit(solution)/shard_map/ppermute | solution.py:52
  28.6 0.6 copy-start.2
  38.8 7.8 %copy-start.1 = (f32[768]{0:T(1024)S(1)}, f32[768]{0:T(1024)}, u32[]{:S(2)}) copy-start(f32[768]{0:T(1024)} %param.11) | copy-start | bytes 9220
  39.0 6.1 %collective-permute-start.7 = (bf16[128,768]{1,0:T(8,128)(2,1)}, bf16[128,768]{1,0:T(8,128)(2,1)S(1)}, u32[]{:S(2)}, u32[]{:S(2)}) collective-permute-start(bf16[128,768]{1,0:T(8,128)(2,1)} %get-tuple-element.24), channel_id=1, source_target_pairs={{0,2},{1,3},{2,0},{3,1},{4,6},{5,7},{6,4},{7,5},{8,10},{9,11},{10,... | collective-permute-start | bytes 589832 | tf_op jit(solution)/shard_map/ppermute | solution.py:52
  46.7 2.7 %collective-permute-start.8 = (bf16[128,768]{1,0:T(8,128)(2,1)S(1)}, bf16[128,768]{1,0:T(8,128)(2,1)S(1)}, u32[]{:S(2)}, u32[]{:S(2)}) collective-permute-start(bf16[128,768]{1,0:T(8,128)(2,1)S(1)} %multiply_convert_fusion), channel_id=1, source_target_pairs={{0,1},{1,0},{2,3},{3,2},{4,5},{5,4},{6,7},{7,6},{8,9},{9,8},{10,11... | collective-permute-start | bytes 589832 | tf_op jit(solution)/shard_map/ppermute | solution.py:48
  49.7 5.9 %collective-permute-start.11 = (bf16[64,768]{1,0:T(8,128)(2,1)S(1)}, bf16[64,768]{1,0:T(8,128)(2,1)S(1)}, u32[]{:S(2)}, u32[]{:S(2)}) collective-permute-start(bf16[64,768]{1,0:T(8,128)(2,1)S(1)} %get-tuple-element.28), channel_id=1, source_target_pairs={{0,6},{1,7},{2,4},{3,5},{4,2},{5,3},{6,0},{7,1},{8,14},{9,15},{10,... | collective-permute-start | bytes 294920 | tf_op jit(solution)/shard_map/ppermute | solution.py:52
  52.5 8.3 %collective-permute-start.10 = (bf16[64,768]{1,0:T(8,128)(2,1)S(1)}, bf16[64,768]{1,0:T(8,128)(2,1)S(1)}, u32[]{:S(2)}, u32[]{:S(2)}) collective-permute-start(bf16[64,768]{1,0:T(8,128)(2,1)S(1)} %get-tuple-element.29), channel_id=1, source_target_pairs={{0,4},{1,5},{2,6},{3,7},{4,0},{5,1},{6,2},{7,3},{8,12},{9,13},{10,... | collective-permute-start | bytes 294920 | tf_op jit(solution)/shard_map/ppermute | solution.py:52
  52.5 8.3 %collective-permute-start.9 = (bf16[64,768]{1,0:T(8,128)(2,1)S(1)}, bf16[64,768]{1,0:T(8,128)(2,1)S(1)}, u32[]{:S(2)}, u32[]{:S(2)}) collective-permute-start(bf16[64,768]{1,0:T(8,128)(2,1)S(1)} %get-tuple-element.30), channel_id=1, source_target_pairs={{0,2},{1,3},{2,0},{3,1},{4,6},{5,7},{6,4},{7,5},{8,10},{9,11},{10,... | collective-permute-start | bytes 294920 | tf_op jit(solution)/shard_map/ppermute | solution.py:52
  65.5 9.9 %collective-permute-start.14 = (bf16[64,64]{0,1:T(8,128)(2,1)S(1)}, bf16[64,64]{0,1:T(8,128)(2,1)S(1)}, u32[]{:S(2)}, u32[]{:S(2)}) collective-permute-start(bf16[64,64]{0,1:T(8,128)(2,1)S(1)} %get-tuple-element.32), channel_id=1, source_target_pairs={{0,6},{1,7},{2,4},{3,5},{4,2},{5,3},{6,0},{7,1},{8,14},{9,15},{10,... | collective-permute-start | bytes 24584 | tf_op jit(solution)/shard_map/ppermute | solution.py:52
  67.6 7.7 %collective-permute-start.13 = (bf16[64,64]{0,1:T(8,128)(2,1)S(1)}, bf16[64,64]{0,1:T(8,128)(2,1)S(1)}, u32[]{:S(2)}, u32[]{:S(2)}) collective-permute-start(bf16[64,64]{0,1:T(8,128)(2,1)S(1)} %get-tuple-element.33), channel_id=1, source_target_pairs={{0,4},{1,5},{2,6},{3,7},{4,0},{5,1},{6,2},{7,3},{8,12},{9,13},{10,... | collective-permute-start | bytes 24584 | tf_op jit(solution)/shard_map/ppermute | solution.py:52
  67.6 7.7 %collective-permute-start.12 = (bf16[64,64]{0,1:T(8,128)(2,1)S(1)}, bf16[64,64]{0,1:T(8,128)(2,1)S(1)}, u32[]{:S(2)}, u32[]{:S(2)}) collective-permute-start(bf16[64,64]{0,1:T(8,128)(2,1)S(1)} %get-tuple-element.34), channel_id=1, source_target_pairs={{0,2},{1,3},{2,0},{3,1},{4,6},{5,7},{6,4},{7,5},{8,10},{9,11},{10,... | collective-permute-start | bytes 24584 | tf_op jit(solution)/shard_map/ppermute | solution.py:52
  69.0 15.6 %all-to-all-start.1 = ((f32[32,2,768]{2,1,0:T(2,128)}), f32[32,2,768]{2,1,0:T(2,128)S(1)}, u32[]{:S(2)}, u32[]{:S(2)}) async-start(f32[32,2,768]{2,1,0:T(2,128)} %reshape.175), calls=%async_computation.1 | async-start | bytes 393216 | tf_op jit(solution)/shard_map/all_to_all | solution.py:16
  75.6 2.3 %collective-permute-start.15 = (bf16[128,64]{0,1:T(8,128)(2,1)S(1)}, bf16[128,64]{0,1:T(8,128)(2,1)S(1)}, u32[]{:S(2)}, u32[]{:S(2)}) collective-permute-start(bf16[128,64]{0,1:T(8,128)(2,1)S(1)} %slice.117), channel_id=1, source_target_pairs={{0,1},{1,0},{2,3},{3,2},{4,5},{5,4},{6,7},{7,6},{8,9},{9,8},{10,11... | collective-permute-start | bytes 49160 | tf_op jit(solution)/shard_map/ppermute | solution.py:48

commit v6 on v5

--- a/solution.py
+++ b/solution.py
@@ -271,7 +271,9 @@
             pltpu.VMEM(((len(kinds) * labels + SUBLANES) * chunks, LANES), F32),
             pltpu.SemaphoreType.DMA((2 * PIECES + len(later),)),
         ],
-        compiler_params=pltpu.CompilerParams(vmem_limit_bytes=56 * 1024 * 1024),
+        compiler_params=pltpu.CompilerParams(
+            vmem_limit_bytes=(56 if after is None else 52) * 1024 * 1024
+        ),
         cost_estimate=pl.CostEstimate(
             flops=len(kinds) * labels * length * width,
             bytes_accessed=4 * vocab_rows * width,
@@ -321,13 +323,13 @@
     sent, after = [], None
     half = len(others) - len(others) // 3
     for ks in (others[:half], others[half:] + [0]):
-        later = () if after is None else (free_rows,)
+        later = () if after is None else (free_rows, enc_weight)
         *terms, note = partial_means(
             starts(ks), token_table, other_table, after, labels, length,
             [BF16 if k else F32 for k in ks], later
         )
         if later:
-            *terms, free_rows = terms
+            *terms, free_rows, enc_weight = terms
         sent += terms
         after = swap_cores(note)
     arrived = [to_chip(term, k) for term, k in zip(sent, others)]
@@ -394,13 +396,15 @@
         errors, all_docs, (((0,), (0,)), ((), ())), preferred_element_type=F32
     ).astype(BF16)
     doc_terms, late_errors = lax.optimization_barrier((doc_terms, errors))
-    doc_grad = jnp.sum(exchange(doc_terms, ALL), axis=0)
+    doc_parts = exchange(doc_terms, ALL)
     picked = lax.dot_general(
         to_rows, late_errors, (((0,), (1,)), ((), ())), preferred_element_type=F32
     ).astype(BF16)
     picked = picked.reshape(chips, 2 * label_cap, all_count)
     arrived = {k: to_chip(picked[k], k) for k in others}
     returned = jnp.concatenate([picked[0]] + [arrived[k] for k in range(1, chips)])
+    returned, doc_parts = lax.optimization_barrier((returned, doc_parts))
+    doc_grad = jnp.sum(doc_parts, axis=0)
     chip_errors = lax.dot_general(
         to_slots, returned, (((0,), (0,)), ((), ())), preferred_element_type=F32
     ).astype(BF16)

time: 85.8 us -> 82.3 us (0.959)
  matrix products: 8.77 us -> 6.22 us
  waiting for transfers between devices: 19.4 us -> 20.9 us
  starting transfers between devices: 30.1 us -> 28.7 us
    ppermute x12, waiting for transfers between devices: 12.5 us -> 18.5 us  [to_chip(): lax.ppermute(x, 'shard', [(i, i ^ 2 * k) for i in range(lax.axis_size('sh...]
    all_to_all x2, waiting for transfers between devices: 5.83 us -> 1.45 us  [exchange(): return lax.all_to_all(blocks, axes, split_axis=0, concat_axis=0, tiled=True)]
    dot_general x1, matrix products: 2.27 us -> 0.73 us  [by_sums(): delta = jnp.dot(to_rows, got_vectors, preferred_element_type=F32)]
    dot_general x1, matrix products: 1.43 us -> 0.44 us  [by_sums(): projected = jnp.dot(pooled, enc_weight, preferred_element_type=F32)]
  transfers between devices with their start and end apart: 18 -> 18, of which waited for: 6 -> 8; matrix products, arithmetic and copies ran while one was open for 8% -> 8% of each run, Pallas kernels for 23% -> 24%
where the time goes in v6:
time: 82.3 us; the launch traced here: 81.5 us
  starting transfers between devices  28.7 us (35%)
  waiting for transfers between devices  20.9 us (25%)
  Pallas kernels  19.6 us (24%)
  matrix products  6.22 us (8%)
  local copies, waits for them, and re-layouts  3.12 us (4%)
  other arithmetic  2.01 us (2%)
  between operations  0.94 us (1%)
    ppermute x12, waiting for transfers between devices, to_chip(): lax.ppermute(x, 'shard', [(i, i ^ 2 * k) for i in range(lax.axis_size('sh...  18.5 us
    pallas_call x2, Pallas kernels, partial_means(): pl.pallas_call(functools.partial(sum_kernel, length, 0 if after is None e...  18.1 us
    ppermute x12, starting transfers between devices, to_chip(): lax.ppermute(x, 'shard', [(i, i ^ 2 * k) for i in range(lax.axis_size('sh...  16.1 us
    all_to_all x2, starting transfers between devices, exchange(): return lax.all_to_all(blocks, axes, split_axis=0, concat_axis=0, tiled=True)  11 us
    dot_general x1, matrix products, by_sums(): lax.dot_general(errors, all_docs, (((0,), (0,)), ((), ())), preferred_ele...  1.99 us
  transfers between devices with their start and end apart: 18, of which 8 were waited for; matrix products, arithmetic and copies ran while one was open for 8% of the time, Pallas kernels for 24%

profile of v6, /device:TPU:1, one launch (start us, length us, event | category | flops | bytes accessed | tf_op | source)
XLA Modules:
  0.0 81.5 jit_solution(8078480574837045369)
XLA Ops:
  0.6 0.1 collective-permute-start.1
  0.8 2.8 %collective-permute-start = (s32[128,8]{0,1:T(8,128)}, s32[128,8]{0,1:T(8,128)S(1)}, u32[]{:S(2)}, u32[]{:S(2)}) collective-permute-start(s32[128,8]{0,1:T(8,128)} %param.12), channel_id=1, source_target_pairs={{0,2},{1,3},{2,0},{3,1},{4,6},{5,7},{6,4},{7,5},{8,10},{9,11},{10,... | collective-permute-start | bytes 12296 | tf_op jit(solution)/shard_map/ppermute | solution.py:52
  3.5 2.2 %collective-permute-start.2 = (s32[128,8]{0,1:T(8,128)}, s32[128,8]{0,1:T(8,128)S(1)}, u32[]{:S(2)}, u32[]{:S(2)}) collective-permute-start(s32[128,8]{0,1:T(8,128)} %param.12), channel_id=1, source_target_pairs={{0,6},{1,7},{2,4},{3,5},{4,2},{5,3},{6,0},{7,1},{8,14},{9,15},{10,... | collective-permute-start | bytes 12296 | tf_op jit(solution)/shard_map/ppermute | solution.py:52
  5.7 0.1 collective-permute-start.3
  5.8 1.4 %shard_map.112 = bf16[32,2,1408]{2,1,0:T(2,128)(2,1)} custom-call(bf16[2,768]{1,0:T(2,128)(2,1)} %docs_ref.1, s32[2,5]{1,0:T(2,128)} %positives_ref.1, s32[1,128]{1,0:T(1,128)} %bitcast.35, s32[1,128]{1,0:T(1,128)} %bitcast.36), custom_call_target="tpu_custom_call" | custom-call | tf_op jit(solution)/shard_map/pallas_call | solution.py:244
  7.3 5.5 %all-to-all-start = ((bf16[32,2,1408]{2,1,0:T(2,128)(2,1)}), bf16[32,2,1408]{2,1,0:T(2,128)(2,1)S(1)}, u32[]{:S(2)}, u32[]{:S(2)}) async-start(bf16[32,2,1408]{2,1,0:T(2,128)(2,1)} %shard_map.112), calls=%async_computation | async-start | bytes 360448 | tf_op jit(solution)/shard_map/all_to_all | solution.py:16
  12.9 0.7 constant_dynamic-update-slice_fusion
  13.6 0.1 copy.35
  13.7 0.1 sub.51
  13.8 0.1 copy.36
  13.9 0.1 select_n.93
  14.1 0.1 copy.37
  14.3 0.1 copy.38
  14.6 0.6 fusion.30.starts_ref
  15.2 8.9 %shard_map.113 = (bf16[128,768]{1,0:T(8,128)(2,1)}, bf16[128,768]{1,0:T(8,128)(2,1)}, f32[8,128]{1,0:T(8,128)}) custom-call(s32[2048]{0:T(1024)} %fusion.30.starts_ref, bf16[3840,768]{1,0:T(8,128)(2,1)} %near_ref.3, bf16[3840,768]{1,0:T(8,128)(2,1)} %collective-permute-done.1.far_ref), custom_call_target="tpu_custom_call" | custom-call | flops 1572864 | bytes 11796480 | tf_op jit(solution)/shard_map/pallas_call | solution.py:255
  24.1 0.3 collective-permute-start.4
  24.4 2.5 %collective-permute-start.6 = (bf16[128,768]{1,0:T(8,128)(2,1)}, bf16[128,768]{1,0:T(8,128)(2,1)S(1)}, u32[]{:S(2)}, u32[]{:S(2)}) collective-permute-start(bf16[128,768]{1,0:T(8,128)(2,1)} %get-tuple-element.26), channel_id=1, source_target_pairs={{0,4},{1,5},{2,6},{3,7},{4,0},{5,1},{6,2},{7,3},{8,12},{9,13},{10,... | collective-permute-start | bytes 589832 | tf_op jit(solution)/shard_map/ppermute | solution.py:52
  26.9 1.2 %collective-permute-start.5 = (bf16[128,768]{1,0:T(8,128)(2,1)}, bf16[128,768]{1,0:T(8,128)(2,1)S(1)}, u32[]{:S(2)}, u32[]{:S(2)}) collective-permute-start(bf16[128,768]{1,0:T(8,128)(2,1)} %get-tuple-element.25), channel_id=1, source_target_pairs={{0,6},{1,7},{2,4},{3,5},{4,2},{5,3},{6,0},{7,1},{8,14},{9,15},{10,... | collective-permute-start | bytes 589832 | tf_op jit(solution)/shard_map/ppermute | solution.py:52
  28.1 9.3 %shard_map.114 = (bf16[128,768]{1,0:T(8,128)(2,1)S(1)}, f32[128,768]{1,0:T(8,128)S(1)}, bf16[1280,768]{1,0:T(8,128)(2,1)}, bf16[768,768]{1,0:T(8,128)(2,1)S(1)}, f32[8,128]{1,0:T(8,128)}) custom-call(s32[2048]{0:T(1024)S(1)} %fusion.28.starts_ref, bf16[3840,768]{1,0:T(8,128)(2,1)} %near_ref.3, bf16[3840,768]{1,0:T(8,128)(2,1)} %collective-permute-done.1.far_ref, ...), custom_call_target="tpu_custom_call" | custom-call | flops 1572864 | bytes 11796480 | tf_op jit(solution)/shard_map/pallas_call | solution.py:255
  37.4 0.1 fusion.8
  37.6 0.1 collective-permute-start.7
  37.8 0.2 select_reduce_fusion
  38.1 2.2 %collective-permute-done.6 = bf16[128,768]{1,0:T(8,128)(2,1)S(1)} collective-permute-done((bf16[128,768]{1,0:T(8,128)(2,1)}, bf16[128,768]{1,0:T(8,128)(2,1)S(1)}, u32[]{:S(2)}, u32[]{:S(2)}) %collective-permute-start.6) | collective-permute-done | bytes 196640 | tf_op jit(solution)/shard_map/ppermute | solution.py:52
  40.4 4.2 %collective-permute-done.7 = bf16[128,768]{1,0:T(8,128)(2,1)S(1)} collective-permute-done((bf16[128,768]{1,0:T(8,128)(2,1)S(1)}, bf16[128,768]{1,0:T(8,128)(2,1)S(1)}, u32[]{:S(2)}, u32[]{:S(2)}) %collective-permute-start.7) | collective-permute-done | bytes 196640 | tf_op jit(solution)/shard_map/ppermute | solution.py:52
  44.6 0.4 multiply_reduce_fusion
  45.1 0.1 multiply_convert_fusion
  45.2 1.1 %collective-permute-start.8 = (bf16[128,768]{1,0:T(8,128)(2,1)S(1)}, bf16[128,768]{1,0:T(8,128)(2,1)S(1)}, u32[]{:S(2)}, u32[]{:S(2)}) collective-permute-start(bf16[128,768]{1,0:T(8,128)(2,1)S(1)} %multiply_convert_fusion), channel_id=1, source_target_pairs={{0,1},{1,0},{2,3},{3,2},{4,5},{5,4},{6,7},{7,6},{8,9},{9,8},{10,11... | collective-permute-start | bytes 589832 | tf_op jit(solution)/shard_map/ppermute | solution.py:48
  46.4 1.0 %collective-permute-done.8 = bf16[128,768]{1,0:T(8,128)(2,1)S(1)} collective-permute-done((bf16[128,768]{1,0:T(8,128)(2,1)S(1)}, bf16[128,768]{1,0:T(8,128)(2,1)S(1)}, u32[]{:S(2)}, u32[]{:S(2)}) %collective-permute-start.8) | collective-permute-done | bytes 196640 | tf_op jit(solution)/shard_map/ppermute | solution.py:48
  47.3 0.3 convolution_convert_fusion.1
  47.6 3.3 %collective-permute-start.11 = (bf16[64,768]{1,0:T(8,128)(2,1)S(1)}, bf16[64,768]{1,0:T(8,128)(2,1)S(1)}, u32[]{:S(2)}, u32[]{:S(2)}) collective-permute-start(bf16[64,768]{1,0:T(8,128)(2,1)S(1)} %get-tuple-element.34), channel_id=1, source_target_pairs={{0,6},{1,7},{2,4},{3,5},{4,2},{5,3},{6,0},{7,1},{8,14},{9,15},{10,... | collective-permute-start | bytes 294920 | tf_op jit(solution)/shard_map/ppermute | solution.py:52
  51.0 0.4 collective-permute-start.9
  51.8 1.8 %collective-permute-done.11 = bf16[64,768]{1,0:T(8,128)(2,1)S(1)} collective-permute-done((bf16[64,768]{1,0:T(8,128)(2,1)S(1)}, bf16[64,768]{1,0:T(8,128)(2,1)S(1)}, u32[]{:S(2)}, u32[]{:S(2)}) %collective-permute-start.11) | collective-permute-done | bytes 98336 | tf_op jit(solution)/shard_map/ppermute | solution.py:52
  53.6 5.7 %collective-permute-done.10 = bf16[64,768]{1,0:T(8,128)(2,1)S(1)} collective-permute-done((bf16[64,768]{1,0:T(8,128)(2,1)S(1)}, bf16[64,768]{1,0:T(8,128)(2,1)S(1)}, u32[]{:S(2)}, u32[]{:S(2)}) %collective-permute-start.10) | collective-permute-done | bytes 98336 | tf_op jit(solution)/shard_map/ppermute | solution.py:52
  59.3 0.7 add_convert_fusion
  60.0 0.8 fusion.4
  60.8 0.5 fusion.53
  61.2 0.8 reshape.175
  62.0 5.5 %all-to-all-start.1 = ((f32[32,2,768]{2,1,0:T(2,128)}), f32[32,2,768]{2,1,0:T(2,128)S(1)}, u32[]{:S(2)}, u32[]{:S(2)}) async-start(f32[32,2,768]{2,1,0:T(2,128)} %reshape.175), calls=%async_computation.1 | async-start | bytes 393216 | tf_op jit(solution)/shard_map/all_to_all | solution.py:16
  67.5 0.3 fusion.7
  67.9 3.2 %collective-permute-start.14 = (bf16[64,64]{0,1:T(8,128)(2,1)S(1)}, bf16[64,64]{0,1:T(8,128)(2,1)S(1)}, u32[]{:S(2)}, u32[]{:S(2)}) collective-permute-start(bf16[64,64]{0,1:T(8,128)(2,1)S(1)} %get-tuple-element.38), channel_id=1, source_target_pairs={{0,6},{1,7},{2,4},{3,5},{4,2},{5,3},{6,0},{7,1},{8,14},{9,15},{10,... | collective-permute-start | bytes 24584 | tf_op jit(solution)/shard_map/ppermute | solution.py:52
  71.2 0.4 collective-permute-start.12
  71.6 3.4 %collective-permute-done.14 = bf16[64,64]{0,1:T(8,128)(2,1)S(1)} collective-permute-done((bf16[64,64]{0,1:T(8,128)(2,1)S(1)}, bf16[64,64]{0,1:T(8,128)(2,1)S(1)}, u32[]{:S(2)}, u32[]{:S(2)}) %collective-permute-start.14) | collective-permute-done | bytes 8224 | tf_op jit(solution)/shard_map/ppermute | solution.py:52
  75.0 1.2 %collective-permute-done.13 = bf16[64,64]{0,1:T(8,128)(2,1)S(1)} collective-permute-done((bf16[64,64]{0,1:T(8,128)(2,1)S(1)}, bf16[64,64]{0,1:T(8,128)(2,1)S(1)}, u32[]{:S(2)}, u32[]{:S(2)}) %collective-permute-start.13) | collective-permute-done | bytes 8224 | tf_op jit(solution)/shard_map/ppermute | solution.py:52
  76.2 1.5 %all-to-all-done.1 = f32[32,2,768]{2,1,0:T(2,128)S(1)} async-done(((f32[32,2,768]{2,1,0:T(2,128)}), f32[32,2,768]{2,1,0:T(2,128)S(1)}, u32[]{:S(2)}, u32[]{:S(2)}) %all-to-all-start.1) | async-done | bytes 196640 | tf_op jit(solution)/shard_map/all_to_all | solution.py:16
  77.7 0.2 convolution_convert_fusion.3
  77.9 2.0 %convolution_convert_fusion = bf16[1280,768]{1,0:T(8,128)(2,1)} fusion(bf16[64,1280]{1,0:T(8,128)(2,1)S(1)} %fusion.4, bf16[64,768]{1,0:T(8,128)(2,1)S(1)} %reshape.174), kind=kOutput, calls=%fused_computation.1 | convolution fusion | flops 126812160 | bytes 2228224 | tf_op jit(solution)/shard_map/dot_general | solution.py:395
  79.9 0.7 reduce_sum.39
  80.6 0.9 %convolution_convert_fusion.2 = bf16[128,768]{1,0:T(8,128)(2,1)} fusion(bf16[64,768]{1,0:T(8,128)(2,1)S(1)} %reshape.174, bf16[128,64]{0,1:T(8,128)(2,1)S(1)} %collective-permute-done.15, bf16[256,64]{0,1:T(8,128)(2,1)S(1)} %convolution_convert_fusion.3), kind=kOutput, calls=%fused_computation.12 | convolution fusion | flops 12689408 | bytes 327680 | tf_op jit(solution)/shard_map/dot_general | solution.py:412
  (49 shorter events, 1.4 us)
Async XLA Ops:
  0.6 14.6 %collective-permute-start.1 = (bf16[3840,768]{1,0:T(8,128)(2,1)}, bf16[3840,768]{1,0:T(8,128)(2,1)}, u32[]{:S(2)}, u32[]{:S(2)}) collective-permute-start(bf16[3840,768]{1,0:T(8,128)(2,1)} %near_ref.3), channel_id=1, source_target_pairs={{0,1},{1,0},{2,3},{3,2},{4,5},{5,4},{6,7},{7,6},{8,9},{9,8},{10,11... | collective-permute-start | bytes 17694728 | tf_op jit(solution)/shard_map/ppermute | solution.py:48
  0.8 6.5 %collective-permute-start = (s32[128,8]{0,1:T(8,128)}, s32[128,8]{0,1:T(8,128)S(1)}, u32[]{:S(2)}, u32[]{:S(2)}) collective-permute-start(s32[128,8]{0,1:T(8,128)} %param.12), channel_id=1, source_target_pairs={{0,2},{1,3},{2,0},{3,1},{4,6},{5,7},{6,4},{7,5},{8,10},{9,11},{10,... | collective-permute-start | bytes 12296 | tf_op jit(solution)/shard_map/ppermute | solution.py:52
  3.5 10.0 %collective-permute-start.2 = (s32[128,8]{0,1:T(8,128)}, s32[128,8]{0,1:T(8,128)S(1)}, u32[]{:S(2)}, u32[]{:S(2)}) collective-permute-start(s32[128,8]{0,1:T(8,128)} %param.12), channel_id=1, source_target_pairs={{0,6},{1,7},{2,4},{3,5},{4,2},{5,3},{6,0},{7,1},{8,14},{9,15},{10,... | collective-permute-start | bytes 12296 | tf_op jit(solution)/shard_map/ppermute | solution.py:52
  5.7 8.4 %collective-permute-start.3 = (s32[128,8]{0,1:T(8,128)}, s32[128,8]{0,1:T(8,128)S(1)}, u32[]{:S(2)}, u32[]{:S(2)}) collective-permute-start(s32[128,8]{0,1:T(8,128)} %param.12), channel_id=1, source_target_pairs={{0,4},{1,5},{2,6},{3,7},{4,0},{5,1},{6,2},{7,3},{8,12},{9,13},{10,... | collective-permute-start | bytes 12296 | tf_op jit(solution)/shard_map/ppermute | solution.py:52
  7.3 30.0 %all-to-all-start = ((bf16[32,2,1408]{2,1,0:T(2,128)(2,1)}), bf16[32,2,1408]{2,1,0:T(2,128)(2,1)S(1)}, u32[]{:S(2)}, u32[]{:S(2)}) async-start(bf16[32,2,1408]{2,1,0:T(2,128)(2,1)} %shard_map.112), calls=%async_computation | async-start | bytes 360448 | tf_op jit(solution)/shard_map/all_to_all | solution.py:16
  24.1 4.0 %collective-permute-start.4 = (f32[8,128]{1,0:T(8,128)}, f32[8,128]{1,0:T(8,128)S(1)}, u32[]{:S(2)}, u32[]{:S(2)}) collective-permute-start(f32[8,128]{1,0:T(8,128)} %get-tuple-element.20), channel_id=1, source_target_pairs={{0,1},{1,0},{2,3},{3,2},{4,5},{5,4},{6,7},{7,6},{8,9},{9,8},{10,11... | collective-permute-start | bytes 12296 | tf_op jit(solution)/shard_map/ppermute | solution.py:48
  24.4 15.9 %collective-permute-start.6 = (bf16[128,768]{1,0:T(8,128)(2,1)}, bf16[128,768]{1,0:T(8,128)(2,1)S(1)}, u32[]{:S(2)}, u32[]{:S(2)}) collective-permute-start(bf16[128,768]{1,0:T(8,128)(2,1)} %get-tuple-element.26), channel_id=1, source_target_pairs={{0,4},{1,5},{2,6},{3,7},{4,0},{5,1},{6,2},{7,3},{8,12},{9,13},{10,... | collective-permute-start | bytes 589832 | tf_op jit(solution)/shard_map/ppermute | solution.py:52
  26.9 13.5 %collective-permute-start.5 = (bf16[128,768]{1,0:T(8,128)(2,1)}, bf16[128,768]{1,0:T(8,128)(2,1)S(1)}, u32[]{:S(2)}, u32[]{:S(2)}) collective-permute-start(bf16[128,768]{1,0:T(8,128)(2,1)} %get-tuple-element.25), channel_id=1, source_target_pairs={{0,6},{1,7},{2,4},{3,5},{4,2},{5,3},{6,0},{7,1},{8,14},{9,15},{10,... | collective-permute-start | bytes 589832 | tf_op jit(solution)/shard_map/ppermute | solution.py:52
  37.3 7.7 %copy-start = (f32[768]{0:T(1024)S(1)}, f32[768]{0:T(1024)}, u32[]{:S(2)}) copy-start(f32[768]{0:T(1024)} %param.11) | copy-start | bytes 9220
  37.6 7.0 %collective-permute-start.7 = (bf16[128,768]{1,0:T(8,128)(2,1)S(1)}, bf16[128,768]{1,0:T(8,128)(2,1)S(1)}, u32[]{:S(2)}, u32[]{:S(2)}) collective-permute-start(bf16[128,768]{1,0:T(8,128)(2,1)S(1)} %get-tuple-element.27), channel_id=1, source_target_pairs={{0,2},{1,3},{2,0},{3,1},{4,6},{5,7},{6,4},{7,5},{8,10},{9,11},{10,... | collective-permute-start | bytes 589832 | tf_op jit(solution)/shard_map/ppermute | solution.py:52
  45.0 14.2 %copy-start.1 = (bf16[1280,768]{1,0:T(8,128)(2,1)S(1)}, bf16[1280,768]{1,0:T(8,128)(2,1)}, u32[]{:S(2)}) copy-start(bf16[1280,768]{1,0:T(8,128)(2,1)} %get-tuple-element.23) | copy-start | bytes 5898244
  45.2 2.1 %collective-permute-start.8 = (bf16[128,768]{1,0:T(8,128)(2,1)S(1)}, bf16[128,768]{1,0:T(8,128)(2,1)S(1)}, u32[]{:S(2)}, u32[]{:S(2)}) collective-permute-start(bf16[128,768]{1,0:T(8,128)(2,1)S(1)} %multiply_convert_fusion), channel_id=1, source_target_pairs={{0,1},{1,0},{2,3},{3,2},{4,5},{5,4},{6,7},{7,6},{8,9},{9,8},{10,11... | collective-permute-start | bytes 589832 | tf_op jit(solution)/shard_map/ppermute | solution.py:48
  47.6 5.9 %collective-permute-start.11 = (bf16[64,768]{1,0:T(8,128)(2,1)S(1)}, bf16[64,768]{1,0:T(8,128)(2,1)S(1)}, u32[]{:S(2)}, u32[]{:S(2)}) collective-permute-start(bf16[64,768]{1,0:T(8,128)(2,1)S(1)} %get-tuple-element.34), channel_id=1, source_target_pairs={{0,6},{1,7},{2,4},{3,5},{4,2},{5,3},{6,0},{7,1},{8,14},{9,15},{10,... | collective-permute-start | bytes 294920 | tf_op jit(solution)/shard_map/ppermute | solution.py:52
  51.0 8.3 %collective-permute-start.10 = (bf16[64,768]{1,0:T(8,128)(2,1)S(1)}, bf16[64,768]{1,0:T(8,128)(2,1)S(1)}, u32[]{:S(2)}, u32[]{:S(2)}) collective-permute-start(bf16[64,768]{1,0:T(8,128)(2,1)S(1)} %get-tuple-element.35), channel_id=1, source_target_pairs={{0,4},{1,5},{2,6},{3,7},{4,0},{5,1},{6,2},{7,3},{8,12},{9,13},{10,... | collective-permute-start | bytes 294920 | tf_op jit(solution)/shard_map/ppermute | solution.py:52
  51.0 8.3 %collective-permute-start.9 = (bf16[64,768]{1,0:T(8,128)(2,1)S(1)}, bf16[64,768]{1,0:T(8,128)(2,1)S(1)}, u32[]{:S(2)}, u32[]{:S(2)}) collective-permute-start(bf16[64,768]{1,0:T(8,128)(2,1)S(1)} %get-tuple-element.36), channel_id=1, source_target_pairs={{0,2},{1,3},{2,0},{3,1},{4,6},{5,7},{6,4},{7,5},{8,10},{9,11},{10,... | collective-permute-start | bytes 294920 | tf_op jit(solution)/shard_map/ppermute | solution.py:52
  62.0 15.6 %all-to-all-start.1 = ((f32[32,2,768]{2,1,0:T(2,128)}), f32[32,2,768]{2,1,0:T(2,128)S(1)}, u32[]{:S(2)}, u32[]{:S(2)}) async-start(f32[32,2,768]{2,1,0:T(2,128)} %reshape.175), calls=%async_computation.1 | async-start | bytes 393216 | tf_op jit(solution)/shard_map/all_to_all | solution.py:16
  67.9 7.0 %collective-permute-start.14 = (bf16[64,64]{0,1:T(8,128)(2,1)S(1)}, bf16[64,64]{0,1:T(8,128)(2,1)S(1)}, u32[]{:S(2)}, u32[]{:S(2)}) collective-permute-start(bf16[64,64]{0,1:T(8,128)(2,1)S(1)} %get-tuple-element.38), channel_id=1, source_target_pairs={{0,6},{1,7},{2,4},{3,5},{4,2},{5,3},{6,0},{7,1},{8,14},{9,15},{10,... | collective-permute-start | bytes 24584 | tf_op jit(solution)/shard_map/ppermute | solution.py:52
  71.2 4.9 %collective-permute-start.13 = (bf16[64,64]{0,1:T(8,128)(2,1)S(1)}, bf16[64,64]{0,1:T(8,128)(2,1)S(1)}, u32[]{:S(2)}, u32[]{:S(2)}) collective-permute-start(bf16[64,64]{0,1:T(8,128)(2,1)S(1)} %get-tuple-element.39), channel_id=1, source_target_pairs={{0,4},{1,5},{2,6},{3,7},{4,0},{5,1},{6,2},{7,3},{8,12},{9,13},{10,... | collective-permute-start | bytes 24584 | tf_op jit(solution)/shard_map/ppermute | solution.py:52
  71.2 4.9 %collective-permute-start.12 = (bf16[64,64]{0,1:T(8,128)(2,1)S(1)}, bf16[64,64]{0,1:T(8,128)(2,1)S(1)}, u32[]{:S(2)}, u32[]{:S(2)}) collective-permute-start(bf16[64,64]{0,1:T(8,128)(2,1)S(1)} %get-tuple-element.40), channel_id=1, source_target_pairs={{0,2},{1,3},{2,0},{3,1},{4,6},{5,7},{6,4},{7,5},{8,10},{9,11},{10,... | collective-permute-start | bytes 24584 | tf_op jit(solution)/shard_map/ppermute | solution.py:52
  77.8 2.7 %collective-permute-start.15 = (bf16[128,64]{0,1:T(8,128)(2,1)S(1)}, bf16[128,64]{0,1:T(8,128)(2,1)S(1)}, u32[]{:S(2)}, u32[]{:S(2)}) collective-permute-start(bf16[128,64]{0,1:T(8,128)(2,1)S(1)} %slice.117), channel_id=1, source_target_pairs={{0,1},{1,0},{2,3},{3,2},{4,5},{5,4},{6,7},{7,6},{8,9},{9,8},{10,11... | collective-permute-start | bytes 49160 | tf_op jit(solution)/shard_map/ppermute | solution.py:48

commit v7 on v6

--- a/solution.py
+++ b/solution.py
@@ -150,23 +150,23 @@
 PIECES = 4
 
 
-def sum_kernel(length, held, starts_ref, near_ref, far_ref, *refs):
-    moved = held - 1 if held else 0
+def sum_kernel(count, moved, held, me_ref, *refs):
+    ids_refs, (near_ref, far_ref), refs = refs[:count], refs[count : count + 2], refs[count + 2 :]
     refs = refs[1:] if held else refs
-    sources, refs, targets, note, (stage, rows, sums, sems) = (
-        refs[:moved], refs[moved : -5 - moved], refs[len(refs) - 5 - moved : -5], refs[-5], refs[-4:]
-    )
-    outs = refs
+    sources, outs, targets = refs[:moved], refs[moved : moved + count], refs[moved + count : -7]
+    note, stage, rows, sums, found, starts, sems = refs[-7:]
     note[...] = jnp.zeros(note.shape, F32)
     moves = [
-        pltpu.make_async_copy(a, b, sems.at[2 * PIECES + n])
+        pltpu.make_async_copy(a, b, sems.at[2 * PIECES + 1 + n])
         for n, (a, b) in enumerate(zip(sources, targets))
     ]
     vocab_rows, width = near_ref.shape
+    length, labels = ids_refs[0].shape
     chunks = width // LANES
     tile = SUBLANES * chunks
-    labels = outs[0].shape[0]
     piece = vocab_rows // PIECES
+    core = me_ref[0] & 1
+    bases = (core * vocab_rows, (1 - core) * vocab_rows)
 
     copies = []
     for half, table in enumerate((near_ref, far_ref)):
@@ -174,18 +174,26 @@
             at = half * PIECES + p
             copies.append(
                 pltpu.make_async_copy(
-                    table.at[pl.ds(p * piece, piece)], stage.at[pl.ds(at * piece, piece)], sems.at[at]
+                    table.at[pl.ds(p * piece, piece)],
+                    stage.at[pl.ds(pl.multiple_of(bases[half] + p * piece, 16), piece)],
+                    sems.at[at],
                 )
             )
     for copy in copies + moves:
         copy.start()
+    for n, ids_ref in enumerate(ids_refs):
+        row = ids_ref[...] - (me_ref[0] >> 1) * (2 * vocab_rows)
+        row = jnp.where((row >= 0) & (row < 2 * vocab_rows), row, 2 * vocab_rows)
+        found[n * length : (n + 1) * length, :] = (row >> 3) * tile + (row & 7)
+    place = pltpu.make_async_copy(found, starts, sems.at[2 * PIECES])
+    place.start()
     rows[pl.ds(2 * vocab_rows * chunks, tile), :] = jnp.zeros((tile, LANES), F32)
     for at, copy in enumerate(copies):
         copy.wait()
 
         @pl.loop(0, piece // 16, unroll=4)
         def _(group):
-            first = pl.multiple_of(at * piece + group * 16, 16)
+            first = pl.multiple_of(bases[at // PIECES] + at % PIECES * piece + group * 16, 16)
             block = stage[pl.ds(first, 16), :].astype(F32)
             to = pl.multiple_of(first * chunks, 16)
             for h in range(2):
@@ -194,16 +202,21 @@
                         h * SUBLANES : (h + 1) * SUBLANES, c * LANES : (c + 1) * LANES
                     ]
 
-    @pl.loop(0, len(outs) * labels // SUBLANES)
-    def _(group):
-        for q in range(SUBLANES):
-            first = (group * SUBLANES + q) * length
-            terms = [
-                rows[pl.ds(starts_ref[first + j], chunks, stride=SUBLANES), :] for j in range(length)
-            ]
-            while len(terms) > 1:
-                terms = [a + b for a, b in zip(terms[::2], terms[1::2])] + terms[len(terms) // 2 * 2 :]
-            sums[pl.ds(group * tile + q, chunks, stride=SUBLANES), :] = terms[0] / length
+    place.wait()
+    for n in range(count):
+
+        @pl.loop(0, labels // SUBLANES)
+        def _(group):
+            for q in range(SUBLANES):
+                label = group * SUBLANES + q
+                terms = [
+                    rows[pl.ds(starts[n * length + j, label], chunks, stride=SUBLANES), :]
+                    for j in range(length)
+                ]
+                while len(terms) > 1:
+                    terms = [a + b for a, b in zip(terms[::2], terms[1::2])] + terms[len(terms) // 2 * 2 :]
+                to = (n * labels // SUBLANES + group) * tile + q
+                sums[pl.ds(to, chunks, stride=SUBLANES), :] = terms[0] / length
 
     for copy in moves:
         copy.wait()
@@ -249,27 +262,29 @@
     )(docs, positives, ref_owner.reshape(1, labels), ref_row.reshape(1, labels))
 
 
-def partial_means(starts, near, far, after, labels, length, kinds, later=()):
+def partial_means(me, ids, near, far, after, kinds, later=()):
     vocab_rows, width = near.shape
     chunks = width // LANES
+    length, labels = ids[0].shape
+    held = [] if after is None else [after]
     return pl.pallas_call(
-        functools.partial(sum_kernel, length, 0 if after is None else 1 + len(later)),
+        functools.partial(sum_kernel, len(kinds), len(later), bool(held)),
         out_shape=[jax.ShapeDtypeStruct((labels, width), kind) for kind in kinds]
         + [jax.ShapeDtypeStruct(x.shape, x.dtype) for x in later]
         + [jax.ShapeDtypeStruct((SUBLANES, LANES), F32)],
-        in_specs=[
-            pl.BlockSpec(memory_space=pltpu.SMEM),
-            pl.BlockSpec(memory_space=pl.ANY),
-            pl.BlockSpec(memory_space=pl.ANY),
-        ]
-        + [pl.BlockSpec(memory_space=pltpu.VMEM)] * (after is not None)
+        in_specs=[pl.BlockSpec(memory_space=pltpu.SMEM)]
+        + [pl.BlockSpec(memory_space=pltpu.VMEM)] * len(ids)
+        + [pl.BlockSpec(memory_space=pl.ANY)] * 2
+        + [pl.BlockSpec(memory_space=pltpu.VMEM) for _ in held]
         + [pl.BlockSpec(memory_space=pl.ANY) for _ in later],
         out_specs=[pl.BlockSpec(memory_space=pltpu.VMEM)] * (len(kinds) + len(later) + 1),
         scratch_shapes=[
             pltpu.VMEM((2 * vocab_rows, width), BF16),
             pltpu.VMEM(((2 * vocab_rows + 2 * SUBLANES) * chunks, LANES), F32),
             pltpu.VMEM(((len(kinds) * labels + SUBLANES) * chunks, LANES), F32),
-            pltpu.SemaphoreType.DMA((2 * PIECES + len(later),)),
+            pltpu.VMEM((len(ids) * length, labels), I32),
+            pltpu.SMEM((len(ids) * length, labels), I32),
+            pltpu.SemaphoreType.DMA((2 * PIECES + 1 + len(later),)),
         ],
         compiler_params=pltpu.CompilerParams(
             vmem_limit_bytes=(56 if after is None else 52) * 1024 * 1024
@@ -279,7 +294,31 @@
             bytes_accessed=4 * vocab_rows * width,
             transcendentals=0,
         ),
-    )(starts, near, far, *([] if after is None else [after]), *later)
+    )(me, *ids, near, far, *held, *later)
+
+
+def grad_kernel(errors_ref, docs_ref, out_ref):
+    out_ref[...] = lax.dot_general(
+        errors_ref[...], docs_ref[...], (((0,), (0,)), ((), ())), preferred_element_type=F32
+    ).astype(BF16)
+
+
+def rows_grad(errors, docs):
+    count, slab_rows = errors.shape
+    width = docs.shape[1]
+    step = 256 if slab_rows % 256 == 0 else slab_rows
+    return pl.pallas_call(
+        grad_kernel,
+        grid=(slab_rows // step,),
+        out_shape=jax.ShapeDtypeStruct((slab_rows, width), BF16),
+        in_specs=[
+            pl.BlockSpec((count, step), lambda i: (0, i)),
+            pl.BlockSpec((count, width), lambda i: (0, 0)),
+        ],
+        out_specs=pl.BlockSpec((step, width), lambda i: (i, 0)),
+        compiler_params=pltpu.CompilerParams(vmem_limit_bytes=16 * 1024 * 1024),
+        cost_estimate=pl.CostEstimate(flops=1, bytes_accessed=1, transcendentals=0),
+    )(errors, docs)
 
 
 def by_sums(
@@ -301,31 +340,20 @@
 
     other_table = swap_cores(token_table)
 
-    asked = {k: to_chip(label_tokens, k) for k in others}
-    asked[0] = label_tokens
+    ids = label_tokens.T
+    asked = {k: to_chip(ids, k) for k in others}
+    asked[0] = ids
 
     own_blocks = docs_block(docs, positives, ref_owner, ref_row, devices)
-    own_blocks, asked[1] = lax.optimization_barrier((own_blocks, asked[1]))
+    own_blocks, asked = lax.optimization_barrier((own_blocks, asked))
     all_blocks = exchange(own_blocks, ALL)
-
-    def starts(ks):
-        ids = jnp.concatenate([asked[k] for k in ks])
-        near = ids - me * vocab_rows
-        far = ids - (me ^ 1) * vocab_rows
-        row = jnp.where(
-            (near >= 0) & (near < vocab_rows),
-            near,
-            jnp.where((far >= 0) & (far < vocab_rows), far + vocab_rows, 2 * vocab_rows),
-        )
-        first = (row // SUBLANES) * (SUBLANES * (width // LANES)) + row % SUBLANES
-        return first.reshape(len(ks) * tokens)
 
     sent, after = [], None
     half = len(others) - len(others) // 3
     for ks in (others[:half], others[half:] + [0]):
         later = () if after is None else (free_rows, enc_weight)
         *terms, note = partial_means(
-            starts(ks), token_table, other_table, after, labels, length,
+            me.reshape(1), [asked[k] for k in ks], token_table, other_table, after,
             [BF16 if k else F32 for k in ks], later
         )
         if later:
@@ -392,9 +420,6 @@
     errors = (jax.nn.sigmoid(logits) - hits.astype(F32)).astype(BF16)
     doc_terms = jnp.dot(errors, head, preferred_element_type=F32)
     doc_terms = doc_terms.reshape(devices, own_docs, width)
-    free_grad = lax.dot_general(
-        errors, all_docs, (((0,), (0,)), ((), ())), preferred_element_type=F32
-    ).astype(BF16)
     doc_terms, late_errors = lax.optimization_barrier((doc_terms, errors))
     doc_parts = exchange(doc_terms, ALL)
     picked = lax.dot_general(
@@ -403,7 +428,8 @@
     picked = picked.reshape(chips, 2 * label_cap, all_count)
     arrived = {k: to_chip(picked[k], k) for k in others}
     returned = jnp.concatenate([picked[0]] + [arrived[k] for k in range(1, chips)])
-    returned, doc_parts = lax.optimization_barrier((returned, doc_parts))
+    free_grad = rows_grad(errors, all_docs)
+    returned, doc_parts, free_grad = lax.optimization_barrier((returned, doc_parts, free_grad))
     doc_grad = jnp.sum(doc_parts, axis=0)
     chip_errors = lax.dot_general(
         to_slots, returned, (((0,), (0,)), ((), ())), preferred_element_type=F32

time: 82.3 us -> 80.1 us (0.973)
  Pallas kernels: 19.6 us -> 22.5 us
  matrix products: 6.22 us -> 4.24 us
  local copies, waits for them, and re-layouts: 3.12 us -> 1.5 us
  starting transfers between devices: 28.7 us -> 27.3 us
  waiting for transfers between devices: 20.9 us -> 21.9 us
    pallas_call x2 -> x3, Pallas kernels: 18.1 us -> 21 us  [the longest x2 17.9 us: partial_means(): pl.pallas_call(functools.partial(sum_kernel, len(kinds), len(later), bool...]
    dot_general x1 -> x0, matrix products: 1.99 us -> none  [by_sums(): lax.dot_general(errors, all_docs, (((0,), (0,)), ((), ())), preferred_ele...]
    all_to_all x2, starting transfers between devices: 11 us -> 9.78 us  [exchange(): return lax.all_to_all(blocks, axes, split_axis=0, concat_axis=0, tiled=True)]
  transfers between devices with their start and end apart: 18 -> 18, of which waited for: 8 -> 10; matrix products, arithmetic and copies ran while one was open for 8% -> 3% of each run, Pallas kernels for 24% -> 28%
where the time goes in v7:
time: 80.1 us; the launch traced here: 79.6 us
  starting transfers between devices  27.3 us (34%)
  Pallas kernels  22.5 us (28%)
  waiting for transfers between devices  21.9 us (27%)
  matrix products  4.24 us (5%)
  local copies, waits for them, and re-layouts  1.5 us (2%)
  other arithmetic  1.36 us (2%)
  between operations  0.9 us (1%)
    ppermute x12, waiting for transfers between devices, to_chip(): lax.ppermute(x, 'shard', [(i, i ^ 2 * k) for i in range(lax.axis_size('sh...  19 us
    pallas_call x2, Pallas kernels, partial_means(): pl.pallas_call(functools.partial(sum_kernel, len(kinds), len(later), bool...  17.9 us
    ppermute x12, starting transfers between devices, to_chip(): lax.ppermute(x, 'shard', [(i, i ^ 2 * k) for i in range(lax.axis_size('sh...  16.1 us
    all_to_all x2, starting transfers between devices, exchange(): return lax.all_to_all(blocks, axes, split_axis=0, concat_axis=0, tiled=True)  9.78 us
    pallas_call x1, Pallas kernels, rows_grad(): pl.pallas_call(grad_kernel, grid=(slab_rows // step,), out_shape=jax.Shap...  3.11 us
  transfers between devices with their start and end apart: 18, of which 10 were waited for; matrix products, arithmetic and copies ran while one was open for 3% of the time, Pallas kernels for 28%

profile of v7, /device:TPU:1, one launch (start us, length us, event | category | flops | bytes accessed | tf_op | source)
XLA Modules:
  0.0 79.6 jit_solution(18410556754840670262)
XLA Ops:
  0.6 0.1 collective-permute-start.3
  0.8 2.8 %collective-permute-start = (s32[8,128]{1,0:T(8,128)}, s32[8,128]{1,0:T(8,128)S(1)}, u32[]{:S(2)}, u32[]{:S(2)}) collective-permute-start(s32[8,128]{1,0:T(8,128)} %bitcast.31), channel_id=1, source_target_pairs={{0,2},{1,3},{2,0},{3,1},{4,6},{5,7},{6,4},{7,5},{8,10},{9,11},{10,... | collective-permute-start | bytes 12296 | tf_op jit(solution)/shard_map/ppermute | solution.py:52
  3.5 2.3 %collective-permute-start.1 = (s32[8,128]{1,0:T(8,128)}, s32[8,128]{1,0:T(8,128)S(1)}, u32[]{:S(2)}, u32[]{:S(2)}) collective-permute-start(s32[8,128]{1,0:T(8,128)} %bitcast.32), channel_id=1, source_target_pairs={{0,4},{1,5},{2,6},{3,7},{4,0},{5,1},{6,2},{7,3},{8,12},{9,13},{10,... | collective-permute-start | bytes 12296 | tf_op jit(solution)/shard_map/ppermute | solution.py:52
  5.8 1.4 %shard_map.112 = bf16[32,2,1408]{2,1,0:T(2,128)(2,1)} custom-call(bf16[2,768]{1,0:T(2,128)(2,1)} %docs_ref.1, s32[2,5]{1,0:T(2,128)} %positives_ref.1, s32[1,128]{1,0:T(1,128)} %bitcast.39, s32[1,128]{1,0:T(1,128)} %bitcast.40), custom_call_target="tpu_custom_call" | custom-call | tf_op jit(solution)/shard_map/pallas_call | solution.py:257
  7.3 3.0 %collective-permute-done.2.refs_0_ = s32[8,128]{1,0:T(8,128)S(1)} collective-permute-done((s32[8,128]{1,0:T(8,128)}, s32[8,128]{1,0:T(8,128)S(1)}, u32[]{:S(2)}, u32[]{:S(2)}) %collective-permute-start.2) | collective-permute-done | bytes 4128 | tf_op jit(solution)/shard_map/ppermute | solution.py:52
  10.3 4.3 %all-to-all-start = ((bf16[32,2,1408]{2,1,0:T(2,128)(2,1)}), bf16[32,2,1408]{2,1,0:T(2,128)(2,1)S(1)}, u32[]{:S(2)}, u32[]{:S(2)}) async-start(bf16[32,2,1408]{2,1,0:T(2,128)(2,1)} %shard_map.112), calls=%async_computation | async-start | bytes 360448 | tf_op jit(solution)/shard_map/all_to_all | solution.py:16
  14.7 9.1 %shard_map.113 = (bf16[128,768]{1,0:T(8,128)(2,1)}, bf16[128,768]{1,0:T(8,128)(2,1)}, f32[8,128]{1,0:T(8,128)}) custom-call(s32[1]{0:T(128)} %bitcast.3.me_ref, s32[8,128]{1,0:T(8,128)} %copy-done.2, s32[8,128]{1,0:T(8,128)} %copy-done.1, bf16[3840,768]{1,0:T(8,128)(2,1)} %refs_2_.3, bf16[3840,768]{1,0:T(8,128)(2,1)} %collective-permute-done.3.refs_3_), custom_call_target="tpu_custom_call" | custom-call | flops 1572864 | bytes 11796480 | tf_op jit(solution)/shard_map/pallas_call | solution.py:270
  23.8 0.3 collective-permute-start.4
  24.1 2.4 %collective-permute-start.6 = (bf16[128,768]{1,0:T(8,128)(2,1)}, bf16[128,768]{1,0:T(8,128)(2,1)S(1)}, u32[]{:S(2)}, u32[]{:S(2)}) collective-permute-start(bf16[128,768]{1,0:T(8,128)(2,1)} %get-tuple-element.33), channel_id=1, source_target_pairs={{0,4},{1,5},{2,6},{3,7},{4,0},{5,1},{6,2},{7,3},{8,12},{9,13},{10,... | collective-permute-start | bytes 589832 | tf_op jit(solution)/shard_map/ppermute | solution.py:52
  26.5 1.2 %collective-permute-start.5 = (bf16[128,768]{1,0:T(8,128)(2,1)}, bf16[128,768]{1,0:T(8,128)(2,1)S(1)}, u32[]{:S(2)}, u32[]{:S(2)}) collective-permute-start(bf16[128,768]{1,0:T(8,128)(2,1)} %get-tuple-element.32), channel_id=1, source_target_pairs={{0,6},{1,7},{2,4},{3,5},{4,2},{5,3},{6,0},{7,1},{8,14},{9,15},{10,... | collective-permute-start | bytes 589832 | tf_op jit(solution)/shard_map/ppermute | solution.py:52
  27.7 8.9 %shard_map.114 = (bf16[128,768]{1,0:T(8,128)(2,1)S(1)}, f32[128,768]{1,0:T(8,128)S(1)}, bf16[1280,768]{1,0:T(8,128)(2,1)}, bf16[768,768]{1,0:T(8,128)(2,1)S(1)}, f32[8,128]{1,0:T(8,128)}) custom-call(s32[1]{0:T(128)} %bitcast.3.me_ref, s32[8,128]{1,0:T(8,128)S(1)} %collective-permute-done.refs_0_, s32[8,128]{1,0:T(8,128)S(1)} %bitcast.34, ...), custom_call_target="tpu_custom_call" | custom-call | flops 1572864 | bytes 11796480 | tf_op jit(solution)/shard_map/pallas_call | solution.py:270
  36.6 0.1 fusion.8
  36.8 0.1 collective-permute-start.7
  36.9 0.1 add_select_fusion.1
  37.0 0.1 bitcast_select_fusion
  37.1 0.2 select_reduce_fusion
  37.4 2.6 %collective-permute-done.6 = bf16[128,768]{1,0:T(8,128)(2,1)S(1)} collective-permute-done((bf16[128,768]{1,0:T(8,128)(2,1)}, bf16[128,768]{1,0:T(8,128)(2,1)S(1)}, u32[]{:S(2)}, u32[]{:S(2)}) %collective-permute-start.6) | collective-permute-done | bytes 196640 | tf_op jit(solution)/shard_map/ppermute | solution.py:52
  40.0 4.4 %collective-permute-done.7 = bf16[128,768]{1,0:T(8,128)(2,1)S(1)} collective-permute-done((bf16[128,768]{1,0:T(8,128)(2,1)S(1)}, bf16[128,768]{1,0:T(8,128)(2,1)S(1)}, u32[]{:S(2)}, u32[]{:S(2)}) %collective-permute-start.7) | collective-permute-done | bytes 196640 | tf_op jit(solution)/shard_map/ppermute | solution.py:52
  44.4 0.4 multiply_reduce_fusion
  44.8 0.1 multiply_convert_fusion
  45.0 0.9 %collective-permute-start.8 = (bf16[128,768]{1,0:T(8,128)(2,1)S(1)}, bf16[128,768]{1,0:T(8,128)(2,1)S(1)}, u32[]{:S(2)}, u32[]{:S(2)}) collective-permute-start(bf16[128,768]{1,0:T(8,128)(2,1)S(1)} %multiply_convert_fusion), channel_id=1, source_target_pairs={{0,1},{1,0},{2,3},{3,2},{4,5},{5,4},{6,7},{7,6},{8,9},{9,8},{10,11... | collective-permute-start | bytes 589832 | tf_op jit(solution)/shard_map/ppermute | solution.py:48
  45.9 0.1 fusion.39
  46.0 1.0 %collective-permute-done.8 = bf16[128,768]{1,0:T(8,128)(2,1)S(1)} collective-permute-done((bf16[128,768]{1,0:T(8,128)(2,1)S(1)}, bf16[128,768]{1,0:T(8,128)(2,1)S(1)}, u32[]{:S(2)}, u32[]{:S(2)}) %collective-permute-start.8) | collective-permute-done | bytes 196640 | tf_op jit(solution)/shard_map/ppermute | solution.py:48
  46.9 0.3 convolution_convert_fusion
  47.2 3.3 %collective-permute-start.11 = (bf16[64,768]{1,0:T(8,128)(2,1)S(1)}, bf16[64,768]{1,0:T(8,128)(2,1)S(1)}, u32[]{:S(2)}, u32[]{:S(2)}) collective-permute-start(bf16[64,768]{1,0:T(8,128)(2,1)S(1)} %get-tuple-element.42), channel_id=1, source_target_pairs={{0,6},{1,7},{2,4},{3,5},{4,2},{5,3},{6,0},{7,1},{8,14},{9,15},{10,... | collective-permute-start | bytes 294920 | tf_op jit(solution)/shard_map/ppermute | solution.py:52
  50.6 0.4 collective-permute-start.9
  51.1 0.1 copy.36
  51.1 0.1 copy.35
  51.4 1.8 %collective-permute-done.11 = bf16[64,768]{1,0:T(8,128)(2,1)S(1)} collective-permute-done((bf16[64,768]{1,0:T(8,128)(2,1)S(1)}, bf16[64,768]{1,0:T(8,128)(2,1)S(1)}, u32[]{:S(2)}, u32[]{:S(2)}) %collective-permute-start.11) | collective-permute-done | bytes 98336 | tf_op jit(solution)/shard_map/ppermute | solution.py:52
  53.2 5.7 %collective-permute-done.10 = bf16[64,768]{1,0:T(8,128)(2,1)S(1)} collective-permute-done((bf16[64,768]{1,0:T(8,128)(2,1)S(1)}, bf16[64,768]{1,0:T(8,128)(2,1)S(1)}, u32[]{:S(2)}, u32[]{:S(2)}) %collective-permute-start.10) | collective-permute-done | bytes 98336 | tf_op jit(solution)/shard_map/ppermute | solution.py:52
  58.9 0.7 add_convert_fusion
  59.6 0.8 fusion.4.errors_ref
  60.4 0.5 fusion.41
  60.9 0.8 reshape.150
  61.7 5.5 %all-to-all-start.1 = ((f32[32,2,768]{2,1,0:T(2,128)}), f32[32,2,768]{2,1,0:T(2,128)S(1)}, u32[]{:S(2)}, u32[]{:S(2)}) async-start(f32[32,2,768]{2,1,0:T(2,128)} %reshape.150), calls=%async_computation.1 | async-start | bytes 393216 | tf_op jit(solution)/shard_map/all_to_all | solution.py:16
  67.1 0.3 fusion.7
  67.5 0.1 fusion.38
  67.6 3.2 %collective-permute-start.14 = (bf16[64,64]{0,1:T(8,128)(2,1)S(1)}, bf16[64,64]{0,1:T(8,128)(2,1)S(1)}, u32[]{:S(2)}, u32[]{:S(2)}) collective-permute-start(bf16[64,64]{0,1:T(8,128)(2,1)S(1)} %get-tuple-element.46), channel_id=1, source_target_pairs={{0,6},{1,7},{2,4},{3,5},{4,2},{5,3},{6,0},{7,1},{8,14},{9,15},{10,... | collective-permute-start | bytes 24584 | tf_op jit(solution)/shard_map/ppermute | solution.py:52
  70.8 0.4 collective-permute-start.12
  71.2 3.1 %shard_map.115 = bf16[1280,768]{1,0:T(8,128)(2,1)} custom-call(bf16[64,1280]{1,0:T(8,128)(2,1)S(1)} %fusion.4.errors_ref, bf16[64,768]{1,0:T(8,128)(2,1)S(1)} %reshape.149.docs_ref), custom_call_target="tpu_custom_call" | custom-call | flops 1 | bytes 1 | tf_op jit(solution)/shard_map/pallas_call | solution.py:310
  74.3 0.3 collective-permute-done.14
  74.6 1.2 %collective-permute-done.13 = bf16[64,64]{0,1:T(8,128)(2,1)S(1)} collective-permute-done((bf16[64,64]{0,1:T(8,128)(2,1)S(1)}, bf16[64,64]{0,1:T(8,128)(2,1)S(1)}, u32[]{:S(2)}, u32[]{:S(2)}) %collective-permute-start.13) | collective-permute-done | bytes 8224 | tf_op jit(solution)/shard_map/ppermute | solution.py:52
  75.7 0.1 pad_maximum_fusion
  75.8 1.5 %all-to-all-done.1 = f32[32,2,768]{2,1,0:T(2,128)S(1)} async-done(((f32[32,2,768]{2,1,0:T(2,128)}), f32[32,2,768]{2,1,0:T(2,128)S(1)}, u32[]{:S(2)}, u32[]{:S(2)}) %all-to-all-start.1) | async-done | bytes 196640 | tf_op jit(solution)/shard_map/all_to_all | solution.py:16
  77.3 0.2 convolution_convert_fusion.2
  77.5 0.7 reduce_sum.39
  78.2 0.5 collective-permute-done.15
  78.7 0.9 %convolution_convert_fusion.1 = bf16[128,768]{1,0:T(8,128)(2,1)} fusion(bf16[64,768]{1,0:T(8,128)(2,1)S(1)} %reshape.149.docs_ref, bf16[128,64]{0,1:T(8,128)(2,1)S(1)} %collective-permute-done.15, bf16[256,64]{0,1:T(8,128)(2,1)S(1)} %convolution_convert_fusion.2), kind=kOutput, calls=%fused_computation.11 | convolution fusion | flops 12689408 | bytes 327680 | tf_op jit(solution)/shard_map/dot_general | solution.py:438
  (39 shorter events, 0.6 us)
Async XLA Ops:
  0.6 14.0 %collective-permute-start.3 = (bf16[3840,768]{1,0:T(8,128)(2,1)}, bf16[3840,768]{1,0:T(8,128)(2,1)}, u32[]{:S(2)}, u32[]{:S(2)}) collective-permute-start(bf16[3840,768]{1,0:T(8,128)(2,1)} %refs_2_.3), channel_id=1, source_target_pairs={{0,1},{1,0},{2,3},{3,2},{4,5},{5,4},{6,7},{7,6},{8,9},{9,8},{10,11... | collective-permute-start | bytes 17694728 | tf_op jit(solution)/shard_map/ppermute | solution.py:48
  0.8 6.5 %collective-permute-start = (s32[8,128]{1,0:T(8,128)}, s32[8,128]{1,0:T(8,128)S(1)}, u32[]{:S(2)}, u32[]{:S(2)}) collective-permute-start(s32[8,128]{1,0:T(8,128)} %bitcast.31), channel_id=1, source_target_pairs={{0,2},{1,3},{2,0},{3,1},{4,6},{5,7},{6,4},{7,5},{8,10},{9,11},{10,... | collective-permute-start | bytes 12296 | tf_op jit(solution)/shard_map/ppermute | solution.py:52
  3.5 3.8 %collective-permute-start.1 = (s32[8,128]{1,0:T(8,128)}, s32[8,128]{1,0:T(8,128)S(1)}, u32[]{:S(2)}, u32[]{:S(2)}) collective-permute-start(s32[8,128]{1,0:T(8,128)} %bitcast.32), channel_id=1, source_target_pairs={{0,4},{1,5},{2,6},{3,7},{4,0},{5,1},{6,2},{7,3},{8,12},{9,13},{10,... | collective-permute-start | bytes 12296 | tf_op jit(solution)/shard_map/ppermute | solution.py:52
  5.8 4.5 %collective-permute-start.2 = (s32[8,128]{1,0:T(8,128)}, s32[8,128]{1,0:T(8,128)S(1)}, u32[]{:S(2)}, u32[]{:S(2)}) collective-permute-start(s32[8,128]{1,0:T(8,128)} %bitcast.33), channel_id=1, source_target_pairs={{0,6},{1,7},{2,4},{3,5},{4,2},{5,3},{6,0},{7,1},{8,14},{9,15},{10,... | collective-permute-start | bytes 12296 | tf_op jit(solution)/shard_map/ppermute | solution.py:52
  7.3 7.4 %copy-start.1 = (s32[8,128]{1,0:T(8,128)}, s32[8,128]{1,0:T(8,128)S(1)}, u32[]{:S(2)}) copy-start(s32[8,128]{1,0:T(8,128)S(1)} %collective-permute-done.1.refs_1_) | copy-start | bytes 12292
  10.3 4.4 %copy-start.2 = (s32[8,128]{1,0:T(8,128)}, s32[8,128]{1,0:T(8,128)S(1)}, u32[]{:S(2)}) copy-start(s32[8,128]{1,0:T(8,128)S(1)} %collective-permute-done.2.refs_0_) | copy-start | bytes 12292
  10.3 26.3 %all-to-all-start = ((bf16[32,2,1408]{2,1,0:T(2,128)(2,1)}), bf16[32,2,1408]{2,1,0:T(2,128)(2,1)S(1)}, u32[]{:S(2)}, u32[]{:S(2)}) async-start(bf16[32,2,1408]{2,1,0:T(2,128)(2,1)} %shard_map.112), calls=%async_computation | async-start | bytes 360448 | tf_op jit(solution)/shard_map/all_to_all | solution.py:16
  14.7 13.0 %copy-start = (s32[128,8]{0,1:T(8,128)S(1)}, s32[128,8]{0,1:T(8,128)}, u32[]{:S(2)}) copy-start(s32[128,8]{0,1:T(8,128)} %param.12) | copy-start | bytes 12292
  23.8 3.9 %collective-permute-start.4 = (f32[8,128]{1,0:T(8,128)}, f32[8,128]{1,0:T(8,128)S(1)}, u32[]{:S(2)}, u32[]{:S(2)}) collective-permute-start(f32[8,128]{1,0:T(8,128)} %get-tuple-element.27), channel_id=1, source_target_pairs={{0,1},{1,0},{2,3},{3,2},{4,5},{5,4},{6,7},{7,6},{8,9},{9,8},{10,11... | collective-permute-start | bytes 12296 | tf_op jit(solution)/shard_map/ppermute | solution.py:48
  24.1 15.9 %collective-permute-start.6 = (bf16[128,768]{1,0:T(8,128)(2,1)}, bf16[128,768]{1,0:T(8,128)(2,1)S(1)}, u32[]{:S(2)}, u32[]{:S(2)}) collective-permute-start(bf16[128,768]{1,0:T(8,128)(2,1)} %get-tuple-element.33), channel_id=1, source_target_pairs={{0,4},{1,5},{2,6},{3,7},{4,0},{5,1},{6,2},{7,3},{8,12},{9,13},{10,... | collective-permute-start | bytes 589832 | tf_op jit(solution)/shard_map/ppermute | solution.py:52
  26.5 13.5 %collective-permute-start.5 = (bf16[128,768]{1,0:T(8,128)(2,1)}, bf16[128,768]{1,0:T(8,128)(2,1)S(1)}, u32[]{:S(2)}, u32[]{:S(2)}) collective-permute-start(bf16[128,768]{1,0:T(8,128)(2,1)} %get-tuple-element.32), channel_id=1, source_target_pairs={{0,6},{1,7},{2,4},{3,5},{4,2},{5,3},{6,0},{7,1},{8,14},{9,15},{10,... | collective-permute-start | bytes 589832 | tf_op jit(solution)/shard_map/ppermute | solution.py:52
  36.5 8.3 %copy-start.3 = (f32[768]{0:T(1024)S(1)}, f32[768]{0:T(1024)}, u32[]{:S(2)}) copy-start(f32[768]{0:T(1024)} %param.11) | copy-start | bytes 9220
  36.8 7.6 %collective-permute-start.7 = (bf16[128,768]{1,0:T(8,128)(2,1)S(1)}, bf16[128,768]{1,0:T(8,128)(2,1)S(1)}, u32[]{:S(2)}, u32[]{:S(2)}) collective-permute-start(bf16[128,768]{1,0:T(8,128)(2,1)S(1)} %get-tuple-element.34), channel_id=1, source_target_pairs={{0,2},{1,3},{2,0},{3,1},{4,6},{5,7},{6,4},{7,5},{8,10},{9,11},{10,... | collective-permute-start | bytes 589832 | tf_op jit(solution)/shard_map/ppermute | solution.py:52
  44.8 14.1 %copy-start.4 = (bf16[1280,768]{1,0:T(8,128)(2,1)S(1)}, bf16[1280,768]{1,0:T(8,128)(2,1)}, u32[]{:S(2)}) copy-start(bf16[1280,768]{1,0:T(8,128)(2,1)} %get-tuple-element.30) | copy-start | bytes 5898244
  45.0 2.0 %collective-permute-start.8 = (bf16[128,768]{1,0:T(8,128)(2,1)S(1)}, bf16[128,768]{1,0:T(8,128)(2,1)S(1)}, u32[]{:S(2)}, u32[]{:S(2)}) collective-permute-start(bf16[128,768]{1,0:T(8,128)(2,1)S(1)} %multiply_convert_fusion), channel_id=1, source_target_pairs={{0,1},{1,0},{2,3},{3,2},{4,5},{5,4},{6,7},{7,6},{8,9},{9,8},{10,11... | collective-permute-start | bytes 589832 | tf_op jit(solution)/shard_map/ppermute | solution.py:48
  47.2 5.9 %collective-permute-start.11 = (bf16[64,768]{1,0:T(8,128)(2,1)S(1)}, bf16[64,768]{1,0:T(8,128)(2,1)S(1)}, u32[]{:S(2)}, u32[]{:S(2)}) collective-permute-start(bf16[64,768]{1,0:T(8,128)(2,1)S(1)} %get-tuple-element.42), channel_id=1, source_target_pairs={{0,6},{1,7},{2,4},{3,5},{4,2},{5,3},{6,0},{7,1},{8,14},{9,15},{10,... | collective-permute-start | bytes 294920 | tf_op jit(solution)/shard_map/ppermute | solution.py:52
  50.6 8.3 %collective-permute-start.10 = (bf16[64,768]{1,0:T(8,128)(2,1)S(1)}, bf16[64,768]{1,0:T(8,128)(2,1)S(1)}, u32[]{:S(2)}, u32[]{:S(2)}) collective-permute-start(bf16[64,768]{1,0:T(8,128)(2,1)S(1)} %get-tuple-element.43), channel_id=1, source_target_pairs={{0,4},{1,5},{2,6},{3,7},{4,0},{5,1},{6,2},{7,3},{8,12},{9,13},{10,... | collective-permute-start | bytes 294920 | tf_op jit(solution)/shard_map/ppermute | solution.py:52
  50.6 8.3 %collective-permute-start.9 = (bf16[64,768]{1,0:T(8,128)(2,1)S(1)}, bf16[64,768]{1,0:T(8,128)(2,1)S(1)}, u32[]{:S(2)}, u32[]{:S(2)}) collective-permute-start(bf16[64,768]{1,0:T(8,128)(2,1)S(1)} %get-tuple-element.44), channel_id=1, source_target_pairs={{0,2},{1,3},{2,0},{3,1},{4,6},{5,7},{6,4},{7,5},{8,10},{9,11},{10,... | collective-permute-start | bytes 294920 | tf_op jit(solution)/shard_map/ppermute | solution.py:52
  61.7 15.6 %all-to-all-start.1 = ((f32[32,2,768]{2,1,0:T(2,128)}), f32[32,2,768]{2,1,0:T(2,128)S(1)}, u32[]{:S(2)}, u32[]{:S(2)}) async-start(f32[32,2,768]{2,1,0:T(2,128)} %reshape.150), calls=%async_computation.1 | async-start | bytes 393216 | tf_op jit(solution)/shard_map/all_to_all | solution.py:16
  67.6 7.0 %collective-permute-start.14 = (bf16[64,64]{0,1:T(8,128)(2,1)S(1)}, bf16[64,64]{0,1:T(8,128)(2,1)S(1)}, u32[]{:S(2)}, u32[]{:S(2)}) collective-permute-start(bf16[64,64]{0,1:T(8,128)(2,1)S(1)} %get-tuple-element.46), channel_id=1, source_target_pairs={{0,6},{1,7},{2,4},{3,5},{4,2},{5,3},{6,0},{7,1},{8,14},{9,15},{10,... | collective-permute-start | bytes 24584 | tf_op jit(solution)/shard_map/ppermute | solution.py:52
  70.8 4.9 %collective-permute-start.13 = (bf16[64,64]{0,1:T(8,128)(2,1)S(1)}, bf16[64,64]{0,1:T(8,128)(2,1)S(1)}, u32[]{:S(2)}, u32[]{:S(2)}) collective-permute-start(bf16[64,64]{0,1:T(8,128)(2,1)S(1)} %get-tuple-element.47), channel_id=1, source_target_pairs={{0,4},{1,5},{2,6},{3,7},{4,0},{5,1},{6,2},{7,3},{8,12},{9,13},{10,... | collective-permute-start | bytes 24584 | tf_op jit(solution)/shard_map/ppermute | solution.py:52
  70.8 4.9 %collective-permute-start.12 = (bf16[64,64]{0,1:T(8,128)(2,1)S(1)}, bf16[64,64]{0,1:T(8,128)(2,1)S(1)}, u32[]{:S(2)}, u32[]{:S(2)}) collective-permute-start(bf16[64,64]{0,1:T(8,128)(2,1)S(1)} %get-tuple-element.48), channel_id=1, source_target_pairs={{0,2},{1,3},{2,0},{3,1},{4,6},{5,7},{6,4},{7,5},{8,10},{9,11},{10,... | collective-permute-start | bytes 24584 | tf_op jit(solution)/shard_map/ppermute | solution.py:52
  77.5 1.2 %collective-permute-start.15 = (bf16[128,64]{0,1:T(8,128)(2,1)S(1)}, bf16[128,64]{0,1:T(8,128)(2,1)S(1)}, u32[]{:S(2)}, u32[]{:S(2)}) collective-permute-start(bf16[128,64]{0,1:T(8,128)(2,1)S(1)} %slice.117), channel_id=1, source_target_pairs={{0,1},{1,0},{2,3},{3,2},{4,5},{5,4},{6,7},{7,6},{8,9},{9,8},{10,11... | collective-permute-start | bytes 49160 | tf_op jit(solution)/shard_map/ppermute | solution.py:48

commit v8 on v7

--- a/solution.py
+++ b/solution.py
@@ -147,7 +147,7 @@
 
 LANES = 128
 SUBLANES = 8
-PIECES = 4
+PIECES = 8
 
 
 def sum_kernel(count, moved, held, me_ref, *refs):
@@ -191,7 +191,7 @@
     for at, copy in enumerate(copies):
         copy.wait()
 
-        @pl.loop(0, piece // 16, unroll=4)
+        @pl.loop(0, piece // 16, unroll=6)
         def _(group):
             first = pl.multiple_of(bases[at // PIECES] + at % PIECES * piece + group * 16, 16)
             block = stage[pl.ds(first, 16), :].astype(F32)
@@ -205,7 +205,7 @@
     place.wait()
     for n in range(count):
 
-        @pl.loop(0, labels // SUBLANES)
+        @pl.loop(0, labels // SUBLANES, unroll=4)
         def _(group):
             for q in range(SUBLANES):
                 label = group * SUBLANES + q

time: 80.1 us -> 79.7 us (level)
  transfers between devices with their start and end apart: 18 -> 18, of which waited for: 10 -> 10; matrix products, arithmetic and copies ran while one was open for 3% -> 3% of each run, Pallas kernels for 28% -> 27%
where the time goes in v8:
time: 79.7 us; the launch traced here: 79.2 us
  starting transfers between devices  27 us (34%)
  waiting for transfers between devices  22.5 us (28%)
  Pallas kernels  21.7 us (27%)
  matrix products  4.23 us (5%)
  local copies, waits for them, and re-layouts  1.5 us (2%)
  other arithmetic  1.36 us (2%)
  between operations  0.9 us (1%)
    ppermute x12, waiting for transfers between devices, to_chip(): lax.ppermute(x, 'shard', [(i, i ^ 2 * k) for i in range(lax.axis_size('sh...  19.6 us
    pallas_call x2, Pallas kernels, partial_means(): pl.pallas_call(functools.partial(sum_kernel, len(kinds), len(later), bool...  17.1 us
    ppermute x12, starting transfers between devices, to_chip(): lax.ppermute(x, 'shard', [(i, i ^ 2 * k) for i in range(lax.axis_size('sh...  16.1 us
    all_to_all x2, starting transfers between devices, exchange(): return lax.all_to_all(blocks, axes, split_axis=0, concat_axis=0, tiled=True)  9.79 us
    pallas_call x1, Pallas kernels, rows_grad(): pl.pallas_call(grad_kernel, grid=(slab_rows // step,), out_shape=jax.Shap...  3.11 us
  transfers between devices with their start and end apart: 18, of which 10 were waited for; matrix products, arithmetic and copies ran while one was open for 3% of the time, Pallas kernels for 27%

profile of v8, /device:TPU:1, one launch (start us, length us, event | category | flops | bytes accessed | tf_op | source)
XLA Modules:
  0.0 79.2 jit_solution(8325329596005348070)
XLA Ops:
  0.6 0.1 collective-permute-start.3
  0.8 2.8 %collective-permute-start = (s32[8,128]{1,0:T(8,128)}, s32[8,128]{1,0:T(8,128)S(1)}, u32[]{:S(2)}, u32[]{:S(2)}) collective-permute-start(s32[8,128]{1,0:T(8,128)} %bitcast.31), channel_id=1, source_target_pairs={{0,2},{1,3},{2,0},{3,1},{4,6},{5,7},{6,4},{7,5},{8,10},{9,11},{10,... | collective-permute-start | bytes 12296 | tf_op jit(solution)/shard_map/ppermute | solution.py:52
  3.5 2.3 %collective-permute-start.1 = (s32[8,128]{1,0:T(8,128)}, s32[8,128]{1,0:T(8,128)S(1)}, u32[]{:S(2)}, u32[]{:S(2)}) collective-permute-start(s32[8,128]{1,0:T(8,128)} %bitcast.32), channel_id=1, source_target_pairs={{0,4},{1,5},{2,6},{3,7},{4,0},{5,1},{6,2},{7,3},{8,12},{9,13},{10,... | collective-permute-start | bytes 12296 | tf_op jit(solution)/shard_map/ppermute | solution.py:52
  5.8 1.4 %shard_map.112 = bf16[32,2,1408]{2,1,0:T(2,128)(2,1)} custom-call(bf16[2,768]{1,0:T(2,128)(2,1)} %docs_ref.1, s32[2,5]{1,0:T(2,128)} %positives_ref.1, s32[1,128]{1,0:T(1,128)} %bitcast.39, s32[1,128]{1,0:T(1,128)} %bitcast.40), custom_call_target="tpu_custom_call" | custom-call | tf_op jit(solution)/shard_map/pallas_call | solution.py:257
  7.3 3.0 %collective-permute-done.2.refs_0_ = s32[8,128]{1,0:T(8,128)S(1)} collective-permute-done((s32[8,128]{1,0:T(8,128)}, s32[8,128]{1,0:T(8,128)S(1)}, u32[]{:S(2)}, u32[]{:S(2)}) %collective-permute-start.2) | collective-permute-done | bytes 4128 | tf_op jit(solution)/shard_map/ppermute | solution.py:52
  10.3 4.3 %all-to-all-start = ((bf16[32,2,1408]{2,1,0:T(2,128)(2,1)}), bf16[32,2,1408]{2,1,0:T(2,128)(2,1)S(1)}, u32[]{:S(2)}, u32[]{:S(2)}) async-start(bf16[32,2,1408]{2,1,0:T(2,128)(2,1)} %shard_map.112), calls=%async_computation | async-start | bytes 360448 | tf_op jit(solution)/shard_map/all_to_all | solution.py:16
  14.7 8.7 %shard_map.113 = (bf16[128,768]{1,0:T(8,128)(2,1)}, bf16[128,768]{1,0:T(8,128)(2,1)}, f32[8,128]{1,0:T(8,128)}) custom-call(s32[1]{0:T(128)} %bitcast.3.me_ref, s32[8,128]{1,0:T(8,128)} %copy-done.2, s32[8,128]{1,0:T(8,128)} %copy-done.1, bf16[3840,768]{1,0:T(8,128)(2,1)} %refs_2_.3, bf16[3840,768]{1,0:T(8,128)(2,1)} %collective-permute-done.3.refs_3_), custom_call_target="tpu_custom_call" | custom-call | flops 1572864 | bytes 11796480 | tf_op jit(solution)/shard_map/pallas_call | solution.py:270
  23.4 0.3 collective-permute-start.4
  23.7 2.4 %collective-permute-start.6 = (bf16[128,768]{1,0:T(8,128)(2,1)}, bf16[128,768]{1,0:T(8,128)(2,1)S(1)}, u32[]{:S(2)}, u32[]{:S(2)}) collective-permute-start(bf16[128,768]{1,0:T(8,128)(2,1)} %get-tuple-element.33), channel_id=1, source_target_pairs={{0,4},{1,5},{2,6},{3,7},{4,0},{5,1},{6,2},{7,3},{8,12},{9,13},{10,... | collective-permute-start | bytes 589832 | tf_op jit(solution)/shard_map/ppermute | solution.py:52
  26.1 1.2 %collective-permute-start.5 = (bf16[128,768]{1,0:T(8,128)(2,1)}, bf16[128,768]{1,0:T(8,128)(2,1)S(1)}, u32[]{:S(2)}, u32[]{:S(2)}) collective-permute-start(bf16[128,768]{1,0:T(8,128)(2,1)} %get-tuple-element.32), channel_id=1, source_target_pairs={{0,6},{1,7},{2,4},{3,5},{4,2},{5,3},{6,0},{7,1},{8,14},{9,15},{10,... | collective-permute-start | bytes 589832 | tf_op jit(solution)/shard_map/ppermute | solution.py:52
  27.3 8.5 %shard_map.114 = (bf16[128,768]{1,0:T(8,128)(2,1)S(1)}, f32[128,768]{1,0:T(8,128)S(1)}, bf16[1280,768]{1,0:T(8,128)(2,1)}, bf16[768,768]{1,0:T(8,128)(2,1)S(1)}, f32[8,128]{1,0:T(8,128)}) custom-call(s32[1]{0:T(128)} %bitcast.3.me_ref, s32[8,128]{1,0:T(8,128)S(1)} %collective-permute-done.refs_0_, s32[8,128]{1,0:T(8,128)S(1)} %bitcast.34, ...), custom_call_target="tpu_custom_call" | custom-call | flops 1572864 | bytes 11796480 | tf_op jit(solution)/shard_map/pallas_call | solution.py:270
  35.8 0.1 fusion.8
  36.0 0.1 collective-permute-start.7
  36.1 0.1 add_select_fusion.1
  36.2 0.1 bitcast_select_fusion
  36.3 0.2 select_reduce_fusion
  36.6 3.0 %collective-permute-done.6 = bf16[128,768]{1,0:T(8,128)(2,1)S(1)} collective-permute-done((bf16[128,768]{1,0:T(8,128)(2,1)}, bf16[128,768]{1,0:T(8,128)(2,1)S(1)}, u32[]{:S(2)}, u32[]{:S(2)}) %collective-permute-start.6) | collective-permute-done | bytes 196640 | tf_op jit(solution)/shard_map/ppermute | solution.py:52
  39.5 4.6 %collective-permute-done.7 = bf16[128,768]{1,0:T(8,128)(2,1)S(1)} collective-permute-done((bf16[128,768]{1,0:T(8,128)(2,1)S(1)}, bf16[128,768]{1,0:T(8,128)(2,1)S(1)}, u32[]{:S(2)}, u32[]{:S(2)}) %collective-permute-start.7) | collective-permute-done | bytes 196640 | tf_op jit(solution)/shard_map/ppermute | solution.py:52
  44.2 0.4 multiply_reduce_fusion
  44.7 0.1 multiply_convert_fusion
  44.8 0.7 collective-permute-start.8
  45.5 0.1 fusion.39
  45.5 1.0 %collective-permute-done.8 = bf16[128,768]{1,0:T(8,128)(2,1)S(1)} collective-permute-done((bf16[128,768]{1,0:T(8,128)(2,1)S(1)}, bf16[128,768]{1,0:T(8,128)(2,1)S(1)}, u32[]{:S(2)}, u32[]{:S(2)}) %collective-permute-start.8) | collective-permute-done | bytes 196640 | tf_op jit(solution)/shard_map/ppermute | solution.py:48
  46.5 0.3 convolution_convert_fusion
  46.8 3.3 %collective-permute-start.11 = (bf16[64,768]{1,0:T(8,128)(2,1)S(1)}, bf16[64,768]{1,0:T(8,128)(2,1)S(1)}, u32[]{:S(2)}, u32[]{:S(2)}) collective-permute-start(bf16[64,768]{1,0:T(8,128)(2,1)S(1)} %get-tuple-element.42), channel_id=1, source_target_pairs={{0,6},{1,7},{2,4},{3,5},{4,2},{5,3},{6,0},{7,1},{8,14},{9,15},{10,... | collective-permute-start | bytes 294920 | tf_op jit(solution)/shard_map/ppermute | solution.py:52
  50.2 0.4 collective-permute-start.9
  50.6 0.1 copy.36
  50.7 0.1 copy.35
  51.0 1.8 %collective-permute-done.11 = bf16[64,768]{1,0:T(8,128)(2,1)S(1)} collective-permute-done((bf16[64,768]{1,0:T(8,128)(2,1)S(1)}, bf16[64,768]{1,0:T(8,128)(2,1)S(1)}, u32[]{:S(2)}, u32[]{:S(2)}) %collective-permute-start.11) | collective-permute-done | bytes 98336 | tf_op jit(solution)/shard_map/ppermute | solution.py:52
  52.8 5.7 %collective-permute-done.10 = bf16[64,768]{1,0:T(8,128)(2,1)S(1)} collective-permute-done((bf16[64,768]{1,0:T(8,128)(2,1)S(1)}, bf16[64,768]{1,0:T(8,128)(2,1)S(1)}, u32[]{:S(2)}, u32[]{:S(2)}) %collective-permute-start.10) | collective-permute-done | bytes 98336 | tf_op jit(solution)/shard_map/ppermute | solution.py:52
  58.5 0.7 add_convert_fusion
  59.2 0.8 fusion.4.errors_ref
  60.0 0.5 fusion.41
  60.5 0.8 %reshape.150 = f32[32,2,768]{2,1,0:T(2,128)} reshape(f32[64,768]{1,0:T(8,128)S(1)} %fusion.41) | data formatting | bytes 393216 | tf_op jit(solution)/shard_map/reshape | solution.py:422
  61.3 5.5 %all-to-all-start.1 = ((f32[32,2,768]{2,1,0:T(2,128)}), f32[32,2,768]{2,1,0:T(2,128)S(1)}, u32[]{:S(2)}, u32[]{:S(2)}) async-start(f32[32,2,768]{2,1,0:T(2,128)} %reshape.150), calls=%async_computation.1 | async-start | bytes 393216 | tf_op jit(solution)/shard_map/all_to_all | solution.py:16
  66.7 0.3 fusion.7
  67.1 0.1 fusion.38
  67.2 3.3 %collective-permute-start.14 = (bf16[64,64]{0,1:T(8,128)(2,1)S(1)}, bf16[64,64]{0,1:T(8,128)(2,1)S(1)}, u32[]{:S(2)}, u32[]{:S(2)}) collective-permute-start(bf16[64,64]{0,1:T(8,128)(2,1)S(1)} %get-tuple-element.46), channel_id=1, source_target_pairs={{0,6},{1,7},{2,4},{3,5},{4,2},{5,3},{6,0},{7,1},{8,14},{9,15},{10,... | collective-permute-start | bytes 24584 | tf_op jit(solution)/shard_map/ppermute | solution.py:52
  70.4 0.4 collective-permute-start.12
  70.8 3.1 %shard_map.115 = bf16[1280,768]{1,0:T(8,128)(2,1)} custom-call(bf16[64,1280]{1,0:T(8,128)(2,1)S(1)} %fusion.4.errors_ref, bf16[64,768]{1,0:T(8,128)(2,1)S(1)} %reshape.149.docs_ref), custom_call_target="tpu_custom_call" | custom-call | flops 1 | bytes 1 | tf_op jit(solution)/shard_map/pallas_call | solution.py:310
  73.9 0.3 collective-permute-done.14
  74.2 1.2 %collective-permute-done.13 = bf16[64,64]{0,1:T(8,128)(2,1)S(1)} collective-permute-done((bf16[64,64]{0,1:T(8,128)(2,1)S(1)}, bf16[64,64]{0,1:T(8,128)(2,1)S(1)}, u32[]{:S(2)}, u32[]{:S(2)}) %collective-permute-start.13) | collective-permute-done | bytes 8224 | tf_op jit(solution)/shard_map/ppermute | solution.py:52
  75.3 0.1 pad_maximum_fusion
  75.4 1.5 %all-to-all-done.1 = f32[32,2,768]{2,1,0:T(2,128)S(1)} async-done(((f32[32,2,768]{2,1,0:T(2,128)}), f32[32,2,768]{2,1,0:T(2,128)S(1)}, u32[]{:S(2)}, u32[]{:S(2)}) %all-to-all-start.1) | async-done | bytes 196640 | tf_op jit(solution)/shard_map/all_to_all | solution.py:16
  76.9 0.2 convolution_convert_fusion.2
  77.1 0.7 reduce_sum.39
  77.8 0.5 collective-permute-done.15
  78.3 0.9 %convolution_convert_fusion.1 = bf16[128,768]{1,0:T(8,128)(2,1)} fusion(bf16[64,768]{1,0:T(8,128)(2,1)S(1)} %reshape.149.docs_ref, bf16[128,64]{0,1:T(8,128)(2,1)S(1)} %collective-permute-done.15, bf16[256,64]{0,1:T(8,128)(2,1)S(1)} %convolution_convert_fusion.2), kind=kOutput, calls=%fused_computation.11 | convolution fusion | flops 12689408 | bytes 327680 | tf_op jit(solution)/shard_map/dot_general | solution.py:438
  (39 shorter events, 0.6 us)
Async XLA Ops:
  0.6 14.0 %collective-permute-start.3 = (bf16[3840,768]{1,0:T(8,128)(2,1)}, bf16[3840,768]{1,0:T(8,128)(2,1)}, u32[]{:S(2)}, u32[]{:S(2)}) collective-permute-start(bf16[3840,768]{1,0:T(8,128)(2,1)} %refs_2_.3), channel_id=1, source_target_pairs={{0,1},{1,0},{2,3},{3,2},{4,5},{5,4},{6,7},{7,6},{8,9},{9,8},{10,11... | collective-permute-start | bytes 17694728 | tf_op jit(solution)/shard_map/ppermute | solution.py:48
  0.8 6.5 %collective-permute-start = (s32[8,128]{1,0:T(8,128)}, s32[8,128]{1,0:T(8,128)S(1)}, u32[]{:S(2)}, u32[]{:S(2)}) collective-permute-start(s32[8,128]{1,0:T(8,128)} %bitcast.31), channel_id=1, source_target_pairs={{0,2},{1,3},{2,0},{3,1},{4,6},{5,7},{6,4},{7,5},{8,10},{9,11},{10,... | collective-permute-start | bytes 12296 | tf_op jit(solution)/shard_map/ppermute | solution.py:52
  3.5 3.8 %collective-permute-start.1 = (s32[8,128]{1,0:T(8,128)}, s32[8,128]{1,0:T(8,128)S(1)}, u32[]{:S(2)}, u32[]{:S(2)}) collective-permute-start(s32[8,128]{1,0:T(8,128)} %bitcast.32), channel_id=1, source_target_pairs={{0,4},{1,5},{2,6},{3,7},{4,0},{5,1},{6,2},{7,3},{8,12},{9,13},{10,... | collective-permute-start | bytes 12296 | tf_op jit(solution)/shard_map/ppermute | solution.py:52
  5.8 4.5 %collective-permute-start.2 = (s32[8,128]{1,0:T(8,128)}, s32[8,128]{1,0:T(8,128)S(1)}, u32[]{:S(2)}, u32[]{:S(2)}) collective-permute-start(s32[8,128]{1,0:T(8,128)} %bitcast.33), channel_id=1, source_target_pairs={{0,6},{1,7},{2,4},{3,5},{4,2},{5,3},{6,0},{7,1},{8,14},{9,15},{10,... | collective-permute-start | bytes 12296 | tf_op jit(solution)/shard_map/ppermute | solution.py:52
  7.3 7.4 %copy-start.1 = (s32[8,128]{1,0:T(8,128)}, s32[8,128]{1,0:T(8,128)S(1)}, u32[]{:S(2)}) copy-start(s32[8,128]{1,0:T(8,128)S(1)} %collective-permute-done.1.refs_1_) | copy-start | bytes 12292
  10.3 4.4 %copy-start.2 = (s32[8,128]{1,0:T(8,128)}, s32[8,128]{1,0:T(8,128)S(1)}, u32[]{:S(2)}) copy-start(s32[8,128]{1,0:T(8,128)S(1)} %collective-permute-done.2.refs_0_) | copy-start | bytes 12292
  10.3 25.5 %all-to-all-start = ((bf16[32,2,1408]{2,1,0:T(2,128)(2,1)}), bf16[32,2,1408]{2,1,0:T(2,128)(2,1)S(1)}, u32[]{:S(2)}, u32[]{:S(2)}) async-start(bf16[32,2,1408]{2,1,0:T(2,128)(2,1)} %shard_map.112), calls=%async_computation | async-start | bytes 360448 | tf_op jit(solution)/shard_map/all_to_all | solution.py:16
  14.7 12.6 %copy-start = (s32[128,8]{0,1:T(8,128)S(1)}, s32[128,8]{0,1:T(8,128)}, u32[]{:S(2)}) copy-start(s32[128,8]{0,1:T(8,128)} %param.12) | copy-start | bytes 12292
  23.4 3.9 %collective-permute-start.4 = (f32[8,128]{1,0:T(8,128)}, f32[8,128]{1,0:T(8,128)S(1)}, u32[]{:S(2)}, u32[]{:S(2)}) collective-permute-start(f32[8,128]{1,0:T(8,128)} %get-tuple-element.27), channel_id=1, source_target_pairs={{0,1},{1,0},{2,3},{3,2},{4,5},{5,4},{6,7},{7,6},{8,9},{9,8},{10,11... | collective-permute-start | bytes 12296 | tf_op jit(solution)/shard_map/ppermute | solution.py:48
  23.7 15.9 %collective-permute-start.6 = (bf16[128,768]{1,0:T(8,128)(2,1)}, bf16[128,768]{1,0:T(8,128)(2,1)S(1)}, u32[]{:S(2)}, u32[]{:S(2)}) collective-permute-start(bf16[128,768]{1,0:T(8,128)(2,1)} %get-tuple-element.33), channel_id=1, source_target_pairs={{0,4},{1,5},{2,6},{3,7},{4,0},{5,1},{6,2},{7,3},{8,12},{9,13},{10,... | collective-permute-start | bytes 589832 | tf_op jit(solution)/shard_map/ppermute | solution.py:52
  26.1 13.5 %collective-permute-start.5 = (bf16[128,768]{1,0:T(8,128)(2,1)}, bf16[128,768]{1,0:T(8,128)(2,1)S(1)}, u32[]{:S(2)}, u32[]{:S(2)}) collective-permute-start(bf16[128,768]{1,0:T(8,128)(2,1)} %get-tuple-element.32), channel_id=1, source_target_pairs={{0,6},{1,7},{2,4},{3,5},{4,2},{5,3},{6,0},{7,1},{8,14},{9,15},{10,... | collective-permute-start | bytes 589832 | tf_op jit(solution)/shard_map/ppermute | solution.py:52
  35.7 8.9 %copy-start.3 = (f32[768]{0:T(1024)S(1)}, f32[768]{0:T(1024)}, u32[]{:S(2)}) copy-start(f32[768]{0:T(1024)} %param.11) | copy-start | bytes 9220
  36.0 8.2 %collective-permute-start.7 = (bf16[128,768]{1,0:T(8,128)(2,1)S(1)}, bf16[128,768]{1,0:T(8,128)(2,1)S(1)}, u32[]{:S(2)}, u32[]{:S(2)}) collective-permute-start(bf16[128,768]{1,0:T(8,128)(2,1)S(1)} %get-tuple-element.34), channel_id=1, source_target_pairs={{0,2},{1,3},{2,0},{3,1},{4,6},{5,7},{6,4},{7,5},{8,10},{9,11},{10,... | collective-permute-start | bytes 589832 | tf_op jit(solution)/shard_map/ppermute | solution.py:52
  44.6 13.9 %copy-start.4 = (bf16[1280,768]{1,0:T(8,128)(2,1)S(1)}, bf16[1280,768]{1,0:T(8,128)(2,1)}, u32[]{:S(2)}) copy-start(bf16[1280,768]{1,0:T(8,128)(2,1)} %get-tuple-element.30) | copy-start | bytes 5898244
  44.8 1.7 %collective-permute-start.8 = (bf16[128,768]{1,0:T(8,128)(2,1)S(1)}, bf16[128,768]{1,0:T(8,128)(2,1)S(1)}, u32[]{:S(2)}, u32[]{:S(2)}) collective-permute-start(bf16[128,768]{1,0:T(8,128)(2,1)S(1)} %multiply_convert_fusion), channel_id=1, source_target_pairs={{0,1},{1,0},{2,3},{3,2},{4,5},{5,4},{6,7},{7,6},{8,9},{9,8},{10,11... | collective-permute-start | bytes 589832 | tf_op jit(solution)/shard_map/ppermute | solution.py:48
  46.8 5.9 %collective-permute-start.11 = (bf16[64,768]{1,0:T(8,128)(2,1)S(1)}, bf16[64,768]{1,0:T(8,128)(2,1)S(1)}, u32[]{:S(2)}, u32[]{:S(2)}) collective-permute-start(bf16[64,768]{1,0:T(8,128)(2,1)S(1)} %get-tuple-element.42), channel_id=1, source_target_pairs={{0,6},{1,7},{2,4},{3,5},{4,2},{5,3},{6,0},{7,1},{8,14},{9,15},{10,... | collective-permute-start | bytes 294920 | tf_op jit(solution)/shard_map/ppermute | solution.py:52
  50.2 8.3 %collective-permute-start.10 = (bf16[64,768]{1,0:T(8,128)(2,1)S(1)}, bf16[64,768]{1,0:T(8,128)(2,1)S(1)}, u32[]{:S(2)}, u32[]{:S(2)}) collective-permute-start(bf16[64,768]{1,0:T(8,128)(2,1)S(1)} %get-tuple-element.43), channel_id=1, source_target_pairs={{0,4},{1,5},{2,6},{3,7},{4,0},{5,1},{6,2},{7,3},{8,12},{9,13},{10,... | collective-permute-start | bytes 294920 | tf_op jit(solution)/shard_map/ppermute | solution.py:52
  50.2 8.3 %collective-permute-start.9 = (bf16[64,768]{1,0:T(8,128)(2,1)S(1)}, bf16[64,768]{1,0:T(8,128)(2,1)S(1)}, u32[]{:S(2)}, u32[]{:S(2)}) collective-permute-start(bf16[64,768]{1,0:T(8,128)(2,1)S(1)} %get-tuple-element.44), channel_id=1, source_target_pairs={{0,2},{1,3},{2,0},{3,1},{4,6},{5,7},{6,4},{7,5},{8,10},{9,11},{10,... | collective-permute-start | bytes 294920 | tf_op jit(solution)/shard_map/ppermute | solution.py:52
  61.3 15.6 %all-to-all-start.1 = ((f32[32,2,768]{2,1,0:T(2,128)}), f32[32,2,768]{2,1,0:T(2,128)S(1)}, u32[]{:S(2)}, u32[]{:S(2)}) async-start(f32[32,2,768]{2,1,0:T(2,128)} %reshape.150), calls=%async_computation.1 | async-start | bytes 393216 | tf_op jit(solution)/shard_map/all_to_all | solution.py:16
  67.2 7.0 %collective-permute-start.14 = (bf16[64,64]{0,1:T(8,128)(2,1)S(1)}, bf16[64,64]{0,1:T(8,128)(2,1)S(1)}, u32[]{:S(2)}, u32[]{:S(2)}) collective-permute-start(bf16[64,64]{0,1:T(8,128)(2,1)S(1)} %get-tuple-element.46), channel_id=1, source_target_pairs={{0,6},{1,7},{2,4},{3,5},{4,2},{5,3},{6,0},{7,1},{8,14},{9,15},{10,... | collective-permute-start | bytes 24584 | tf_op jit(solution)/shard_map/ppermute | solution.py:52
  70.4 4.9 %collective-permute-start.13 = (bf16[64,64]{0,1:T(8,128)(2,1)S(1)}, bf16[64,64]{0,1:T(8,128)(2,1)S(1)}, u32[]{:S(2)}, u32[]{:S(2)}) collective-permute-start(bf16[64,64]{0,1:T(8,128)(2,1)S(1)} %get-tuple-element.47), channel_id=1, source_target_pairs={{0,4},{1,5},{2,6},{3,7},{4,0},{5,1},{6,2},{7,3},{8,12},{9,13},{10,... | collective-permute-start | bytes 24584 | tf_op jit(solution)/shard_map/ppermute | solution.py:52
  70.4 4.9 %collective-permute-start.12 = (bf16[64,64]{0,1:T(8,128)(2,1)S(1)}, bf16[64,64]{0,1:T(8,128)(2,1)S(1)}, u32[]{:S(2)}, u32[]{:S(2)}) collective-permute-start(bf16[64,64]{0,1:T(8,128)(2,1)S(1)} %get-tuple-element.48), channel_id=1, source_target_pairs={{0,2},{1,3},{2,0},{3,1},{4,6},{5,7},{6,4},{7,5},{8,10},{9,11},{10,... | collective-permute-start | bytes 24584 | tf_op jit(solution)/shard_map/ppermute | solution.py:52
  77.1 1.2 %collective-permute-start.15 = (bf16[128,64]{0,1:T(8,128)(2,1)S(1)}, bf16[128,64]{0,1:T(8,128)(2,1)S(1)}, u32[]{:S(2)}, u32[]{:S(2)}) collective-permute-start(bf16[128,64]{0,1:T(8,128)(2,1)S(1)} %slice.117), channel_id=1, source_target_pairs={{0,1},{1,0},{2,3},{3,2},{4,5},{5,4},{6,7},{7,6},{8,9},{9,8},{10,11... | collective-permute-start | bytes 49160 | tf_op jit(solution)/shard_map/ppermute | solution.py:48

commit v9 on v8

--- a/solution.py
+++ b/solution.py
@@ -147,7 +147,7 @@
 
 LANES = 128
 SUBLANES = 8
-PIECES = 8
+PIECES = 12
 
 
 def sum_kernel(count, moved, held, me_ref, *refs):
@@ -191,7 +191,7 @@
     for at, copy in enumerate(copies):
         copy.wait()
 
-        @pl.loop(0, piece // 16, unroll=6)
+        @pl.loop(0, piece // 16, unroll=5)
         def _(group):
             first = pl.multiple_of(bases[at // PIECES] + at % PIECES * piece + group * 16, 16)
             block = stage[pl.ds(first, 16), :].astype(F32)
@@ -205,7 +205,7 @@
     place.wait()
     for n in range(count):
 
-        @pl.loop(0, labels // SUBLANES, unroll=4)
+        @pl.loop(0, labels // SUBLANES, unroll=8)
         def _(group):
             for q in range(SUBLANES):
                 label = group * SUBLANES + q
@@ -297,6 +297,23 @@
     )(me, *ids, near, far, *held, *later)
 
 
+def terms_kernel(errors_ref, head_ref, out_ref):
+    terms = jnp.dot(errors_ref[...], head_ref[...], preferred_element_type=F32)
+    devices, own_docs, _ = out_ref.shape
+    for d in range(devices):
+        out_ref[d, :, :] = terms[d * own_docs : (d + 1) * own_docs, :]
+
+
+def terms_by_device(errors, head, devices):
+    return pl.pallas_call(
+        terms_kernel,
+        out_shape=jax.ShapeDtypeStruct((devices, errors.shape[0] // devices, head.shape[1]), F32),
+        in_specs=[pl.BlockSpec(memory_space=pltpu.VMEM)] * 2,
+        out_specs=pl.BlockSpec(memory_space=pltpu.VMEM),
+        compiler_params=pltpu.CompilerParams(vmem_limit_bytes=16 * 1024 * 1024),
+    )(errors, head)
+
+
 def grad_kernel(errors_ref, docs_ref, out_ref):
     out_ref[...] = lax.dot_general(
         errors_ref[...], docs_ref[...], (((0,), (0,)), ((), ())), preferred_element_type=F32
@@ -418,8 +435,7 @@
     for column in range(pos_count):
         hits = hits | (all_positives[:, column : column + 1] == label_columns[None, :])
     errors = (jax.nn.sigmoid(logits) - hits.astype(F32)).astype(BF16)
-    doc_terms = jnp.dot(errors, head, preferred_element_type=F32)
-    doc_terms = doc_terms.reshape(devices, own_docs, width)
+    doc_terms = terms_by_device(errors, head, devices)
     doc_terms, late_errors = lax.optimization_barrier((doc_terms, errors))
     doc_parts = exchange(doc_terms, ALL)
     picked = lax.dot_general(

time: 79.7 us -> 79.5 us (level)
  Pallas kernels: 21.7 us -> 22.8 us
    pallas_call x0 -> x1, Pallas kernels: none -> 1.16 us  [terms_by_device(): pl.pallas_call(terms_kernel, out_shape=jax.ShapeDtypeStruct((devices, err...]
where the time goes in v9:
time: 79.5 us; the launch traced here: 79.1 us
  starting transfers between devices  27 us (34%)
  Pallas kernels  22.8 us (29%)
  waiting for transfers between devices  22.6 us (28%)
  matrix products  3.77 us (5%)
  other arithmetic  1.36 us (2%)
  between operations  0.9 us (1%)
    ppermute x12, waiting for transfers between devices, to_chip(): lax.ppermute(x, 'shard', [(i, i ^ 2 * k) for i in range(lax.axis_size('sh...  19.6 us
    pallas_call x2, Pallas kernels, partial_means(): pl.pallas_call(functools.partial(sum_kernel, len(kinds), len(later), bool...  17.1 us
    ppermute x12, starting transfers between devices, to_chip(): lax.ppermute(x, 'shard', [(i, i ^ 2 * k) for i in range(lax.axis_size('sh...  16.1 us
    all_to_all x2, starting transfers between devices, exchange(): return lax.all_to_all(blocks, axes, split_axis=0, concat_axis=0, tiled=True)  9.79 us
    pallas_call x1, Pallas kernels, rows_grad(): pl.pallas_call(grad_kernel, grid=(slab_rows // step,), out_shape=jax.Shap...  3.11 us
  transfers between devices with their start and end apart: 18, of which 10 were waited for; matrix products, arithmetic and copies ran while one was open for 3% of the time, Pallas kernels for 27%

profile of v9, /device:TPU:1, one launch (start us, length us, event | category | flops | bytes accessed | tf_op | source)
XLA Modules:
  0.0 79.1 jit_solution(7170225605171622207)
XLA Ops:
  0.6 0.1 collective-permute-start.3
  0.8 2.8 %collective-permute-start = (s32[8,128]{1,0:T(8,128)}, s32[8,128]{1,0:T(8,128)S(1)}, u32[]{:S(2)}, u32[]{:S(2)}) collective-permute-start(s32[8,128]{1,0:T(8,128)} %bitcast.29), channel_id=1, source_target_pairs={{0,2},{1,3},{2,0},{3,1},{4,6},{5,7},{6,4},{7,5},{8,10},{9,11},{10,... | collective-permute-start | bytes 12296 | tf_op jit(solution)/shard_map/ppermute | solution.py:52
  3.5 2.3 %collective-permute-start.1 = (s32[8,128]{1,0:T(8,128)}, s32[8,128]{1,0:T(8,128)S(1)}, u32[]{:S(2)}, u32[]{:S(2)}) collective-permute-start(s32[8,128]{1,0:T(8,128)} %bitcast.30), channel_id=1, source_target_pairs={{0,4},{1,5},{2,6},{3,7},{4,0},{5,1},{6,2},{7,3},{8,12},{9,13},{10,... | collective-permute-start | bytes 12296 | tf_op jit(solution)/shard_map/ppermute | solution.py:52
  5.8 1.4 %shard_map.112 = bf16[32,2,1408]{2,1,0:T(2,128)(2,1)} custom-call(bf16[2,768]{1,0:T(2,128)(2,1)} %docs_ref.1, s32[2,5]{1,0:T(2,128)} %positives_ref.1, s32[1,128]{1,0:T(1,128)} %bitcast.37, s32[1,128]{1,0:T(1,128)} %bitcast.38), custom_call_target="tpu_custom_call" | custom-call | tf_op jit(solution)/shard_map/pallas_call | solution.py:257
  7.3 3.0 %collective-permute-done.2.refs_0_ = s32[8,128]{1,0:T(8,128)S(1)} collective-permute-done((s32[8,128]{1,0:T(8,128)}, s32[8,128]{1,0:T(8,128)S(1)}, u32[]{:S(2)}, u32[]{:S(2)}) %collective-permute-start.2) | collective-permute-done | bytes 4128 | tf_op jit(solution)/shard_map/ppermute | solution.py:52
  10.3 4.3 %all-to-all-start = ((bf16[32,2,1408]{2,1,0:T(2,128)(2,1)}), bf16[32,2,1408]{2,1,0:T(2,128)(2,1)S(1)}, u32[]{:S(2)}, u32[]{:S(2)}) async-start(bf16[32,2,1408]{2,1,0:T(2,128)(2,1)} %shard_map.112), calls=%async_computation | async-start | bytes 360448 | tf_op jit(solution)/shard_map/all_to_all | solution.py:16
  14.7 8.6 %shard_map.113 = (bf16[128,768]{1,0:T(8,128)(2,1)}, bf16[128,768]{1,0:T(8,128)(2,1)}, f32[8,128]{1,0:T(8,128)}) custom-call(s32[1]{0:T(128)} %bitcast.3.me_ref, s32[8,128]{1,0:T(8,128)} %copy-done.2, s32[8,128]{1,0:T(8,128)} %copy-done.1, bf16[3840,768]{1,0:T(8,128)(2,1)} %refs_2_.3, bf16[3840,768]{1,0:T(8,128)(2,1)} %collective-permute-done.3.refs_3_), custom_call_target="tpu_custom_call" | custom-call | flops 1572864 | bytes 11796480 | tf_op jit(solution)/shard_map/pallas_call | solution.py:270
  23.3 0.3 collective-permute-start.4
  23.7 2.4 %collective-permute-start.6 = (bf16[128,768]{1,0:T(8,128)(2,1)}, bf16[128,768]{1,0:T(8,128)(2,1)S(1)}, u32[]{:S(2)}, u32[]{:S(2)}) collective-permute-start(bf16[128,768]{1,0:T(8,128)(2,1)} %get-tuple-element.33), channel_id=1, source_target_pairs={{0,4},{1,5},{2,6},{3,7},{4,0},{5,1},{6,2},{7,3},{8,12},{9,13},{10,... | collective-permute-start | bytes 589832 | tf_op jit(solution)/shard_map/ppermute | solution.py:52
  26.1 1.2 %collective-permute-start.5 = (bf16[128,768]{1,0:T(8,128)(2,1)}, bf16[128,768]{1,0:T(8,128)(2,1)S(1)}, u32[]{:S(2)}, u32[]{:S(2)}) collective-permute-start(bf16[128,768]{1,0:T(8,128)(2,1)} %get-tuple-element.32), channel_id=1, source_target_pairs={{0,6},{1,7},{2,4},{3,5},{4,2},{5,3},{6,0},{7,1},{8,14},{9,15},{10,... | collective-permute-start | bytes 589832 | tf_op jit(solution)/shard_map/ppermute | solution.py:52
  27.2 8.4 %shard_map.114 = (bf16[128,768]{1,0:T(8,128)(2,1)S(1)}, f32[128,768]{1,0:T(8,128)S(1)}, bf16[1280,768]{1,0:T(8,128)(2,1)}, bf16[768,768]{1,0:T(8,128)(2,1)S(1)}, f32[8,128]{1,0:T(8,128)}) custom-call(s32[1]{0:T(128)} %bitcast.3.me_ref, s32[8,128]{1,0:T(8,128)S(1)} %collective-permute-done.refs_0_, s32[8,128]{1,0:T(8,128)S(1)} %bitcast.32, ...), custom_call_target="tpu_custom_call" | custom-call | flops 1572864 | bytes 11796480 | tf_op jit(solution)/shard_map/pallas_call | solution.py:270
  35.8 0.1 fusion.8
  35.9 0.1 collective-permute-start.7
  36.1 0.1 add_select_fusion.1
  36.2 0.1 bitcast_select_fusion
  36.2 0.2 select_reduce_fusion
  36.5 3.0 %collective-permute-done.6 = bf16[128,768]{1,0:T(8,128)(2,1)S(1)} collective-permute-done((bf16[128,768]{1,0:T(8,128)(2,1)}, bf16[128,768]{1,0:T(8,128)(2,1)S(1)}, u32[]{:S(2)}, u32[]{:S(2)}) %collective-permute-start.6) | collective-permute-done | bytes 196640 | tf_op jit(solution)/shard_map/ppermute | solution.py:52
  39.5 4.6 %collective-permute-done.7 = bf16[128,768]{1,0:T(8,128)(2,1)S(1)} collective-permute-done((bf16[128,768]{1,0:T(8,128)(2,1)S(1)}, bf16[128,768]{1,0:T(8,128)(2,1)S(1)}, u32[]{:S(2)}, u32[]{:S(2)}) %collective-permute-start.7) | collective-permute-done | bytes 196640 | tf_op jit(solution)/shard_map/ppermute | solution.py:52
  44.2 0.4 multiply_reduce_fusion
  44.6 0.1 multiply_convert_fusion
  44.8 0.7 collective-permute-start.8
  45.4 0.1 fusion.39
  45.5 1.0 %collective-permute-done.8 = bf16[128,768]{1,0:T(8,128)(2,1)S(1)} collective-permute-done((bf16[128,768]{1,0:T(8,128)(2,1)S(1)}, bf16[128,768]{1,0:T(8,128)(2,1)S(1)}, u32[]{:S(2)}, u32[]{:S(2)}) %collective-permute-start.8) | collective-permute-done | bytes 196640 | tf_op jit(solution)/shard_map/ppermute | solution.py:48
  46.5 0.3 convolution_convert_fusion
  46.8 3.3 %collective-permute-start.11 = (bf16[64,768]{1,0:T(8,128)(2,1)S(1)}, bf16[64,768]{1,0:T(8,128)(2,1)S(1)}, u32[]{:S(2)}, u32[]{:S(2)}) collective-permute-start(bf16[64,768]{1,0:T(8,128)(2,1)S(1)} %get-tuple-element.42), channel_id=1, source_target_pairs={{0,6},{1,7},{2,4},{3,5},{4,2},{5,3},{6,0},{7,1},{8,14},{9,15},{10,... | collective-permute-start | bytes 294920 | tf_op jit(solution)/shard_map/ppermute | solution.py:52
  50.1 0.4 collective-permute-start.9
  50.6 0.1 copy.36
  50.7 0.1 copy.35
  50.8 0.1 copy.34
  51.0 1.8 %collective-permute-done.11 = bf16[64,768]{1,0:T(8,128)(2,1)S(1)} collective-permute-done((bf16[64,768]{1,0:T(8,128)(2,1)S(1)}, bf16[64,768]{1,0:T(8,128)(2,1)S(1)}, u32[]{:S(2)}, u32[]{:S(2)}) %collective-permute-start.11) | collective-permute-done | bytes 98336 | tf_op jit(solution)/shard_map/ppermute | solution.py:52
  52.7 5.7 %collective-permute-done.10 = bf16[64,768]{1,0:T(8,128)(2,1)S(1)} collective-permute-done((bf16[64,768]{1,0:T(8,128)(2,1)S(1)}, bf16[64,768]{1,0:T(8,128)(2,1)S(1)}, u32[]{:S(2)}, u32[]{:S(2)}) %collective-permute-start.10) | collective-permute-done | bytes 98336 | tf_op jit(solution)/shard_map/ppermute | solution.py:52
  58.5 0.7 add_convert_fusion.head_ref
  59.2 0.8 fusion.4.errors_ref
  60.0 1.2 %shard_map.115 = f32[32,2,768]{2,1,0:T(2,128)} custom-call(bf16[64,1280]{1,0:T(8,128)(2,1)S(1)} %fusion.4.errors_ref, bf16[1280,768]{1,0:T(8,128)(2,1)S(1)} %add_convert_fusion.head_ref), custom_call_target="tpu_custom_call" | custom-call | tf_op jit(solution)/shard_map/pallas_call | solution.py:308
  61.1 5.5 %all-to-all-start.1 = ((f32[32,2,768]{2,1,0:T(2,128)}), f32[32,2,768]{2,1,0:T(2,128)S(1)}, u32[]{:S(2)}, u32[]{:S(2)}) async-start(f32[32,2,768]{2,1,0:T(2,128)} %shard_map.115), calls=%async_computation.1 | async-start | bytes 393216 | tf_op jit(solution)/shard_map/all_to_all | solution.py:16
  66.6 0.3 fusion.7
  66.9 0.1 fusion.38
  67.0 3.2 %collective-permute-start.14 = (bf16[64,64]{0,1:T(8,128)(2,1)S(1)}, bf16[64,64]{0,1:T(8,128)(2,1)S(1)}, u32[]{:S(2)}, u32[]{:S(2)}) collective-permute-start(bf16[64,64]{0,1:T(8,128)(2,1)S(1)} %get-tuple-element.46), channel_id=1, source_target_pairs={{0,6},{1,7},{2,4},{3,5},{4,2},{5,3},{6,0},{7,1},{8,14},{9,15},{10,... | collective-permute-start | bytes 24584 | tf_op jit(solution)/shard_map/ppermute | solution.py:52
  70.3 0.4 collective-permute-start.12
  70.6 3.1 %shard_map.116 = bf16[1280,768]{1,0:T(8,128)(2,1)} custom-call(bf16[64,1280]{1,0:T(8,128)(2,1)S(1)} %fusion.4.errors_ref, bf16[64,768]{1,0:T(8,128)(2,1)S(1)} %reshape.146.docs_ref), custom_call_target="tpu_custom_call" | custom-call | flops 1 | bytes 1 | tf_op jit(solution)/shard_map/pallas_call | solution.py:327
  73.8 0.3 collective-permute-done.14
  74.1 1.2 %collective-permute-done.13 = bf16[64,64]{0,1:T(8,128)(2,1)S(1)} collective-permute-done((bf16[64,64]{0,1:T(8,128)(2,1)S(1)}, bf16[64,64]{0,1:T(8,128)(2,1)S(1)}, u32[]{:S(2)}, u32[]{:S(2)}) %collective-permute-start.13) | collective-permute-done | bytes 8224 | tf_op jit(solution)/shard_map/ppermute | solution.py:52
  75.2 0.1 pad_maximum_fusion
  75.3 1.5 %all-to-all-done.1 = f32[32,2,768]{2,1,0:T(2,128)S(1)} async-done(((f32[32,2,768]{2,1,0:T(2,128)}), f32[32,2,768]{2,1,0:T(2,128)S(1)}, u32[]{:S(2)}, u32[]{:S(2)}) %all-to-all-start.1) | async-done | bytes 196640 | tf_op jit(solution)/shard_map/all_to_all | solution.py:16
  76.8 0.2 convolution_convert_fusion.2
  77.0 0.7 reduce_sum.39
  77.7 0.5 collective-permute-done.15
  78.2 0.9 %convolution_convert_fusion.1 = bf16[128,768]{1,0:T(8,128)(2,1)} fusion(bf16[64,768]{1,0:T(8,128)(2,1)S(1)} %reshape.146.docs_ref, bf16[128,64]{0,1:T(8,128)(2,1)S(1)} %collective-permute-done.15, bf16[256,64]{0,1:T(8,128)(2,1)S(1)} %convolution_convert_fusion.2), kind=kOutput, calls=%fused_computation.11 | convolution fusion | flops 12689408 | bytes 327680 | tf_op jit(solution)/shard_map/dot_general | solution.py:454
  (38 shorter events, 0.6 us)
Async XLA Ops:
  0.6 14.0 %collective-permute-start.3 = (bf16[3840,768]{1,0:T(8,128)(2,1)}, bf16[3840,768]{1,0:T(8,128)(2,1)}, u32[]{:S(2)}, u32[]{:S(2)}) collective-permute-start(bf16[3840,768]{1,0:T(8,128)(2,1)} %refs_2_.3), channel_id=1, source_target_pairs={{0,1},{1,0},{2,3},{3,2},{4,5},{5,4},{6,7},{7,6},{8,9},{9,8},{10,11... | collective-permute-start | bytes 17694728 | tf_op jit(solution)/shard_map/ppermute | solution.py:48
  0.8 6.5 %collective-permute-start = (s32[8,128]{1,0:T(8,128)}, s32[8,128]{1,0:T(8,128)S(1)}, u32[]{:S(2)}, u32[]{:S(2)}) collective-permute-start(s32[8,128]{1,0:T(8,128)} %bitcast.29), channel_id=1, source_target_pairs={{0,2},{1,3},{2,0},{3,1},{4,6},{5,7},{6,4},{7,5},{8,10},{9,11},{10,... | collective-permute-start | bytes 12296 | tf_op jit(solution)/shard_map/ppermute | solution.py:52
  3.5 3.8 %collective-permute-start.1 = (s32[8,128]{1,0:T(8,128)}, s32[8,128]{1,0:T(8,128)S(1)}, u32[]{:S(2)}, u32[]{:S(2)}) collective-permute-start(s32[8,128]{1,0:T(8,128)} %bitcast.30), channel_id=1, source_target_pairs={{0,4},{1,5},{2,6},{3,7},{4,0},{5,1},{6,2},{7,3},{8,12},{9,13},{10,... | collective-permute-start | bytes 12296 | tf_op jit(solution)/shard_map/ppermute | solution.py:52
  5.8 4.5 %collective-permute-start.2 = (s32[8,128]{1,0:T(8,128)}, s32[8,128]{1,0:T(8,128)S(1)}, u32[]{:S(2)}, u32[]{:S(2)}) collective-permute-start(s32[8,128]{1,0:T(8,128)} %bitcast.31), channel_id=1, source_target_pairs={{0,6},{1,7},{2,4},{3,5},{4,2},{5,3},{6,0},{7,1},{8,14},{9,15},{10,... | collective-permute-start | bytes 12296 | tf_op jit(solution)/shard_map/ppermute | solution.py:52
  7.3 7.4 %copy-start.1 = (s32[8,128]{1,0:T(8,128)}, s32[8,128]{1,0:T(8,128)S(1)}, u32[]{:S(2)}) copy-start(s32[8,128]{1,0:T(8,128)S(1)} %collective-permute-done.1.refs_1_) | copy-start | bytes 12292
  10.3 4.4 %copy-start.2 = (s32[8,128]{1,0:T(8,128)}, s32[8,128]{1,0:T(8,128)S(1)}, u32[]{:S(2)}) copy-start(s32[8,128]{1,0:T(8,128)S(1)} %collective-permute-done.2.refs_0_) | copy-start | bytes 12292
  10.3 25.4 %all-to-all-start = ((bf16[32,2,1408]{2,1,0:T(2,128)(2,1)}), bf16[32,2,1408]{2,1,0:T(2,128)(2,1)S(1)}, u32[]{:S(2)}, u32[]{:S(2)}) async-start(bf16[32,2,1408]{2,1,0:T(2,128)(2,1)} %shard_map.112), calls=%async_computation | async-start | bytes 360448 | tf_op jit(solution)/shard_map/all_to_all | solution.py:16
  14.7 12.6 %copy-start = (s32[128,8]{0,1:T(8,128)S(1)}, s32[128,8]{0,1:T(8,128)}, u32[]{:S(2)}) copy-start(s32[128,8]{0,1:T(8,128)} %param.12) | copy-start | bytes 12292
  23.3 3.9 %collective-permute-start.4 = (f32[8,128]{1,0:T(8,128)}, f32[8,128]{1,0:T(8,128)S(1)}, u32[]{:S(2)}, u32[]{:S(2)}) collective-permute-start(f32[8,128]{1,0:T(8,128)} %get-tuple-element.27), channel_id=1, source_target_pairs={{0,1},{1,0},{2,3},{3,2},{4,5},{5,4},{6,7},{7,6},{8,9},{9,8},{10,11... | collective-permute-start | bytes 12296 | tf_op jit(solution)/shard_map/ppermute | solution.py:48
  23.7 15.9 %collective-permute-start.6 = (bf16[128,768]{1,0:T(8,128)(2,1)}, bf16[128,768]{1,0:T(8,128)(2,1)S(1)}, u32[]{:S(2)}, u32[]{:S(2)}) collective-permute-start(bf16[128,768]{1,0:T(8,128)(2,1)} %get-tuple-element.33), channel_id=1, source_target_pairs={{0,4},{1,5},{2,6},{3,7},{4,0},{5,1},{6,2},{7,3},{8,12},{9,13},{10,... | collective-permute-start | bytes 589832 | tf_op jit(solution)/shard_map/ppermute | solution.py:52
  26.1 13.5 %collective-permute-start.5 = (bf16[128,768]{1,0:T(8,128)(2,1)}, bf16[128,768]{1,0:T(8,128)(2,1)S(1)}, u32[]{:S(2)}, u32[]{:S(2)}) collective-permute-start(bf16[128,768]{1,0:T(8,128)(2,1)} %get-tuple-element.32), channel_id=1, source_target_pairs={{0,6},{1,7},{2,4},{3,5},{4,2},{5,3},{6,0},{7,1},{8,14},{9,15},{10,... | collective-permute-start | bytes 589832 | tf_op jit(solution)/shard_map/ppermute | solution.py:52
  35.7 8.9 %copy-start.3 = (f32[768]{0:T(1024)S(1)}, f32[768]{0:T(1024)}, u32[]{:S(2)}) copy-start(f32[768]{0:T(1024)} %param.11) | copy-start | bytes 9220
  35.9 8.2 %collective-permute-start.7 = (bf16[128,768]{1,0:T(8,128)(2,1)S(1)}, bf16[128,768]{1,0:T(8,128)(2,1)S(1)}, u32[]{:S(2)}, u32[]{:S(2)}) collective-permute-start(bf16[128,768]{1,0:T(8,128)(2,1)S(1)} %get-tuple-element.34), channel_id=1, source_target_pairs={{0,2},{1,3},{2,0},{3,1},{4,6},{5,7},{6,4},{7,5},{8,10},{9,11},{10,... | collective-permute-start | bytes 589832 | tf_op jit(solution)/shard_map/ppermute | solution.py:52
  44.6 13.9 %copy-start.4 = (bf16[1280,768]{1,0:T(8,128)(2,1)S(1)}, bf16[1280,768]{1,0:T(8,128)(2,1)}, u32[]{:S(2)}) copy-start(bf16[1280,768]{1,0:T(8,128)(2,1)} %get-tuple-element.30) | copy-start | bytes 5898244
  44.8 1.7 %collective-permute-start.8 = (bf16[128,768]{1,0:T(8,128)(2,1)S(1)}, bf16[128,768]{1,0:T(8,128)(2,1)S(1)}, u32[]{:S(2)}, u32[]{:S(2)}) collective-permute-start(bf16[128,768]{1,0:T(8,128)(2,1)S(1)} %multiply_convert_fusion), channel_id=1, source_target_pairs={{0,1},{1,0},{2,3},{3,2},{4,5},{5,4},{6,7},{7,6},{8,9},{9,8},{10,11... | collective-permute-start | bytes 589832 | tf_op jit(solution)/shard_map/ppermute | solution.py:48
  46.8 5.9 %collective-permute-start.11 = (bf16[64,768]{1,0:T(8,128)(2,1)S(1)}, bf16[64,768]{1,0:T(8,128)(2,1)S(1)}, u32[]{:S(2)}, u32[]{:S(2)}) collective-permute-start(bf16[64,768]{1,0:T(8,128)(2,1)S(1)} %get-tuple-element.42), channel_id=1, source_target_pairs={{0,6},{1,7},{2,4},{3,5},{4,2},{5,3},{6,0},{7,1},{8,14},{9,15},{10,... | collective-permute-start | bytes 294920 | tf_op jit(solution)/shard_map/ppermute | solution.py:52
  50.1 8.3 %collective-permute-start.10 = (bf16[64,768]{1,0:T(8,128)(2,1)S(1)}, bf16[64,768]{1,0:T(8,128)(2,1)S(1)}, u32[]{:S(2)}, u32[]{:S(2)}) collective-permute-start(bf16[64,768]{1,0:T(8,128)(2,1)S(1)} %get-tuple-element.43), channel_id=1, source_target_pairs={{0,4},{1,5},{2,6},{3,7},{4,0},{5,1},{6,2},{7,3},{8,12},{9,13},{10,... | collective-permute-start | bytes 294920 | tf_op jit(solution)/shard_map/ppermute | solution.py:52
  50.1 8.3 %collective-permute-start.9 = (bf16[64,768]{1,0:T(8,128)(2,1)S(1)}, bf16[64,768]{1,0:T(8,128)(2,1)S(1)}, u32[]{:S(2)}, u32[]{:S(2)}) collective-permute-start(bf16[64,768]{1,0:T(8,128)(2,1)S(1)} %get-tuple-element.44), channel_id=1, source_target_pairs={{0,2},{1,3},{2,0},{3,1},{4,6},{5,7},{6,4},{7,5},{8,10},{9,11},{10,... | collective-permute-start | bytes 294920 | tf_op jit(solution)/shard_map/ppermute | solution.py:52
  61.1 15.6 %all-to-all-start.1 = ((f32[32,2,768]{2,1,0:T(2,128)}), f32[32,2,768]{2,1,0:T(2,128)S(1)}, u32[]{:S(2)}, u32[]{:S(2)}) async-start(f32[32,2,768]{2,1,0:T(2,128)} %shard_map.115), calls=%async_computation.1 | async-start | bytes 393216 | tf_op jit(solution)/shard_map/all_to_all | solution.py:16
  67.0 7.0 %collective-permute-start.14 = (bf16[64,64]{0,1:T(8,128)(2,1)S(1)}, bf16[64,64]{0,1:T(8,128)(2,1)S(1)}, u32[]{:S(2)}, u32[]{:S(2)}) collective-permute-start(bf16[64,64]{0,1:T(8,128)(2,1)S(1)} %get-tuple-element.46), channel_id=1, source_target_pairs={{0,6},{1,7},{2,4},{3,5},{4,2},{5,3},{6,0},{7,1},{8,14},{9,15},{10,... | collective-permute-start | bytes 24584 | tf_op jit(solution)/shard_map/ppermute | solution.py:52
  70.3 4.9 %collective-permute-start.13 = (bf16[64,64]{0,1:T(8,128)(2,1)S(1)}, bf16[64,64]{0,1:T(8,128)(2,1)S(1)}, u32[]{:S(2)}, u32[]{:S(2)}) collective-permute-start(bf16[64,64]{0,1:T(8,128)(2,1)S(1)} %get-tuple-element.47), channel_id=1, source_target_pairs={{0,4},{1,5},{2,6},{3,7},{4,0},{5,1},{6,2},{7,3},{8,12},{9,13},{10,... | collective-permute-start | bytes 24584 | tf_op jit(solution)/shard_map/ppermute | solution.py:52
  70.3 4.9 %collective-permute-start.12 = (bf16[64,64]{0,1:T(8,128)(2,1)S(1)}, bf16[64,64]{0,1:T(8,128)(2,1)S(1)}, u32[]{:S(2)}, u32[]{:S(2)}) collective-permute-start(bf16[64,64]{0,1:T(8,128)(2,1)S(1)} %get-tuple-element.48), channel_id=1, source_target_pairs={{0,2},{1,3},{2,0},{3,1},{4,6},{5,7},{6,4},{7,5},{8,10},{9,11},{10,... | collective-permute-start | bytes 24584 | tf_op jit(solution)/shard_map/ppermute | solution.py:52
  76.9 1.2 %collective-permute-start.15 = (bf16[128,64]{0,1:T(8,128)(2,1)S(1)}, bf16[128,64]{0,1:T(8,128)(2,1)S(1)}, u32[]{:S(2)}, u32[]{:S(2)}) collective-permute-start(bf16[128,64]{0,1:T(8,128)(2,1)S(1)} %slice.117), channel_id=1, source_target_pairs={{0,1},{1,0},{2,3},{3,2},{4,5},{5,4},{6,7},{7,6},{8,9},{9,8},{10,11... | collective-permute-start | bytes 49160 | tf_op jit(solution)/shard_map/ppermute | solution.py:48
